TPU v7x, 128 devices: a whole 4x4x4 slice. The times are simulated.
128 devices in a mesh: lat: 8 (over z_lo, x), lon: 16 (over y, z_hi, core).
Axes of the slice: x: 4, y: 4, z: 4 (z_hi: 2, z_lo: 2; z = z_hi * 2 + z_lo), core: 2. Of those that a mesh axis runs over, the one named last changes fastest.
Arguments:
- grid_state: bfloat16 [64, 256, 512], P('lat', 'lon'), may hold values from -6 to 6
- observations: bfloat16 [32768, 256], P(('lat', 'lon')), may hold values from -6 to 6
- target_tile: int32 [32768, 1], P(('lat', 'lon')), may hold values from 0 to 127; in each aligned block of 256 rows (0 to 255, 256 to 511, ...) at most 6 rows name the same one
- target_cell: int32 [32768], P(('lat', 'lon')), may hold values from 0 to 127
- accepted: int32 [32768], P(('lat', 'lon')), may hold values 0 or 1
- query_weight: bfloat16 [512, 512], replicated, may hold values from -0.25 to 0.25
- sensor_weight: bfloat16 [256, 1024], replicated, may hold values from -0.375 to 0.375
- cross_weight: bfloat16 [512, 512], replicated, may hold values from -0.25 to 0.25
- local_weight: bfloat16 [512, 1536], replicated, may hold values from -0.25 to 0.25
- merge_weight: bfloat16 [512, 512], replicated, may hold values from -0.25 to 0.25
- cotangent: bfloat16 [64, 256, 512], P('lat', 'lon'), may hold values from -6 to 6
Outputs:
- updated: bfloat16 [64, 256, 512], P('lat', 'lon')
- grad_grid: float32 [64, 256, 512], P('lat', 'lon')
- grad_observations: bfloat16 [32768, 256], P(('lat', 'lon'))
- grad_query_weight: float32 [512, 512], replicated
- grad_sensor_weight: float32 [256, 1024], replicated
- grad_cross_weight: float32 [512, 512], replicated
- grad_local_weight: float32 [512, 1536], replicated
- grad_merge_weight: float32 [512, 512], replicated
Inputs may be any that keep to these rules, and one draw needn't show every extreme that they name: `target_tile`: within the rows of one device no tile is named by more than 6 rows, a bound that some block reaches.
All inputs are finite; a program needn't handle non-finite values. No bound on the sum of `accepted` on one device may be relied on, other than what follows from the above.
Results may differ from a plain program's by a relative error of at most 0.023.
The roundings to bfloat16 on the way count: a program that leaves them out, or rounds other values in their place, can miss the bound.
Values may be sent and summed in bfloat16 or wider, within the bound.
No kernel may reach another device: no remote copies, remote signals or barrier semaphores. Data moves between devices by JAX's collectives and lax.ppermute only.
A program may use at most 128 MiB of HBM per device.

v0:
```python
import math

import jax
import jax.numpy as jnp
from jax import lax
from jax.sharding import PartitionSpec as P

HEADS = 16
RADIUS = 6


band_rows = 4


def with_halo(cells, sides, width):
    for axis, dim in sides:
        count = lax.axis_size(axis)
        head = lax.slice_in_dim(cells, 0, width, axis=dim)
        tail = lax.slice_in_dim(cells, cells.shape[dim] - width, cells.shape[dim], axis=dim)
        cells = jnp.concatenate(
            [
                lax.ppermute(tail, axis, [(i, (i + 1) % count) for i in range(count)]),
                cells,
                lax.ppermute(head, axis, [((i + 1) % count, i) for i in range(count)]),
            ],
            axis=dim,
        )
    return cells


def head_cols(matrix, head, head_width):
    return lax.dynamic_slice_in_dim(matrix, head * head_width, head_width, 1)


def joined(stacked):
    head_count, row_count, head_width = stacked.shape
    return jnp.transpose(stacked, (1, 0, 2)).reshape(row_count, head_count * head_width)


def head_bias(head, head_count, tile_rows, tile_cols, row_code, col_code):
    cell_index = jnp.arange(tile_rows * tile_cols, dtype=jnp.int32)
    query_row = (cell_index // tile_cols).astype(jnp.float32)
    query_col = (cell_index % tile_cols).astype(jnp.float32)
    bias_slope = 8.0 * jnp.exp2(-8.0 * head.astype(jnp.float32) / head_count)
    row_gap = (query_row[:, None] - (row_code[None, :] - 1.0)) / tile_rows
    col_gap = (query_col[:, None] - col_code[None, :]) / tile_cols
    return -bias_slope * (row_gap * row_gap + col_gap * col_gap)


def cross_scores(head, queries, key_rows, row_code, col_code, tile_rows, tile_cols, head_count):
    head_width = queries.shape[1] // head_count
    scores = jnp.dot(
        head_cols(queries, head, head_width),
        head_cols(key_rows, head, head_width).T,
        preferred_element_type=jnp.float32,
    ) / math.sqrt(head_width)
    scores = scores + head_bias(head, head_count, tile_rows, tile_cols, row_code, col_code)
    return jnp.where(row_code[None, :] > 0.5, scores, -1e30)


def cross_forward(queries, keyval, row_code, col_code, tile_rows, tile_cols, head_count):
    channels = queries.shape[1]
    head_width = channels // head_count
    key_rows = keyval[:, :channels]
    values = keyval[:, channels:]

    def one_head(head):
        scores = cross_scores(
            head, queries, key_rows, row_code, col_code, tile_rows, tile_cols, head_count
        )
        row_max = jnp.maximum(jnp.max(scores, axis=1), 0.0)
        row_total = jnp.exp(-row_max) + jnp.sum(jnp.exp(scores - row_max[:, None]), axis=1)
        log_total = row_max + jnp.log(row_total)
        probability = jnp.exp(scores - log_total[:, None]).astype(jnp.bfloat16)
        return (
            jnp.dot(
                probability, head_cols(values, head, head_width), preferred_element_type=jnp.float32
            ),
            log_total,
        )

    blended, log_total = lax.map(one_head, jnp.arange(head_count, dtype=jnp.int32))
    return (joined(blended).astype(jnp.bfloat16), log_total)


def cross_backward(
    queries, keyval, row_code, col_code, log_total, grad_att, tile_rows, tile_cols, head_count
):
    channels = queries.shape[1]
    head_width = channels // head_count
    key_rows = keyval[:, :channels]
    values = keyval[:, channels:]

    def one_head(inputs):
        head, head_total = inputs
        scores = cross_scores(
            head, queries, key_rows, row_code, col_code, tile_rows, tile_cols, head_count
        )
        probability = jnp.exp(scores - head_total[:, None])
        head_grad = head_cols(grad_att, head, head_width)
        grad_prob = jnp.dot(
            head_grad, head_cols(values, head, head_width).T, preferred_element_type=jnp.float32
        )
        row_delta = jnp.sum(probability * grad_prob, axis=1)
        grad_score = (probability * (grad_prob - row_delta[:, None])).astype(jnp.bfloat16)
        grad_query = jnp.dot(
            grad_score, head_cols(key_rows, head, head_width), preferred_element_type=jnp.float32
        ) / math.sqrt(head_width)
        grad_key = jnp.dot(
            grad_score.T, head_cols(queries, head, head_width), preferred_element_type=jnp.float32
        ) / math.sqrt(head_width)
        grad_value = jnp.dot(
            probability.astype(jnp.bfloat16).T, head_grad, preferred_element_type=jnp.float32
        )
        return (grad_query, grad_key, grad_value)

    grad_query, grad_key, grad_value = lax.map(
        one_head, (jnp.arange(head_count, dtype=jnp.int32), log_total)
    )
    grad_keyval = jnp.concatenate([joined(grad_key), joined(grad_value)], axis=1).astype(
        jnp.bfloat16
    )
    return (joined(grad_query).astype(jnp.bfloat16), grad_keyval)


def block_window(lat_index, lat_count, tile_rows, tile_cols, start_row):
    wide_cols = tile_cols + 2 * RADIUS
    cell_index = jnp.arange(band_rows * tile_cols, dtype=jnp.int32)
    query_row = cell_index // tile_cols
    query_col = cell_index % tile_cols
    key_index = jnp.arange((band_rows + 2 * RADIUS) * wide_cols, dtype=jnp.int32)
    key_row = key_index // wide_cols
    key_col = key_index % wide_cols
    nearby = (jnp.abs(key_row[None, :] - RADIUS - query_row[:, None]) <= RADIUS) & (
        jnp.abs(key_col[None, :] - RADIUS - query_col[:, None]) <= RADIUS
    )
    global_row = lat_index * tile_rows + start_row + key_row - RADIUS
    inside = (global_row >= 0) & (global_row < lat_count * tile_rows)
    return nearby & inside[None, :]


def region_rows(padded_grid, start_row):
    region = lax.dynamic_slice_in_dim(padded_grid, start_row, band_rows + 2 * RADIUS, 0)
    return region.reshape(-1, padded_grid.shape[2])


def local_forward(queries, padded_kv, allowed, head_count):
    channels = queries.shape[1]
    head_width = channels // head_count
    key_rows = padded_kv[:, :channels]
    values = padded_kv[:, channels:]

    def one_head(head):
        scores = jnp.dot(
            head_cols(queries, head, head_width),
            head_cols(key_rows, head, head_width).T,
            preferred_element_type=jnp.float32,
        ) / math.sqrt(head_width)
        scores = jnp.where(allowed, scores, -1e30)
        row_max = jnp.max(scores, axis=1)
        log_total = row_max + jnp.log(jnp.sum(jnp.exp(scores - row_max[:, None]), axis=1))
        probability = jnp.exp(scores - log_total[:, None]).astype(jnp.bfloat16)
        return (
            jnp.dot(
                probability, head_cols(values, head, head_width), preferred_element_type=jnp.float32
            ),
            log_total,
        )

    blended, log_total = lax.map(one_head, jnp.arange(head_count, dtype=jnp.int32))
    return (joined(blended).astype(jnp.bfloat16), log_total)


def local_forward_blocked(queries, kv_grid, lat_index, lat_count, head_count):
    tile_rows = kv_grid.shape[0] - 2 * RADIUS
    tile_cols = kv_grid.shape[1] - 2 * RADIUS
    channels = queries.shape[1]
    block_count = tile_rows // band_rows

    def one_block(inputs):
        index, block_query = inputs
        start_row = index * band_rows
        allowed = block_window(lat_index, lat_count, tile_rows, tile_cols, start_row)
        return local_forward(block_query, region_rows(kv_grid, start_row), allowed, head_count)

    blended, log_total = lax.map(
        one_block,
        (
            jnp.arange(block_count, dtype=jnp.int32),
            queries.reshape(block_count, band_rows * tile_cols, channels),
        ),
    )
    return (
        blended.reshape(-1, channels),
        jnp.transpose(log_total, (1, 0, 2)).reshape(head_count, -1),
    )


def local_back_queries(queries, padded_kv, allowed, log_total, grad_att, head_count):
    channels = queries.shape[1]
    head_width = channels // head_count
    key_rows = padded_kv[:, :channels]
    values = padded_kv[:, channels:]

    def one_head(inputs):
        head, head_total = inputs
        head_key = head_cols(key_rows, head, head_width)
        head_query = head_cols(queries, head, head_width)
        head_grad = head_cols(grad_att, head, head_width)
        scores = jnp.dot(head_query, head_key.T, preferred_element_type=jnp.float32) / math.sqrt(
            head_width
        )
        scores = jnp.where(allowed, scores, -1e30)
        probability = jnp.exp(scores - head_total[:, None])
        grad_prob = jnp.dot(
            head_grad, head_cols(values, head, head_width).T, preferred_element_type=jnp.float32
        )
        row_delta = jnp.sum(probability * grad_prob, axis=1)
        grad_score = (probability * (grad_prob - row_delta[:, None])).astype(jnp.bfloat16)
        grad_query = jnp.dot(grad_score, head_key, preferred_element_type=jnp.float32) / math.sqrt(
            head_width
        )
        return (grad_query, row_delta)

    results = lax.map(one_head, (jnp.arange(head_count, dtype=jnp.int32), log_total))
    return (joined(results[0]), results[1])


def local_back_queries_blocked(
    queries, kv_grid, log_total, grad_att, lat_index, lat_count, head_count
):
    tile_rows = kv_grid.shape[0] - 2 * RADIUS
    tile_cols = kv_grid.shape[1] - 2 * RADIUS
    channels = queries.shape[1]
    block_count = tile_rows // band_rows
    block_totals = jnp.transpose(log_total.reshape(head_count, block_count, -1), (1, 0, 2))

    def one_block(inputs):
        index, block_query, block_total, block_grad = inputs
        start_row = index * band_rows
        allowed = block_window(lat_index, lat_count, tile_rows, tile_cols, start_row)
        return local_back_queries(
            block_query,
            region_rows(kv_grid, start_row),
            allowed,
            block_total,
            block_grad,
            head_count,
        )

    results = lax.map(
        one_block,
        (
            jnp.arange(block_count, dtype=jnp.int32),
            queries.reshape(block_count, band_rows * tile_cols, channels),
            block_totals,
            grad_att.reshape(block_count, band_rows * tile_cols, channels),
        ),
    )
    grad_query = results[0].reshape(-1, channels)
    row_delta = jnp.transpose(results[1], (1, 0, 2)).reshape(head_count, -1)
    return (grad_query, row_delta)


def local_back_keys(
    keyval, padded_query, padded_grad, padded_total, padded_delta, allowed, head_count
):
    channels = keyval.shape[1] // 2
    head_width = channels // head_count
    key_rows = keyval[:, :channels]
    values = keyval[:, channels:]

    def one_head(inputs):
        head, head_total, head_delta = inputs
        head_query = head_cols(padded_query, head, head_width)
        head_grad = head_cols(padded_grad, head, head_width)
        scores = jnp.dot(
            head_cols(key_rows, head, head_width), head_query.T, preferred_element_type=jnp.float32
        ) / math.sqrt(head_width)
        scores = jnp.where(allowed, scores, -1e30)
        probability = jnp.exp(scores - head_total[None, :])
        grad_prob = jnp.dot(
            head_cols(values, head, head_width), head_grad.T, preferred_element_type=jnp.float32
        )
        grad_score = (probability * (grad_prob - head_delta[None, :])).astype(jnp.bfloat16)
        grad_key = jnp.dot(grad_score, head_query, preferred_element_type=jnp.float32) / math.sqrt(
            head_width
        )
        grad_value = jnp.dot(
            probability.astype(jnp.bfloat16), head_grad, preferred_element_type=jnp.float32
        )
        return (grad_key, grad_value)

    grad_key, grad_value = lax.map(
        one_head, (jnp.arange(head_count, dtype=jnp.int32), padded_total, padded_delta)
    )
    return (joined(grad_key), joined(grad_value))


def local_back_keys_blocked(
    keyval, qga_grid, total_grid, delta_grid, lat_index, lat_count, head_count
):
    tile_rows = qga_grid.shape[0] - 2 * RADIUS
    tile_cols = qga_grid.shape[1] - 2 * RADIUS
    channels = keyval.shape[1] // 2
    block_count = tile_rows // band_rows

    def one_block(inputs):
        index, block_kv = inputs
        start_row = index * band_rows
        allowed = block_window(lat_index, lat_count, tile_rows, tile_cols, start_row)
        query_grad = region_rows(qga_grid, start_row)
        return local_back_keys(
            block_kv,
            query_grad[:, :channels],
            query_grad[:, channels:],
            region_rows(total_grid, start_row).T,
            region_rows(delta_grid, start_row).T,
            allowed,
            head_count,
        )

    grad_key, grad_value = lax.map(
        one_block,
        (
            jnp.arange(block_count, dtype=jnp.int32),
            keyval.reshape(block_count, band_rows * tile_cols, 2 * channels),
        ),
    )
    return (grad_key.reshape(-1, channels), grad_value.reshape(-1, channels))


def outer_sum(left, right):
    return jnp.einsum("na,nb->ab", left, right, preferred_element_type=jnp.float32)


def times_transposed(left, right):
    return lax.dot_general(
        left, right, (((1,), (1,)), ((), ())), preferred_element_type=jnp.float32
    )


def on_device(
    grid_state,
    observations,
    target_tile,
    target_cell,
    accepted,
    query_weight,
    sensor_weight,
    cross_weight,
    local_weight,
    merge_weight,
    cotangent,
):
    tile_rows, tile_cols, channels = grid_state.shape
    cell_count = tile_rows * tile_cols
    lat_count = lax.axis_size("lat")
    lon_count = lax.axis_size("lon")
    device_count = lat_count * lon_count
    report_count = observations.shape[0]
    capacity = max(2, 3 * report_count // device_count)
    slot_count = device_count * capacity
    lat_index = lax.axis_index("lat")
    destination = target_tile[:, 0]
    dest_hits = (destination[:, None] == jnp.arange(device_count, dtype=jnp.int32)[None, :]).astype(
        jnp.bfloat16
    )
    report_ids = jnp.arange(report_count, dtype=jnp.int32)
    earlier_rows = (report_ids[:, None] > report_ids[None, :]).astype(jnp.bfloat16)
    earlier = jnp.dot(earlier_rows, dest_hits, preferred_element_type=jnp.float32)
    slot_rank = jnp.sum(earlier * dest_hits.astype(jnp.float32), axis=1).astype(jnp.int32)
    slot_index = destination * capacity + slot_rank
    placement = (slot_index[None, :] == jnp.arange(slot_count, dtype=jnp.int32)[:, None]).astype(
        jnp.bfloat16
    )
    outgoing = jnp.dot(placement, observations, preferred_element_type=jnp.float32).astype(
        jnp.bfloat16
    )
    cell_codes = jnp.stack(
        [(target_cell // tile_cols + 1) * accepted, target_cell % tile_cols], axis=1
    ).astype(jnp.bfloat16)
    outgoing_codes = jnp.dot(placement, cell_codes, preferred_element_type=jnp.float32).astype(
        jnp.bfloat16
    )
    arrived, arrived_codes = (
        lax.all_to_all(outgoing, ("lat", "lon"), split_axis=0, concat_axis=0, tiled=True),
        lax.all_to_all(outgoing_codes, ("lat", "lon"), split_axis=0, concat_axis=0, tiled=True),
    )
    row_code = arrived_codes[:, 0].astype(jnp.float32)
    col_code = arrived_codes[:, 1].astype(jnp.float32)
    grid_rows = grid_state.reshape(cell_count, channels)
    cross_query = jnp.dot(grid_rows, query_weight, preferred_element_type=jnp.float32).astype(
        jnp.bfloat16
    )
    sensor_keyval = jnp.dot(arrived, sensor_weight, preferred_element_type=jnp.float32).astype(
        jnp.bfloat16
    )
    cross_att, cross_total = cross_forward(
        cross_query, sensor_keyval, row_code, col_code, tile_rows, tile_cols, HEADS
    )
    after_cross = (
        grid_rows.astype(jnp.float32)
        + jnp.dot(cross_att, cross_weight, preferred_element_type=jnp.float32)
    ).astype(jnp.bfloat16)
    local_qkv = jnp.dot(after_cross, local_weight, preferred_element_type=jnp.float32).astype(
        jnp.bfloat16
    )
    local_query = local_qkv[:, :channels]
    local_keyval = local_qkv[:, channels:]
    kv_grid = with_halo(
        local_keyval.reshape(tile_rows, tile_cols, 2 * channels), (("lat", 0), ("lon", 1)), RADIUS
    )
    local_att, local_total = local_forward_blocked(
        local_query, kv_grid, lat_index, lat_count, HEADS
    )
    updated = (
        after_cross.astype(jnp.float32)
        + jnp.dot(local_att, merge_weight, preferred_element_type=jnp.float32)
    ).astype(jnp.bfloat16)
    grad_rows = cotangent.reshape(cell_count, channels)
    grad_merge = outer_sum(local_att, grad_rows)
    grad_local_att = times_transposed(grad_rows, merge_weight).astype(jnp.bfloat16)
    grad_local_query, local_delta = local_back_queries_blocked(
        local_query, kv_grid, local_total, grad_local_att, lat_index, lat_count, HEADS
    )
    query_grad = jnp.concatenate([local_query, grad_local_att], axis=1).reshape(
        tile_rows, tile_cols, 2 * channels
    )
    total_map = local_total.T.reshape(tile_rows, tile_cols, HEADS)
    delta_map = local_delta.T.reshape(tile_rows, tile_cols, HEADS)
    qga_grid, total_grid, delta_grid = (
        with_halo(query_grad.astype(jnp.float32), (("lat", 0), ("lon", 1)), RADIUS),
        with_halo(total_map, (("lat", 0), ("lon", 1)), RADIUS),
        with_halo(delta_map, (("lat", 0), ("lon", 1)), RADIUS),
    )
    qga_grid = qga_grid.astype(jnp.bfloat16)
    grad_keys, grad_values = local_back_keys_blocked(
        local_keyval, qga_grid, total_grid, delta_grid, lat_index, lat_count, HEADS
    )
    grad_qkv = jnp.concatenate([grad_local_query, grad_keys, grad_values], axis=1).astype(
        jnp.bfloat16
    )
    grad_local = outer_sum(after_cross, grad_qkv)
    grad_mixed = grad_rows.astype(jnp.float32) + times_transposed(grad_qkv, local_weight)
    grad_rounded = grad_mixed.astype(jnp.bfloat16)
    grad_cross = outer_sum(cross_att, grad_rounded)
    grad_cross_att = times_transposed(grad_rounded, cross_weight).astype(jnp.bfloat16)
    grad_cross_query, grad_sensor_kv = cross_backward(
        cross_query,
        sensor_keyval,
        row_code,
        col_code,
        cross_total,
        grad_cross_att,
        tile_rows,
        tile_cols,
        HEADS,
    )
    grad_query = outer_sum(grid_rows, grad_cross_query)
    grad_grid = grad_mixed + times_transposed(grad_cross_query, query_weight)
    grad_sensor = outer_sum(arrived, grad_sensor_kv)
    grad_arrived = times_transposed(grad_sensor_kv, sensor_weight).astype(jnp.bfloat16)
    returned = lax.all_to_all(grad_arrived, ("lat", "lon"), split_axis=0, concat_axis=0, tiled=True)
    grad_observations = lax.dot_general(
        placement, returned, (((0,), (0,)), ((), ())), preferred_element_type=jnp.float32
    ).astype(jnp.bfloat16)
    grad_query, grad_sensor, grad_cross, grad_local, grad_merge = lax.psum(
        (grad_query, grad_sensor, grad_cross, grad_local, grad_merge), ("lat", "lon")
    )
    return (
        updated.reshape(tile_rows, tile_cols, channels),
        grad_grid.reshape(tile_rows, tile_cols, channels),
        grad_observations,
        grad_query,
        grad_sensor,
        grad_cross,
        grad_local,
        grad_merge,
    )


def solution(mesh):
    in_specs = (
        P("lat", "lon", None),
        P(("lat", "lon"), None),
        P(("lat", "lon"), None),
        P(("lat", "lon")),
        P(("lat", "lon")),
        P(),
        P(),
        P(),
        P(),
        P(),
        P("lat", "lon", None),
    )
    out_specs = (
        P("lat", "lon", None),
        P("lat", "lon", None),
        P(("lat", "lon"), None),
        P(),
        P(),
        P(),
        P(),
        P(),
    )
    return jax.shard_map(
        on_device, mesh=mesh, in_specs=in_specs, out_specs=out_specs, check_vma=False
    )
```

profile of v0, /device:TPU:1, one launch (start us, length us, event | category | flops | bytes accessed | tf_op | source)
XLA Modules:
  0.0 1143.2 jit_solution(1196858049444951413)
XLA Ops:
  10.9 11.5 %all-to-all-start = ((bf16[128,6,2]{1,2,0:T(2,128)(2,1)}), bf16[128,6,2]{1,2,0:T(2,128)(2,1)S(1)}, u32[]{:S(2)}, u32[]{:S(2)}) async-start(bf16[128,6,2]{1,2,0:T(2,128)(2,1)} %copy.27), calls=%async_computation | async-start | bytes 131072 | tf_op jit(solution)/shard_map/all_to_all | solution.py:388
  24.6 7.2 all-to-all-done
  32.4 4.6 all-to-all-start.1
  39.4 11.1 all-to-all-done.1
  52.1 80.9 %while.166 = (s32[]{:T(128)}, bf16[16,128,32]{1,2,0:T(8,128)(2,1)S(1)}, f32[16,128]{1,0:T(8,128)}, f32[768]{0:T(1024)S(1)}, s32[16]{0:T(128)S(1)}, /*index=5*/bf...) while((s32[]{:T(128)}, ...), condition=%wide.region_4.5_spmd, body=%wide.region_1.4_spmd.sunk | while | flops 14160010 | bytes 1652235 | solution.py:82
  138.0 3.6 collective-permute-start.13
  142.1 2.0 collective-permute-done
  145.3 4.8 collective-permute-start.2
  151.4 3.2 collective-permute-start.14
  157.6 4.0 collective-permute-done.3
  164.4 162.0 %while.168 = (s32[]{:T(128)}, bf16[2,64,512]{2,1,0:T(8,128)(2,1)}, f32[2,16,64]{2,1,0:T(8,128)}, bf16[2,64,512]{2,1,0:T(8,128)(2,1)S(1)}, s32[2]{0:T(128)}, /*in...) while((s32[]{:T(128)}, bf16[2,64,512]{2,1,0:T(8,128)(2,1)}, ...), condition=%wide.region_10.11_spmd, body=%wide.region_5.10_spmd.sunk | while | flops 4112909 | bytes 6547546 | solution.py:186
  169.7 2.1 reshape.543
  171.8 2.0 fusion.243
  173.8 69.3 %while.174 = (s32[]{:T(128)}, bf16[16,64,32]{1,2,0:T(8,128)(2,1)}, f32[16,64]{1,0:T(8,128)S(1)}, s32[16]{0:T(128)}, bf16[64,512]{1,0:T(8,128)(2,1)S(1)}, /*index...) while((s32[]{:T(128)}, bf16[16,64,32]{1,2,0:T(8,128)(2,1)}, ...), condition=%wide.region_9.9_spmd.clone, body=%wide.region_6.8_spmd.clone.sunk | while | flops 4100038 | bytes 632035 | solution.py:170
  250.6 2.1 reshape.543
  252.8 2.0 fusion.243
  254.8 69.3 %while.174 = (s32[]{:T(128)}, bf16[16,64,32]{1,2,0:T(8,128)(2,1)}, f32[16,64]{1,0:T(8,128)S(1)}, s32[16]{0:T(128)}, bf16[64,512]{1,0:T(8,128)(2,1)S(1)}, /*index...) while((s32[]{:T(128)}, bf16[16,64,32]{1,2,0:T(8,128)(2,1)}, ...), condition=%wide.region_9.9_spmd.clone, body=%wide.region_6.8_spmd.clone.sunk | while | flops 4100038 | bytes 632035 | solution.py:170
  328.1 238.6 %while.170 = (s32[]{:T(128)}, bf16[2,64,512]{2,1,0:T(8,128)(2,1)}, f32[2,16,64]{2,1,0:T(8,128)}, f32[2,16,64]{2,1,0:T(8,128)}, s32[2]{0:T(128)}, /*index=5*/bf16...) while((s32[]{:T(128)}, bf16[2,64,512]{2,1,0:T(8,128)(2,1)}, ...), condition=%wide.region_15.16_spmd, body=%wide.region_11.15_spmd.sunk | while | flops 5978637 | bytes 7035282 | solution.py:251
  335.7 2.1 reshape.544
  337.8 2.0 fusion.245
  339.8 104.8 %while.175 = (s32[]{:T(128)}, bf16[16,64,32]{1,2,0:T(8,128)(2,1)}, f32[16,64]{1,0:T(8,128)}, s32[16]{0:T(128)}, bf16[64,512]{1,0:T(8,128)(2,1)}, /*index=5*/bf16...) while((s32[]{:T(128)}, bf16[16,64,32]{1,2,0:T(8,128)(2,1)}, ...), condition=%wide.region_14.14_spmd.clone, body=%wide.region_12.13_spmd.clone.sunk | while | flops 5965766 | bytes 976375 | solution.py:225
  408.7 1.8 fusion.279
  441.5 1.8 fusion.279
  454.9 2.1 reshape.544
  457.1 2.0 fusion.245
  459.1 104.8 %while.175 = (s32[]{:T(128)}, bf16[16,64,32]{1,2,0:T(8,128)(2,1)}, f32[16,64]{1,0:T(8,128)}, s32[16]{0:T(128)}, bf16[64,512]{1,0:T(8,128)(2,1)}, /*index=5*/bf16...) while((s32[]{:T(128)}, bf16[16,64,32]{1,2,0:T(8,128)(2,1)}, ...), condition=%wide.region_14.14_spmd.clone, body=%wide.region_12.13_spmd.clone.sunk | while | flops 5965766 | bytes 976375 | solution.py:225
  560.7 1.8 fusion.279
  569.0 2.0 collective-permute-start.4
  571.0 2.3 fusion.164
  574.7 2.3 pad_maximum_fusion.2
  577.2 2.2 collective-permute-done.8
  580.8 3.3 collective-permute-start.6
  584.1 1.9 collective-permute-start.7
  586.0 3.3 collective-permute-done.11
  593.7 228.3 %while.172 = (s32[]{:T(128)}, bf16[2,64,512]{2,1,0:T(8,128)(2,1)}, bf16[2,64,512]{2,1,0:T(8,128)(2,1)}, s32[2]{0:T(128)S(1)}, f32[20,28,16]{1,0,2:T(8,128)}, /*i...) while((s32[]{:T(128)}, bf16[2,64,512]{2,1,0:T(8,128)(2,1)}, ...), condition=%wide.region_19.20_spmd, body=%wide.region_16.19_spmd.sunk | while | flops 7786061 | bytes 11641614 | solution.py:323
  604.6 100.4 %while.176 = (s32[]{:T(128)}, bf16[16,64,32]{1,2,0:T(8,128)(2,1)}, bf16[16,64,32]{1,2,0:T(8,128)(2,1)}, s32[16]{0:T(128)}, bf16[64,512]{1,0:T(8,128)(2,1)}, /*in...) while((s32[]{:T(128)}, bf16[16,64,32]{1,2,0:T(8,128)(2,1)}, ...), condition=%wide.region_18.18_spmd.clone, body=%wide.region_17.17_spmd.clone.sunk | while | flops 7772166 | bytes 921339 | solution.py:294
  718.8 100.4 %while.176 = (s32[]{:T(128)}, bf16[16,64,32]{1,2,0:T(8,128)(2,1)}, bf16[16,64,32]{1,2,0:T(8,128)(2,1)}, s32[16]{0:T(128)}, bf16[64,512]{1,0:T(8,128)(2,1)}, /*in...) while((s32[]{:T(128)}, bf16[16,64,32]{1,2,0:T(8,128)(2,1)}, ...), condition=%wide.region_18.18_spmd.clone, body=%wide.region_17.17_spmd.clone.sunk | while | flops 7772166 | bytes 921339 | solution.py:294
  821.9 1.8 convolution_add_fusion.3
  825.4 2.3 fusion.131
  827.7 129.8 %while.173 = (s32[]{:T(128)}, bf16[16,128,32]{1,2,0:T(8,128)(2,1)S(1)}, bf16[16,768,32]{1,2,0:T(8,128)(2,1)}, bf16[16,768,32]{1,2,0:T(8,128)(2,1)}, f32[768]{0:T...) while((s32[]{:T(128)}, ...), condition=%wide.region_22.23_spmd, body=%wide.region_20.22_spmd.sunk | while | flops 33258632 | bytes 3909683 | solution.py:117
  958.8 3.0 fusion.127
  963.1 2.5 convolution_convert_fusion.2
  965.6 2.0 all_to_all.30
  967.6 9.4 all-to-all-start.2
  978.0 2.1 convolution_add_fusion
  980.0 11.5 %all-to-all-done.2 = bf16[128,6,256]{2,1,0:T(8,128)(2,1)S(1)} async-done(((bf16[128,6,256]{2,1,0:T(8,128)(2,1)}), bf16[128,6,256]{2,1,0:T(8,128)(2,1)S(1)}, u32[]{:S(2)}, u32[]{:S(2)}) %all-to-all-start.2) | async-done | bytes 393248 | tf_op jit(solution)/shard_map/all_to_all | solution.py:464
  992.7 135.4 %all-reduce.3.cloned.1.call-done = (f32[512,512]{0,1:T(8,128)}, f32[256,1024]{1,0:T(8,128)}, f32[512,512]{1,0:T(8,128)}, f32[512,1536]{1,0:T(8,128)}, f32[512,512]{1,0:T(8,128)}) async-done(((f32[512,512]{0,1:T(8,128)}, f32[256,1024]{1,0:T(8,128)}, f32[512,512]{1,0:T(8,128)}, f32[512,1536]{1,0:T(8,128)}, f32[512,512]{1,0:T(8,128)}), (f32[512,512]{0,1:T(8,128)}, f32[256,1024]{1,0:T(8,128)}, ...) | async-done | bytes 7340048 | tf_op jit(solution)/shard_map/psum | solution.py:468
  1128.1 2.6 copy.39
  (1176 shorter events, 752.5 us)
Async XLA Ops:
  7.2 127.5 %copy-start = (bf16[512,1536]{1,0:T(8,128)(2,1)S(1)}, bf16[512,1536]{1,0:T(8,128)(2,1)}, u32[]{:S(2)}) copy-start(bf16[512,1536]{1,0:T(8,128)(2,1)} %param.35) | copy-start | bytes 4718596
  8.2 28.9 %copy-start.13 = (bf16[512,512]{1,0:T(8,128)(2,1)S(1)}, bf16[512,512]{1,0:T(8,128)(2,1)}, u32[]{:S(2)}) copy-start(bf16[512,512]{1,0:T(8,128)(2,1)} %param.32) | copy-start | bytes 1572868
  8.2 28.9 %copy-start.16 = (bf16[8,16,512]{2,1,0:T(8,128)(2,1)S(1)}, bf16[8,16,512]{2,1,0:T(8,128)(2,1)}, u32[]{:S(2)}) copy-start(bf16[8,16,512]{2,1,0:T(8,128)(2,1)} %param.27) | copy-start | bytes 393220
  9.0 29.0 %copy-start.37 = (s32[256]{0:T(256)}, s32[256]{0:T(256)S(1)}, u32[]{:S(2)}) copy-start(s32[256]{0:T(256)S(1)} %convert_add_fusion) | copy-start | bytes 3076
  10.9 20.9 %all-to-all-start = ((bf16[128,6,2]{1,2,0:T(2,128)(2,1)}), bf16[128,6,2]{1,2,0:T(2,128)(2,1)S(1)}, u32[]{:S(2)}, u32[]{:S(2)}) async-start(bf16[128,6,2]{1,2,0:T(2,128)(2,1)} %copy.27), calls=%async_computation | async-start | bytes 131072 | tf_op jit(solution)/shard_map/all_to_all | solution.py:388
  22.4 15.6 %copy-start.11 = (bf16[512,512]{1,0:T(8,128)(2,1)S(1)}, bf16[512,512]{1,0:T(8,128)(2,1)}, u32[]{:S(2)}) copy-start(bf16[512,512]{1,0:T(8,128)(2,1)} %param.36) | copy-start | bytes 1572868
  22.4 15.6 %copy-start.33 = (bf16[8,16,512]{2,1,0:T(8,128)(2,1)S(1)}, bf16[8,16,512]{2,1,0:T(8,128)(2,1)}, u32[]{:S(2)}) copy-start(bf16[8,16,512]{2,1,0:T(8,128)(2,1)} %param.37) | copy-start | bytes 393220
  32.4 18.1 %all-to-all-start.1 = ((bf16[128,6,256]{2,1,0:T(8,128)(2,1)}), bf16[128,6,256]{2,1,0:T(8,128)(2,1)S(1)}, u32[]{:S(2)}, u32[]{:S(2)}) async-start(bf16[128,6,256]{2,1,0:T(8,128)(2,1)} %all_to_all.27), calls=%async_computation.1 | async-start | bytes 1048576 | tf_op jit(solution)/shard_map/all_to_all | solution.py:387
  37.0 1091.1 %all-reduce.3.cloned.1.call-start = ((), (), s32[]{:S(2)}) async-start(), calls=%async_computation.3 | async-start | bytes 14680064 | tf_op jit(solution)/shard_map/psum | solution.py:468
  38.0 13.4 %copy-start.23 = (bf16[256,1024]{1,0:T(8,128)(2,1)S(1)}, bf16[256,1024]{1,0:T(8,128)(2,1)}, u32[]{:S(2)}) copy-start(bf16[256,1024]{1,0:T(8,128)(2,1)} %param.33) | copy-start | bytes 1572868
  38.3 99.1 %copy-start.7 = (bf16[128,512]{1,0:T(8,128)(2,1)}, bf16[128,512]{1,0:T(8,128)(2,1)S(1)}, u32[]{:S(2)}) copy-start(bf16[128,512]{1,0:T(8,128)(2,1)S(1)} %convolution_convert_fusion.6) | copy-start | bytes 393220
  133.0 2.1 copy-start.1
  133.0 2.1 copy-start.4
  133.0 2.1 copy-start.35
  135.9 6.2 collective-permute-start.1
  136.9 7.3 collective-permute-start
  137.9 12.1 %collective-permute-start.12 = (bf16[6,16,1024]{2,0,1:T(8,128)(2,1)S(1)}, bf16[6,16,1024]{2,0,1:T(8,128)(2,1)S(1)}, u32[]{:S(2)}, u32[]{:S(2)}) collective-permute-start(bf16[6,16,1024]{2,0,1:T(8,128)(2,1)S(1)} %copy.33), channel_id=1, source_target_pairs={{0,16},{16,32},{32,48},{48,64},{64,80},{80,96},{96,112},{112,0},{1... | collective-permute-start | bytes 589832 | tf_op jit(solution)/shard_map/ppermute | solution.py:22
  138.0 12.1 %collective-permute-start.13 = (bf16[6,16,1024]{2,0,1:T(8,128)(2,1)S(1)}, bf16[6,16,1024]{2,0,1:T(8,128)(2,1)S(1)}, u32[]{:S(2)}, u32[]{:S(2)}) collective-permute-start(bf16[6,16,1024]{2,0,1:T(8,128)(2,1)S(1)} %copy.34), channel_id=1, source_target_pairs={{16,0},{32,16},{48,32},{64,48},{80,64},{96,80},{112,96},{0,112},{1... | collective-permute-start | bytes 589832 | tf_op jit(solution)/shard_map/ppermute | solution.py:24
  145.3 12.3 %collective-permute-start.2 = (bf16[20,6,1024]{2,1,0:T(8,128)(2,1)S(1)}, bf16[20,6,1024]{2,1,0:T(8,128)(2,1)S(1)}, u32[]{:S(2)}, u32[]{:S(2)}) collective-permute-start(bf16[20,6,1024]{2,1,0:T(8,128)(2,1)S(1)} %get-tuple-element.1431), channel_id=1, source_target_pairs={{0,1},{1,2},{2,3},{3,4},{4,5},{5,6},{6,7},{7,8},{8,9},{9,10},{10,1... | collective-permute-start | bytes 737288 | tf_op jit(solution)/shard_map/ppermute | solution.py:22
  150.1 11.5 %collective-permute-start.3 = (bf16[20,6,1024]{2,1,0:T(8,128)(2,1)S(1)}, bf16[20,6,1024]{2,1,0:T(8,128)(2,1)S(1)}, u32[]{:S(2)}, u32[]{:S(2)}) collective-permute-start(bf16[20,6,1024]{2,1,0:T(8,128)(2,1)S(1)} %get-tuple-element.1432), channel_id=1, source_target_pairs={{1,0},{2,1},{3,2},{4,3},{5,4},{6,5},{7,6},{8,7},{9,8},{10,9},{11,1... | collective-permute-start | bytes 737288 | tf_op jit(solution)/shard_map/ppermute | solution.py:24
  150.4 7.2 copy-start.2
  151.4 421.9 %collective-permute-start.14 = (bf16[20,6,1024]{2,0,1:T(8,128)(2,1)}, bf16[20,6,1024]{2,0,1:T(8,128)(2,1)}, u32[]{:S(2)}, u32[]{:S(2)}) collective-permute-start(bf16[20,6,1024]{2,0,1:T(8,128)(2,1)} %get-tuple-element.1427), channel_id=1, source_target_pairs={{0,1},{1,2},{2,3},{3,4},{4,5},{5,6},{6,7},{7,8},{8,9},{9,10},{10,1... | collective-permute-start | bytes 737288 | tf_op jit(solution)/shard_map/ppermute | solution.py:22
  154.6 420.1 %collective-permute-start.15 = (bf16[20,6,1024]{2,0,1:T(8,128)(2,1)}, bf16[20,6,1024]{2,0,1:T(8,128)(2,1)}, u32[]{:S(2)}, u32[]{:S(2)}) collective-permute-start(bf16[20,6,1024]{2,0,1:T(8,128)(2,1)} %get-tuple-element.1428), channel_id=1, source_target_pairs={{1,0},{2,1},{3,2},{4,3},{5,4},{6,5},{7,6},{8,7},{9,8},{10,9},{11,1... | collective-permute-start | bytes 737288 | tf_op jit(solution)/shard_map/ppermute | solution.py:24
  566.7 7.9 copy-start.3
  568.9 11.8 %collective-permute-start.5 = (f32[6,16,16]{1,0,2:T(8,128)S(1)}, f32[6,16,16]{1,0,2:T(8,128)S(1)}, u32[]{:S(2)}, u32[]{:S(2)}) collective-permute-start(f32[6,16,16]{1,0,2:T(8,128)S(1)} %slice.165), channel_id=1, source_target_pairs={{16,0},{32,16},{48,32},{64,48},{80,64},{96,80},{112,96},{0,112},{1... | collective-permute-start | bytes 18440 | tf_op jit(solution)/shard_map/ppermute | solution.py:24
  568.9 8.2 collective-permute-start.9
  569.0 11.6 %collective-permute-start.4 = (f32[6,16,16]{1,0,2:T(8,128)S(1)}, f32[6,16,16]{1,0,2:T(8,128)S(1)}, u32[]{:S(2)}, u32[]{:S(2)}) collective-permute-start(f32[6,16,16]{1,0,2:T(8,128)S(1)} %slice.163), channel_id=1, source_target_pairs={{0,16},{16,32},{32,48},{48,64},{64,80},{80,96},{96,112},{112,0},{1... | collective-permute-start | bytes 18440 | tf_op jit(solution)/shard_map/ppermute | solution.py:22
  573.3 6.1 collective-permute-start.8
  579.5 6.5 collective-permute-start.10
  580.6 8.7 collective-permute-start.11
  580.8 9.4 collective-permute-start.6
  584.1 7.3 collective-permute-start.7
  604.6 102.5 %copy-start.27 = (bf16[2,64,512]{2,1,0:T(8,128)(2,1)S(1)}, bf16[2,64,512]{2,1,0:T(8,128)(2,1)}, u32[]{:S(2)}) copy-start(bf16[2,64,512]{2,1,0:T(8,128)(2,1)} %get-tuple-element.2461) | copy-start | bytes 393220 | tf_op jit(solution)/shard_map/while
  604.6 102.5 %copy-start.30 = (bf16[2,64,512]{2,1,0:T(8,128)(2,1)S(1)}, bf16[2,64,512]{2,1,0:T(8,128)(2,1)}, u32[]{:S(2)}) copy-start(bf16[2,64,512]{2,1,0:T(8,128)(2,1)} %get-tuple-element.2460) | copy-start | bytes 393220 | tf_op jit(solution)/shard_map/while
  718.7 102.5 %copy-start.27 = (bf16[2,64,512]{2,1,0:T(8,128)(2,1)S(1)}, bf16[2,64,512]{2,1,0:T(8,128)(2,1)}, u32[]{:S(2)}) copy-start(bf16[2,64,512]{2,1,0:T(8,128)(2,1)} %get-tuple-element.2461) | copy-start | bytes 393220 | tf_op jit(solution)/shard_map/while
  718.7 102.5 %copy-start.30 = (bf16[2,64,512]{2,1,0:T(8,128)(2,1)S(1)}, bf16[2,64,512]{2,1,0:T(8,128)(2,1)}, u32[]{:S(2)}) copy-start(bf16[2,64,512]{2,1,0:T(8,128)(2,1)} %get-tuple-element.2460) | copy-start | bytes 393220 | tf_op jit(solution)/shard_map/while
  821.9 2.2 copy-start.19
  825.4 2.3 copy-start.5
  825.4 2.3 copy-start.36
  827.7 129.9 %copy-start.17 = (bf16[8,16,512]{2,1,0:T(8,128)(2,1)S(1)}, bf16[8,16,512]{2,1,0:T(8,128)(2,1)}, u32[]{:S(2)}) copy-start(bf16[8,16,512]{2,1,0:T(8,128)(2,1)} %param.27) | copy-start | bytes 393220
  827.7 131.1 %copy-start.15 = (bf16[768,256]{1,0:T(8,128)(2,1)S(1)}, bf16[768,256]{1,0:T(8,128)(2,1)}, u32[]{:S(2)}) copy-start(bf16[768,256]{1,0:T(8,128)(2,1)} %copy-done.14) | copy-start | bytes 1179652
  965.6 11.4 %copy-start.12 = (bf16[512,512]{1,0:T(8,128)(2,1)S(1)}, bf16[512,512]{1,0:T(8,128)(2,1)}, u32[]{:S(2)}) copy-start(bf16[512,512]{1,0:T(8,128)(2,1)} %param.36) | copy-start | bytes 1572868
  965.6 11.4 %copy-start.25 = (bf16[2,64,512]{2,1,0:T(8,128)(2,1)S(1)}, bf16[2,64,512]{2,1,0:T(8,128)(2,1)}, u32[]{:S(2)}) copy-start(bf16[2,64,512]{2,1,0:T(8,128)(2,1)} %get-tuple-element.1064) | copy-start | bytes 393220
  967.6 23.8 %all-to-all-start.2 = ((bf16[128,6,256]{2,1,0:T(8,128)(2,1)}), bf16[128,6,256]{2,1,0:T(8,128)(2,1)S(1)}, u32[]{:S(2)}, u32[]{:S(2)}) async-start(bf16[128,6,256]{2,1,0:T(8,128)(2,1)} %all_to_all.30), calls=%async_computation.2 | async-start | bytes 1048576 | tf_op jit(solution)/shard_map/all_to_all | solution.py:464
  977.1 14.6 %copy-start.38 = (s32[256]{0:T(256)S(1)}, s32[256]{0:T(256)}, u32[]{:S(2)}) copy-start(s32[256]{0:T(256)} %copy-done.37) | copy-start | bytes 3076
  1128.1 2.6 copy-start.22
  1130.8 2.6 copy-start.6
  1133.4 2.0 copy-start.20
  (16 other events, 19.2 us)
Sparse Core Ops, SparseCore 0:
  961.9 166.1 all-reduce.2
where the time goes:
time: 1160 us; the launch traced here: 1140 us
  matrix products  425 us (37%)
  local copies, waits for them, and re-layouts  329 us (28%)
  waiting for transfers between devices  180 us (16%)
  loops' own time  112 us (10%)
  starting transfers between devices  49.9 us (4%)
  other arithmetic  31.7 us (3%)
  between operations  14.7 us (1%)
    dynamic_slice x128, local copies, waits for them, and re-layouts, cross_forward(): lax.map(one_head, jnp.arange(head_count, dtype=jnp.int32))  141 us
    psum x1, waiting for transfers between devices, on_device(): lax.psum((grad_query, grad_sensor, grad_cross, grad_local, grad_merge), (...  135 us
    dot_general x32, matrix products, one_head(): jnp.dot(grad_score, head_key, preferred_element_type=jnp.float32)  57 us
    dot_general x32, matrix products, one_head(): jnp.dot(grad_score, head_query, preferred_element_type=jnp.float32)  54.7 us
    dynamic_update_slice x64, local copies, waits for them, and re-layouts, local_forward(): lax.map(one_head, jnp.arange(head_count, dtype=jnp.int32))  42.1 us
    dot_general x32, matrix products, one_head(): jnp.dot(head_query, head_key.T, preferred_element_type=jnp.float32)  41.2 us
    dot_general x32, matrix products, one_head(): jnp.dot(head_cols(queries, head, head_width), head_cols(key_rows, head, h...  41 us
    dot_general x32, matrix products, cross_scores(): jnp.dot(head_cols(queries, head, head_width), head_cols(key_rows, head, h...  38.5 us
  transfers between devices with their start and end apart: 20, of which 11 were waited for; matrix products, arithmetic and copies ran while one was open for 33% of the time, Pallas kernels for 0%

commit v1 on v0

v1 whole, which is shorter than its diff:
```python
import functools
import math

import jax
import jax.numpy as jnp
from jax import lax
from jax.experimental import pallas as pl
from jax.experimental.pallas import tpu as pltpu
from jax.sharding import Mesh
from jax.sharding import PartitionSpec as P

B16 = jnp.bfloat16
F32 = jnp.float32
HEADS = 16
WIDTH = 32
GROUP = 4
GROUPS = HEADS // GROUP
RADIUS = 6
TH = 8
TW = 16
CELLS = TH * TW
C = 512
F = 256
OBS = 256
TILES = 128
CAP = 6
PITCH = 8
SLOTS = TILES * CAP
WIRE = TILES * PITCH
NLAT = 64
EDGE = RADIUS * TW
SIDE = 128
REGION = CELLS + 2 * EDGE
KEYS = REGION + 2 * SIDE
SCALE = 1.0 / math.sqrt(WIDTH)
LOG2E = math.log2(math.e)
LANES = GROUP * CELLS
ROWS_A = 5120
ROWS_B = 2048
VMEM_LIMIT = 44 * 1024 * 1024

ALL = ("zlo", "x", "y", "zhi", "core")
CHIPS = ("zlo", "x", "y", "zhi")
LAT = ("zlo", "x")
LON = ("y", "zhi", "core")


def dot(a, b):
    return jnp.dot(a, b, preferred_element_type=F32)


def dot_nt(a, b):
    return lax.dot_general(a, b, (((1,), (1,)), ((), ())), preferred_element_type=F32)


def iota(shape, dim):
    return lax.broadcasted_iota(jnp.int32, shape, dim)


def one_hot(condition):
    return jnp.where(condition, 1.0, 0.0).astype(B16)


def sixth(index):
    return lax.shift_right_logical(index * 10923, 16)


def call(kernel, outs, args, scratch=(), scalars=0):
    vmem = pl.BlockSpec(memory_space=pltpu.VMEM)
    smem = pl.BlockSpec(memory_space=pltpu.SMEM)
    return pl.pallas_call(
        kernel,
        out_shape=tuple(jax.ShapeDtypeStruct(s, d) for s, d in outs),
        in_specs=[smem] * scalars + [vmem] * (len(args) - scalars),
        out_specs=tuple(vmem for _ in outs),
        scratch_shapes=list(scratch),
        compiler_params=pltpu.CompilerParams(vmem_limit_bytes=VMEM_LIMIT),
    )(*args)


def route_kernel(obs, tile_row, tile_col, cell_col, accept_col, out, slot):
    tcol, trow = tile_col[...], tile_row[...]
    hits = jnp.where(tcol == iota((OBS, TILES), 1), 1.0, 0.0)
    before = one_hot(iota((OBS, OBS), 0) > iota((OBS, OBS), 1))
    rank_col = jnp.sum(dot(before, hits.astype(B16)) * hits, axis=1, keepdims=True).astype(jnp.int32)
    hits_t = jnp.where(trow == iota((TILES, OBS), 0), 1.0, 0.0)
    after = one_hot(iota((OBS, OBS), 0) < iota((OBS, OBS), 1))
    rank_row = jnp.sum(dot(hits_t.astype(B16), after) * hits_t, axis=0, keepdims=True).astype(jnp.int32)
    slot[...] = tcol * PITCH + rank_col
    lane = iota((OBS, F), 1)
    cell = cell_col[...]
    row_code = ((lax.shift_right_logical(cell, 4) + 1) * accept_col[...]).astype(F32)
    col_code = (cell & (TW - 1)).astype(F32)
    codes = (
        jnp.where(lane == rank_col, row_code, 0.0) + jnp.where(lane == rank_col + 8, col_code, 0.0)
    ).astype(B16)
    wire = iota((WIRE, OBS), 0)
    placed = one_hot(wire == trow * PITCH + rank_row)
    coded = one_hot(wire == trow * PITCH + CAP)
    out[...] = (dot(placed, obs[...]) + dot(coded, codes)).astype(B16)


def masked_heads(block):
    lane = lax.shift_right_logical(iota(block.shape, 1), 5)
    zero = jnp.zeros_like(block)
    return jnp.concatenate([jnp.where(lane == h, block, zero) for h in range(GROUP)], axis=0)


def head_blocks(stacked):
    return jnp.concatenate(
        [stacked[h * WIDTH : (h + 1) * WIDTH, h * CELLS : (h + 1) * CELLS] for h in range(GROUP)],
        axis=0,
    ).T


def fold(x, op):
    return op(x.reshape(x.shape[0] // 8, 8, x.shape[1]), axis=0)


def slope_of(group, h):
    return jnp.exp2(jnp.full((1, CELLS), 3.0, F32) - 0.5 * (group * GROUP + h).astype(F32))


def cross_kernel(
    arrived, grid, query_w, sensor_w, cross_w, local_w,
    slots_out, keyval, query, prob, att, after, local_q, local_kv,
    gap, scores,
):
    slot = iota((SLOTS, WIRE), 0)
    source = sixth(slot)
    wire = iota((SLOTS, WIRE), 1)
    rows = arrived[...]
    picked = dot(one_hot(wire == slot + 2 * source), rows).astype(B16)
    codes = dot(one_hot(wire == source * PITCH + CAP), rows[:, :128])
    slots_out[...] = picked
    keyval[...] = dot(picked, sensor_w[...]).astype(B16)
    query[...] = dot(grid[...], query_w[...]).astype(B16)

    index = iota((SLOTS, 128), 0)
    rank = index - CAP * sixth(index)
    lane = iota((SLOTS, 128), 1)
    row_code = jnp.sum(jnp.where(lane == rank, codes, 0.0), axis=1, keepdims=True)
    col_code = jnp.sum(jnp.where(lane == rank + 8, codes, 0.0), axis=1, keepdims=True)
    cell_row = lax.shift_right_logical(lane, 4).astype(F32)
    cell_col = (lane & (TW - 1)).astype(F32)
    row_gap = (cell_row - (row_code - 1.0)) * (1.0 / TH)
    col_gap = (cell_col - col_code) * (1.0 / TW)
    gap[...] = jnp.where(row_code > 0.5, -(row_gap * row_gap + col_gap * col_gap), -1e30)

    step = 96

    def one_group(g, carry):
        lanes = pl.ds(pl.multiple_of(g * 128, 128), 128)
        values = keyval[:, pl.ds(pl.multiple_of(C + g * 128, 128), 128)]
        scores[...] = dot_nt(keyval[:, lanes], masked_heads(query[:, lanes]))
        for h in range(GROUP):
            cols = slice(h * CELLS, (h + 1) * CELLS)
            slope = slope_of(g, h) * LOG2E
            top = jnp.zeros((8, CELLS), F32)
            for r in range(0, SLOTS, step):
                s = scores[r : r + step, cols] * (SCALE * LOG2E) + slope * gap[r : r + step, :]
                scores[r : r + step, cols] = s
                top = jnp.maximum(top, fold(s, jnp.max))
            top = jnp.max(top, axis=0, keepdims=True)
            total = jnp.zeros((8, CELLS), F32)
            for r in range(0, SLOTS, step):
                e = jnp.exp2(scores[r : r + step, cols] - top)
                scores[r : r + step, cols] = e
                total = total + fold(e, jnp.sum)
            total = jnp.sum(total, axis=0, keepdims=True) + jnp.exp2(-top)
            inverse = 1.0 / total
            for r in range(0, SLOTS, step):
                prob[g, r : r + step, cols] = (scores[r : r + step, cols] * inverse).astype(B16)
        att[:, lanes] = head_blocks(dot(values.T, prob[g])).astype(B16)
        return carry

    lax.fori_loop(0, GROUPS, one_group, 0)
    mixed = (grid[...].astype(F32) + dot(att[...], cross_w[...])).astype(B16)
    after[...] = mixed
    qkv = dot(mixed, local_w[...]).astype(B16)
    local_q[...] = qkv[:, :C]
    local_kv[...] = qkv[:, C:]


def side_rows(shape, key_dim, first_col):
    key = iota(shape, key_dim)
    line = sixth(key)
    wanted = line * TW + first_col + key - CAP * line
    return (iota(shape, 1 - key_dim) == wanted) & (key < (TH + 2 * RADIUS) * RADIUS)


def edges_kernel(top, own, bottom, left, right):
    region = jnp.concatenate([top[...], own[...], bottom[...]], axis=0)
    shape = (SIDE, REGION)
    left[...] = dot(one_hot(side_rows(shape, 0, 0)), region).astype(B16)
    right[...] = dot(one_hot(side_rows(shape, 0, TW - RADIUS)), region).astype(B16)


def window(lat_index, shape, key_row, key_col, valid):
    lane = iota(shape, 1)
    row_gap = key_row - lax.shift_right_logical(lane, 4)
    col_gap = key_col - (lane & (TW - 1))
    global_row = lat_index * TH + key_row
    seen = (jnp.abs(row_gap) <= RADIUS) & (jnp.abs(col_gap) <= RADIUS)
    seen = seen & (global_row >= 0) & (global_row < NLAT) & valid
    return jnp.where(seen, 0.0, -1e30)


def local_kernel(
    lat_index, query, top, own, bottom, left, right, cotangent, merge_w, after,
    updated, att, grad_query, grad_region, grad_left, grad_right,
    keyval, bias, scores, grad_prob, prob, grad_score, grad_att,
):
    lat = lat_index[0]
    keyval[0:EDGE] = top[...]
    keyval[EDGE : EDGE + CELLS] = own[...]
    keyval[EDGE + CELLS : REGION] = bottom[...]
    keyval[REGION : REGION + SIDE] = left[...]
    keyval[REGION + SIDE : KEYS] = right[...]
    grad_att[...] = dot_nt(cotangent[...], merge_w[...]).astype(B16)
    key = iota((REGION, CELLS), 0)
    bias[0:REGION] = window(
        lat, (REGION, CELLS), lax.shift_right_logical(key, 4) - RADIUS, key & (TW - 1), key >= 0
    )
    key = iota((SIDE, CELLS), 0)
    line = sixth(key)
    offset = key - CAP * line
    valid = line < TH + 2 * RADIUS
    bias[REGION : REGION + SIDE] = window(
        lat, (SIDE, CELLS), line - RADIUS, offset - RADIUS, valid
    )
    bias[REGION + SIDE : KEYS] = window(lat, (SIDE, CELLS), line - RADIUS, offset + TW, valid)

    step = 96

    def one_group(g, carry):
        lanes = pl.ds(pl.multiple_of(g * 128, 128), 128)
        upper = pl.ds(pl.multiple_of(C + g * 128, 128), 128)
        keys, values = keyval[:, lanes], keyval[:, upper]
        heads_query = masked_heads(query[:, lanes])
        heads_grad = masked_heads(grad_att[:, lanes])
        scores[...] = dot_nt(keys, heads_query)
        grad_prob[...] = dot_nt(values, heads_grad)
        for h in range(GROUP):
            cols = slice(h * CELLS, (h + 1) * CELLS)
            top_score = jnp.full((8, CELLS), -1e30, F32)
            for r in range(0, KEYS, step):
                s = scores[r : r + step, cols] * (SCALE * LOG2E) + bias[r : r + step, :]
                scores[r : r + step, cols] = s
                top_score = jnp.maximum(top_score, fold(s, jnp.max))
            top_score = jnp.max(top_score, axis=0, keepdims=True)
            total = jnp.zeros((8, CELLS), F32)
            delta = jnp.zeros((8, CELLS), F32)
            for r in range(0, KEYS, step):
                e = jnp.exp2(scores[r : r + step, cols] - top_score)
                scores[r : r + step, cols] = e
                total = total + fold(e, jnp.sum)
                delta = delta + fold(e * grad_prob[r : r + step, cols], jnp.sum)
            inverse = 1.0 / jnp.sum(total, axis=0, keepdims=True)
            delta = jnp.sum(delta, axis=0, keepdims=True) * inverse
            for r in range(0, KEYS, step):
                p = scores[r : r + step, cols] * inverse
                prob[r : r + step, cols] = p.astype(B16)
                grad_score[r : r + step, cols] = (
                    p * (grad_prob[r : r + step, cols] - delta)
                ).astype(B16)
        att[:, lanes] = head_blocks(dot(values.T, prob[...])).astype(B16)
        grad_query[:, lanes] = head_blocks(dot(keys.T, grad_score[...])) * SCALE
        grad_key = dot(grad_score[...], heads_query) * SCALE
        grad_value = dot(prob[...], heads_grad)
        for part, where_to in ((grad_key, lanes), (grad_value, upper)):
            grad_region[:, where_to] = part[0:REGION]
            grad_left[:, where_to] = part[REGION : REGION + SIDE].astype(B16)
            grad_right[:, where_to] = part[REGION + SIDE : KEYS].astype(B16)
        return carry

    lax.fori_loop(0, GROUPS, one_group, 0)
    updated[...] = (after[...].astype(F32) + dot(att[...], merge_w[...])).astype(B16)


def gather_kernel(grad_region, from_left, from_right, top, own, bottom):
    shape = (REGION, SIDE)
    total = (
        grad_region[...]
        + dot(one_hot(side_rows(shape, 1, 0)), from_left[...])
        + dot(one_hot(side_rows(shape, 1, TW - RADIUS)), from_right[...])
    )
    top[...] = total[0:EDGE].astype(B16)
    own[...] = total[EDGE : EDGE + CELLS]
    bottom[...] = total[EDGE + CELLS : REGION].astype(B16)


def put_blocks(staged, first, product):
    height = product.shape[0]
    for i in range(product.shape[1] // 128):
        at = first + i * height
        half, row = at // staged.shape[1], at % staged.shape[1]
        staged[half, row : row + height] = product[:, i * 128 : (i + 1) * 128].astype(B16)


def split_halves(core, staged, mine, send):
    for half in range(2):

        @pl.when(core == half)
        def _(half=half):
            mine[...] = staged[half]

        @pl.when(core != half)
        def _(half=half):
            send[...] = staged[half]


def mixed_kernel(
    core_index, grad_query, grad_kv, from_above, from_below, cotangent, local_w, after, cross_att,
    cross_w, local_att,
    mine, send, grad_mixed, grad_cross_att,
    staged, keyval,
):
    keyval[...] = grad_kv[...]
    keyval[0:EDGE] = keyval[0:EDGE] + from_above[...].astype(F32)
    keyval[CELLS - EDGE :] = keyval[CELLS - EDGE :] + from_below[...].astype(F32)
    grad_qkv = jnp.concatenate([grad_query[...].astype(B16), keyval[...].astype(B16)], axis=1)
    put_blocks(staged, 0, dot(local_att[...].T, cotangent[...]))
    put_blocks(staged, 4 * C, dot(after[...].T, grad_qkv))
    mixed = cotangent[...].astype(F32) + dot_nt(grad_qkv, local_w[...])
    grad_mixed[...] = mixed
    rounded = mixed.astype(B16)
    put_blocks(staged, 16 * C, dot(cross_att[...].T, rounded))
    grad_cross_att[...] = dot_nt(rounded, cross_w[...]).astype(B16)
    split_halves(core_index[0], staged, mine, send)


def cross_back_kernel(
    core_index, query, keyval, prob, grad_att, grid, query_w, sensor_w, slots, grad_mixed,
    mine, send, grad_grid, grad_wire,
    staged, grad_prob, grad_score, grad_query, grad_keyval,
):
    step = 96

    def one_group(g, carry):
        lanes = pl.ds(pl.multiple_of(g * 128, 128), 128)
        upper = pl.ds(pl.multiple_of(C + g * 128, 128), 128)
        keys, values = keyval[:, lanes], keyval[:, upper]
        heads_query = masked_heads(query[:, lanes])
        heads_grad = masked_heads(grad_att[:, lanes])
        grad_prob[...] = dot_nt(values, heads_grad)
        for h in range(GROUP):
            cols = slice(h * CELLS, (h + 1) * CELLS)
            delta = jnp.zeros((8, CELLS), F32)
            for r in range(0, SLOTS, step):
                p = prob[g, r : r + step, cols].astype(F32)
                delta = delta + fold(p * grad_prob[r : r + step, cols], jnp.sum)
            delta = jnp.sum(delta, axis=0, keepdims=True)
            for r in range(0, SLOTS, step):
                p = prob[g, r : r + step, cols].astype(F32)
                grad_score[r : r + step, cols] = (
                    p * (grad_prob[r : r + step, cols] - delta)
                ).astype(B16)
        grad_query[:, lanes] = (head_blocks(dot(keys.T, grad_score[...])) * SCALE).astype(B16)
        grad_keyval[:, lanes] = (dot(grad_score[...], heads_query) * SCALE).astype(B16)
        grad_keyval[:, upper] = dot(prob[g], heads_grad).astype(B16)
        return carry

    lax.fori_loop(0, GROUPS, one_group, 0)
    grad_slots = dot_nt(grad_keyval[...], sensor_w[...]).astype(B16)
    wire, slot = iota((WIRE, SLOTS), 0), iota((WIRE, SLOTS), 1)
    source = sixth(slot)
    grad_wire[...] = dot(one_hot(wire == slot + 2 * source), grad_slots).astype(B16)
    put_blocks(staged, 0, dot(grid[...].T, grad_query[...]))
    put_blocks(staged, ROWS_B, dot(slots[...].T, grad_keyval[...]))
    grad_grid[...] = grad_mixed[...] + dot_nt(grad_query[...], query_w[...])
    split_halves(core_index[0], staged, mine, send)


def return_kernel(slot, returned, grad_obs):
    pick = one_hot(slot[...] == iota((OBS, WIRE), 1))
    grad_obs[...] = dot(pick, returned[...]).astype(B16)


def take_blocks(halves, first, out):
    height = out.shape[0]
    for i in range(out.shape[1] // 128):
        at = first + i * height
        half, row = at // halves[0].shape[0], at % halves[0].shape[0]
        out[:, i * 128 : (i + 1) * 128] = halves[half][row : row + height].astype(F32)


def unpack_kernel(starts, core_index, mine, other, *outs):
    for core in range(2):

        @pl.when(core_index[0] == core)
        def _(core=core):
            halves = (mine, other) if core == 0 else (other, mine)
            for start, out in zip(starts, outs, strict=True):
                take_blocks(halves, start, out)


CORE_PAIRS = ((0, 1), (1, 0))


def reduced_share(mine, send):
    partner = lax.ppermute(send, "core", CORE_PAIRS)
    pair = (mine.astype(F32) + partner.astype(F32)).astype(B16)
    chips = 64
    parts = lax.all_to_all(
        pair.reshape(chips, -1, 128), CHIPS, split_axis=0, concat_axis=0, tiled=True
    )
    return jnp.sum(parts.astype(F32), axis=0).astype(B16)


def gathered_halves(share):
    chips = 64
    spread = jnp.broadcast_to(share[None], (chips,) + share.shape)
    mine = lax.all_to_all(spread, CHIPS, split_axis=0, concat_axis=0, tiled=True).reshape(-1, 128)
    return mine, lax.ppermute(mine, "core", CORE_PAIRS)


def on_device(
    grid_state, observations, target_tile, target_cell, accepted,
    query_weight, sensor_weight, cross_weight, local_weight, merge_weight, cotangent,
):
    lat = lax.axis_index(LAT).astype(jnp.int32).reshape(1)
    core = lax.axis_index("core").astype(jnp.int32).reshape(1)
    lat_count, lon_count = NLAT // TH, TILES * TH // NLAT
    down = [(i, i + 1) for i in range(lat_count - 1)]
    up = [(i + 1, i) for i in range(lat_count - 1)]
    east = [(i, (i + 1) % lon_count) for i in range(lon_count)]
    west = [((i + 1) % lon_count, i) for i in range(lon_count)]
    grid = grid_state.reshape(CELLS, C)
    grad_rows = cotangent.reshape(CELLS, C)

    outgoing, slot = call(
        route_kernel,
        [((WIRE, F), B16), ((OBS, 1), jnp.int32)],
        (
            observations, target_tile.reshape(1, OBS), target_tile,
            target_cell.reshape(OBS, 1), accepted.reshape(OBS, 1),
        ),
    )
    arrived = lax.all_to_all(
        outgoing.reshape(TILES, PITCH, F), ALL, split_axis=0, concat_axis=0, tiled=True
    ).reshape(WIRE, F)

    slots, keyval, query, prob, cross_att, after, local_q, local_kv = call(
        cross_kernel,
        [
            ((SLOTS, F), B16), ((SLOTS, 2 * C), B16), ((CELLS, C), B16),
            ((GROUPS, SLOTS, LANES), B16), ((CELLS, C), B16), ((CELLS, C), B16),
            ((CELLS, C), B16), ((CELLS, 2 * C), B16),
        ],
        (arrived, grid, query_weight, sensor_weight, cross_weight, local_weight),
        scratch=[pltpu.VMEM((SLOTS, CELLS), F32), pltpu.VMEM((SLOTS, LANES), F32)],
    )

    top = lax.ppermute(local_kv[CELLS - EDGE :], LAT, down)
    bottom = lax.ppermute(local_kv[:EDGE], LAT, up)
    send_left, send_right = call(
        edges_kernel,
        [((SIDE, 2 * C), B16), ((SIDE, 2 * C), B16)],
        (top, local_kv, bottom),
    )
    left = lax.ppermute(send_right, LON, east)
    right = lax.ppermute(send_left, LON, west)

    updated, local_att, grad_query, grad_region, grad_left, grad_right = call(
        local_kernel,
        [
            ((CELLS, C), B16), ((CELLS, C), B16), ((CELLS, C), F32),
            ((REGION, 2 * C), F32), ((SIDE, 2 * C), B16), ((SIDE, 2 * C), B16),
        ],
        (
            lat, local_q, top, local_kv, bottom, left, right, grad_rows, merge_weight, after,
        ),
        scratch=[
            pltpu.VMEM((KEYS, 2 * C), B16), pltpu.VMEM((KEYS, CELLS), F32),
            pltpu.VMEM((KEYS, LANES), F32), pltpu.VMEM((KEYS, LANES), F32),
            pltpu.VMEM((KEYS, LANES), B16), pltpu.VMEM((KEYS, LANES), B16),
            pltpu.VMEM((CELLS, C), B16),
        ],
        scalars=1,
    )
    back_right = lax.ppermute(grad_left, LON, west)
    back_left = lax.ppermute(grad_right, LON, east)
    grad_top, grad_own, grad_bottom = call(
        gather_kernel,
        [((EDGE, 2 * C), B16), ((CELLS, 2 * C), F32), ((EDGE, 2 * C), B16)],
        (grad_region, back_left, back_right),
    )
    from_below = lax.ppermute(grad_top, LAT, up)
    from_above = lax.ppermute(grad_bottom, LAT, down)

    mine_a, send_a, grad_mixed, grad_cross_att = call(
        mixed_kernel,
        [
            ((ROWS_A, 128), B16), ((ROWS_A, 128), B16), ((CELLS, C), F32), ((CELLS, C), B16),
        ],
        (
            core, grad_query, grad_own, from_above, from_below, grad_rows, local_weight, after,
            cross_att, cross_weight, local_att,
        ),
        scratch=[pltpu.VMEM((2, ROWS_A, 128), B16), pltpu.VMEM((CELLS, 2 * C), F32)],
        scalars=1,
    )
    mine_b, send_b, grad_grid, grad_wire = call(
        cross_back_kernel,
        [
            ((ROWS_B, 128), B16), ((ROWS_B, 128), B16), ((CELLS, C), F32), ((WIRE, F), B16),
        ],
        (
            core, query, keyval, prob, grad_cross_att, grid, query_weight, sensor_weight, slots,
            grad_mixed,
        ),
        scratch=[
            pltpu.VMEM((2, ROWS_B, 128), B16), pltpu.VMEM((SLOTS, LANES), F32),
            pltpu.VMEM((SLOTS, LANES), B16), pltpu.VMEM((CELLS, C), B16),
            pltpu.VMEM((SLOTS, 2 * C), B16),
        ],
        scalars=1,
    )
    share_a = reduced_share(mine_a, send_a)
    returned = lax.all_to_all(
        grad_wire.reshape(TILES, PITCH, F), ALL, split_axis=0, concat_axis=0, tiled=True
    ).reshape(WIRE, F)
    share_b = reduced_share(mine_b, send_b)
    (grad_obs,) = call(return_kernel, [((OBS, F), B16)], (slot, returned))
    grad_merge, grad_local, grad_cross = call(
        functools.partial(unpack_kernel, (0, 4 * C, 16 * C)),
        [((C, C), F32), ((C, 3 * C), F32), ((C, C), F32)],
        (core, *gathered_halves(share_a)),
        scalars=1,
    )
    grad_query_w, grad_sensor = call(
        functools.partial(unpack_kernel, (0, ROWS_B)),
        [((C, C), F32), ((F, 2 * C), F32)],
        (core, *gathered_halves(share_b)),
        scalars=1,
    )
    return (
        updated.reshape(TH, TW, C), grad_grid.reshape(TH, TW, C), grad_obs,
        grad_query_w, grad_sensor, grad_cross, grad_local, grad_merge,
    )


def solution(mesh):
    fine = Mesh(mesh.devices.reshape(2, 4, 4, 2, 2), ALL)
    in_specs = (
        P(LAT, LON, None), P(ALL, None), P(ALL, None), P(ALL), P(ALL),
        P(), P(), P(), P(), P(), P(LAT, LON, None),
    )
    out_specs = (P(LAT, LON, None), P(LAT, LON, None), P(ALL, None), P(), P(), P(), P(), P())
    return jax.shard_map(
        on_device, mesh=fine, in_specs=in_specs, out_specs=out_specs, check_vma=False
    )
```

time: 1160 us -> 231 us (0.20); the launches traced: 1140 us -> 230 us
  matrix products: 425 us -> 0 us
  local copies, waits for them, and re-layouts: 329 us -> 21.2 us
  waiting for transfers between devices: 180 us -> 47.1 us
  loops' own time: 112 us -> 0 us
  blocking collectives: 0 us -> 88.2 us
  Pallas kernels: 0 us -> 35.8 us
  other arithmetic: 31.7 us -> 2.62 us
  starting transfers between devices: 49.9 us -> 34 us
  between operations: 14.7 us -> 0.92 us
    dot_general x387 -> x0, matrix products: 425 us -> none  [the longest x32 57 us: one_head(): jnp.dot(grad_score, head_key, preferred_element_type=jnp.float32)]
    dynamic_slice x178 -> x0, local copies, waits for them, and re-layouts: 183 us -> none  [the longest x128 141 us: cross_forward(): lax.map(one_head, jnp.arange(head_count, dtype=jnp.int32))]
    psum x1 -> x0, waiting for transfers between devices: 135 us -> none  [on_device(): lax.psum((grad_query, grad_sensor, grad_cross, grad_local, grad_merge), (...]
    another operation x11 -> x0, loops' own time: 112 us -> none  [the longest x1 22.5 us: cross_forward(): lax.map(one_head, jnp.arange(head_count, dtype=jnp.int32))]
    all_to_all x0 -> x4, blocking collectives: none -> 88.2 us  [the longest x1 31.4 us: reduced_share(): lax.all_to_all(pair.reshape(chips, -1, 128), CHIPS, split_axis=0, concat_...]
    dynamic_update_slice x98 -> x0, local copies, waits for them, and re-layouts: 77.1 us -> none  [the longest x64 42.1 us: local_forward(): lax.map(one_head, jnp.arange(head_count, dtype=jnp.int32))]
    pallas_call x0 -> x10, Pallas kernels: none -> 35.8 us  [call(): pl.pallas_call(kernel, out_shape=tuple((jax.ShapeDtypeStruct(s, d) for s,...]
    ppermute x16 -> x12, waiting for transfers between devices: 15 us -> 34.3 us  [the longest x1 6.09 us: on_device(): right = lax.ppermute(send_left, LON, west)]
  transfers between devices with their start and end apart: 20 -> 14, of which waited for: 11 -> 12; matrix products, arithmetic and copies ran while one was open for 33% -> 1% of each run, Pallas kernels for 0% -> 5%
where the time goes in v1:
time: 231 us; the launch traced here: 230 us
  blocking collectives  88.2 us (38%)
  waiting for transfers between devices  47.1 us (20%)
  Pallas kernels  35.8 us (15%)
  starting transfers between devices  34 us (15%)
  local copies, waits for them, and re-layouts  21.2 us (9%)
  other arithmetic  2.62 us (1%)
    pallas_call x10, Pallas kernels, call(): pl.pallas_call(kernel, out_shape=tuple((jax.ShapeDtypeStruct(s, d) for s,...  35.8 us
    all_to_all x1, blocking collectives, reduced_share(): lax.all_to_all(pair.reshape(chips, -1, 128), CHIPS, split_axis=0, concat_...  31.4 us
    all_to_all x1, blocking collectives, on_device(): lax.all_to_all(outgoing.reshape(TILES, PITCH, F), ALL, split_axis=0, conc...  24.8 us
    unnamed x65, local copies, waits for them, and re-layouts  18.2 us
    all_to_all x1, blocking collectives, on_device(): lax.all_to_all(grad_wire.reshape(TILES, PITCH, F), ALL, split_axis=0, con...  16.7 us
    all_to_all x1, blocking collectives, gathered_halves(): lax.all_to_all(spread, CHIPS, split_axis=0, concat_axis=0, tiled=True)  15.4 us
    all_to_all x1, waiting for transfers between devices, reduced_share(): lax.all_to_all(pair.reshape(chips, -1, 128), CHIPS, split_axis=0, concat_...  11.3 us
    all_to_all x1, starting transfers between devices, reduced_share(): lax.all_to_all(pair.reshape(chips, -1, 128), CHIPS, split_axis=0, concat_...  8.72 us
  transfers between devices with their start and end apart: 14, of which 12 were waited for; matrix products, arithmetic and copies ran while one was open for 1% of the time, Pallas kernels for 5%

profile of v1, /device:TPU:1, one launch (start us, length us, event | category | flops | bytes accessed | tf_op | source)
XLA Modules:
  0.0 229.9 jit_solution(14921608899789699966)
XLA Ops:
  0.7 0.9 copy.21.cell_col
  6.3 24.8 %all_to_all.30 = bf16[128,8,256]{2,1,0:T(8,128)(2,1)S(1)} all-to-all(bf16[128,8,256]{2,1,0:T(8,128)(2,1)S(1)} %bitcast.26), channel_id=1, replica_groups=mesh['zlo'=2,'x'=4,'y'=4,'zhi'=2,'core'=2] {'zlo','x','y','zhi','core'}, dimensions={0} | all-to-all | bytes 1048576 | tf_op jit(solution)/shard_map/all_to_all | solution.py:440
  31.1 1.0 copy-done.3
  32.1 1.0 copy-done.5
  33.2 1.0 copy-done.7
  34.2 6.6 %shard_map.171 = (bf16[768,256]{1,0:T(8,128)(2,1)S(1)}, bf16[768,1024]{1,0:T(8,128)(2,1)S(1)}, bf16[128,512]{1,0:T(8,128)(2,1)S(1)}, bf16[4,768,512]{2,1,0:T(8,1...) custom-call(bf16[1024,256]{1,0:T(8,128)(2,1)S(1)} %bitcast.22, ...), custom_call_target="tpu_custom_call" | custom-call | tf_op jit(solution)/shard_map/pallas_call | solution.py:71
  40.8 1.7 copy-done.1
  42.5 1.2 copy-done.9
  45.0 1.3 collective-permute-start.1
  46.3 4.0 %collective-permute-start = (bf16[96,1024]{1,0:T(8,128)(2,1)S(1)}, bf16[96,1024]{1,0:T(8,128)(2,1)S(1)}, u32[]{:S(2)}, u32[]{:S(2)}) collective-permute-start(bf16[96,1024]{1,0:T(8,128)(2,1)S(1)} %get-tuple-element.77), channel_id=1, source_target_pairs={{0,16},{16,32},{32,48},{48,64},{64,80},{80,96},{96,112},{1,17},{17... | collective-permute-start | bytes 589832 | tf_op jit(solution)/shard_map/ppermute | solution.py:455
  50.3 2.7 %collective-permute-done.1.bottom = bf16[96,1024]{1,0:T(8,128)(2,1)S(1)} collective-permute-done((bf16[96,1024]{1,0:T(8,128)(2,1)S(1)}, bf16[96,1024]{1,0:T(8,128)(2,1)S(1)}, u32[]{:S(2)}, u32[]{:S(2)}) %collective-permute-start.1) | collective-permute-done | bytes 196640 | tf_op jit(solution)/shard_map/ppermute | solution.py:456
  53.9 1.1 shard_map.172
  55.0 2.3 collective-permute-start.2
  57.3 3.6 %collective-permute-done.2.left = bf16[128,1024]{1,0:T(8,128)(2,1)S(1)} collective-permute-done((bf16[128,1024]{1,0:T(8,128)(2,1)}, bf16[128,1024]{1,0:T(8,128)(2,1)S(1)}, u32[]{:S(2)}, u32[]{:S(2)}) %collective-permute-start.2) | collective-permute-done | bytes 262176 | tf_op jit(solution)/shard_map/ppermute | solution.py:462
  61.6 6.1 %collective-permute-done.3.right = bf16[128,1024]{1,0:T(8,128)(2,1)} collective-permute-done((bf16[128,1024]{1,0:T(8,128)(2,1)}, bf16[128,1024]{1,0:T(8,128)(2,1)}, u32[]{:S(2)}, u32[]{:S(2)}) %collective-permute-start.3) | collective-permute-done | bytes 262176 | tf_op jit(solution)/shard_map/ppermute | solution.py:463
  67.7 0.9 copy-done.17
  68.7 0.9 copy-done.23
  69.6 8.6 %shard_map.173 = (bf16[128,512]{1,0:T(8,128)(2,1)}, bf16[128,512]{1,0:T(8,128)(2,1)S(1)}, f32[128,512]{1,0:T(8,128)S(1)}, f32[320,1024]{1,0:T(8,128)S(1)}, bf16[...) custom-call(s32[1]{0:T(128)} %bitcast.lat_index, bf16[128,512]{1,0:T(8,128)(2,1)S(1)} %copy-done.23, ...), custom_call_target="tpu_custom_call" | custom-call | tf_op jit(solution)/shard_map/pallas_call | solution.py:71
  78.7 5.6 %collective-permute-done.4.from_left = bf16[128,1024]{1,0:T(8,128)(2,1)S(1)} collective-permute-done((bf16[128,1024]{1,0:T(8,128)(2,1)S(1)}, bf16[128,1024]{1,0:T(8,128)(2,1)S(1)}, u32[]{:S(2)}, u32[]{:S(2)}) %collective-permute-start.4) | collective-permute-done | bytes 262176 | tf_op jit(solution)/shard_map/ppermute | solution.py:483
  84.4 4.0 %collective-permute-done.5.from_right = bf16[128,1024]{1,0:T(8,128)(2,1)S(1)} collective-permute-done((bf16[128,1024]{1,0:T(8,128)(2,1)S(1)}, bf16[128,1024]{1,0:T(8,128)(2,1)S(1)}, u32[]{:S(2)}, u32[]{:S(2)}) %collective-permute-start.5) | collective-permute-done | bytes 262176 | tf_op jit(solution)/shard_map/ppermute | solution.py:482
  88.4 1.2 shard_map.174
  89.6 4.8 %collective-permute-start.6 = (bf16[96,1024]{1,0:T(8,128)(2,1)}, bf16[96,1024]{1,0:T(8,128)(2,1)}, u32[]{:S(2)}, u32[]{:S(2)}) collective-permute-start(bf16[96,1024]{1,0:T(8,128)(2,1)} %get-tuple-element.57), channel_id=1, source_target_pairs={{0,16},{16,32},{32,48},{48,64},{64,80},{80,96},{96,112},{1,17},{17... | collective-permute-start | bytes 589832 | tf_op jit(solution)/shard_map/ppermute | solution.py:490
  94.4 1.3 collective-permute-start.7
  95.7 2.1 collective-permute-done.6.from_above
  97.8 4.8 %collective-permute-done.7.from_below = bf16[96,1024]{1,0:T(8,128)(2,1)} collective-permute-done((bf16[96,1024]{1,0:T(8,128)(2,1)}, bf16[96,1024]{1,0:T(8,128)(2,1)}, u32[]{:S(2)}, u32[]{:S(2)}) %collective-permute-start.7) | collective-permute-done | bytes 196640 | tf_op jit(solution)/shard_map/ppermute | solution.py:489
  102.6 0.9 copy-done.25
  103.5 2.7 %shard_map.175 = (bf16[5120,128]{1,0:T(8,128)(2,1)S(1)}, bf16[5120,128]{1,0:T(8,128)(2,1)S(1)}, f32[128,512]{1,0:T(8,128)S(1)}, bf16[128,512]{1,0:T(8,128)(2,1)S(1)}) custom-call(s32[1]{0:T(128)} %bitcast.9.core_index, f32[128,512]{1,0:T(8,128)S(1)} %get-tuple-element.52.grad_query, f32[128,1024]{1,0:T(8,128)S(1)} %get-tuple-element.56.grad_kv, ...), custom_call_target="tpu_custom_call" | custom-call | tf_op jit(solution)/shard_map/pallas_call | solution.py:71
  106.4 2.9 %collective-permute-done.10 = bf16[5120,128]{1,0:T(8,128)(2,1)S(1)} collective-permute-done((bf16[5120,128]{1,0:T(8,128)(2,1)S(1)}, bf16[5120,128]{1,0:T(8,128)(2,1)S(1)}, u32[]{:S(2)}, u32[]{:S(2)}) %collective-permute-start.10) | collective-permute-done | bytes 1310752 | tf_op jit(solution)/shard_map/ppermute | solution.py:402
  109.7 31.4 %all_to_all.31 = bf16[64,80,128]{2,1,0:T(8,128)(2,1)S(1)} all-to-all(bf16[64,80,128]{2,1,0:T(8,128)(2,1)S(1)} %bitcast.30), channel_id=1, replica_groups=mesh['zlo'=2,'x'=4,'y'=4,'zhi'=2,'core'=2] {'zlo','x','y','zhi'}, dimensions={0} | all-to-all | bytes 2621440 | tf_op jit(solution)/shard_map/all_to_all | solution.py:405
  141.3 1.2 broadcast_in_dim.5
  142.5 5.4 %all-to-all-start.5 = ((bf16[64,80,128]{2,1,0:T(8,128)(2,1)}), bf16[64,80,128]{2,1,0:T(8,128)(2,1)S(1)}, u32[]{:S(2)}, u32[]{:S(2)}) async-start(bf16[64,80,128]{2,1,0:T(8,128)(2,1)} %broadcast_in_dim.5), calls=%async_computation.5 | async-start | bytes 2621440 | tf_op jit(solution)/shard_map/all_to_all | solution.py:414
  148.0 1.9 copy-done.2
  149.9 1.4 copy-done.10
  151.3 1.0 copy-done.15
  152.3 9.0 %shard_map.176 = (bf16[2048,128]{1,0:T(8,128)(2,1)S(1)}, bf16[2048,128]{1,0:T(8,128)(2,1)S(1)}, f32[128,512]{1,0:T(8,128)}, bf16[1024,256]{1,0:T(8,128)(2,1)S(1)}) custom-call(s32[1]{0:T(128)} %bitcast.9.core_index, bf16[128,512]{1,0:T(8,128)(2,1)S(1)} %copy-done.21, bf16[768,1024]{1,0:T(8,128)(2,1)S(1)} %copy-done.10, bf16[4,768,512]{2,1,0:T(8,128)(2,1)S(1)} %copy-done.2, ...), custom_call_target="tpu_custom_call" | custom-call | tf_op jit(solution)/shard_map/pallas_call | solution.py:71
  161.3 1.5 collective-permute-start.8
  162.8 1.5 collective-permute-done.8
  164.4 0.9 add_convert_fusion.1
  165.3 1.5 all-to-all-done.5
  166.8 8.7 %all-to-all-start.2 = ((bf16[64,32,128]{2,1,0:T(8,128)(2,1)}), bf16[64,32,128]{2,1,0:T(8,128)(2,1)}, u32[]{:S(2)}, u32[]{:S(2)}) async-start(bf16[64,32,128]{2,1,0:T(8,128)(2,1)} %bitcast.13), calls=%async_computation.2 | async-start | bytes 1048576 | tf_op jit(solution)/shard_map/all_to_all | solution.py:405
  176.2 11.3 %all-to-all-done.2 = bf16[64,32,128]{2,1,0:T(8,128)(2,1)} async-done(((bf16[64,32,128]{2,1,0:T(8,128)(2,1)}), bf16[64,32,128]{2,1,0:T(8,128)(2,1)}, u32[]{:S(2)}, u32[]{:S(2)}) %all-to-all-start.2) | async-done | bytes 524320 | tf_op jit(solution)/shard_map/all_to_all | solution.py:405
  187.5 1.1 reduce_sum.24
  188.8 15.4 %all_to_all.32 = bf16[64,32,128]{2,1,0:T(8,128)(2,1)S(1)} all-to-all(bf16[64,32,128]{2,1,0:T(8,128)(2,1)S(1)} %broadcast_in_dim.4), channel_id=1, replica_groups=mesh['zlo'=2,'x'=4,'y'=4,'zhi'=2,'core'=2] {'zlo','x','y','zhi'}, dimensions={0} | all-to-all | bytes 1048576 | tf_op jit(solution)/shard_map/all_to_all | solution.py:414
  204.2 3.4 %collective-permute-start.9 = (bf16[2048,128]{1,0:T(8,128)(2,1)S(1)}, bf16[2048,128]{1,0:T(8,128)(2,1)S(1)}, u32[]{:S(2)}, u32[]{:S(2)}) collective-permute-start(bf16[2048,128]{1,0:T(8,128)(2,1)S(1)} %bitcast.19), channel_id=1, source_target_pairs={{0,1},{1,0},{2,3},{3,2},{4,5},{5,4},{6,7},{7,6},{8,9},{9,8},{10,11... | collective-permute-start | bytes 1572872 | tf_op jit(solution)/shard_map/ppermute | solution.py:415
  207.5 16.7 %all_to_all.33 = bf16[128,8,256]{2,1,0:T(8,128)(2,1)S(1)} all-to-all(bf16[128,8,256]{2,1,0:T(8,128)(2,1)S(1)} %bitcast.25), channel_id=1, replica_groups=mesh['zlo'=2,'x'=4,'y'=4,'zhi'=2,'core'=2] {'zlo','x','y','zhi','core'}, dimensions={0} | all-to-all | bytes 1048576 | tf_op jit(solution)/shard_map/all_to_all | solution.py:521
  224.3 1.0 shard_map.177
  225.3 1.6 shard_map.178
  226.9 3.0 %shard_map.179 = (f32[512,512]{1,0:T(8,128)}, f32[512,1536]{1,0:T(8,128)}, f32[512,512]{1,0:T(8,128)}) custom-call(s32[1]{0:T(128)} %bitcast.9.core_index, bf16[5120,128]{1,0:T(8,128)(2,1)S(1)} %bitcast.18, bf16[5120,128]{1,0:T(8,128)(2,1)S(1)} %collective-permute-done.11.other), custom_call_target="tpu_custom_call" | custom-call | tf_op jit(solution)/shard_map/pallas_call | solution.py:71
  (68 shorter events, 9.8 us)
Async XLA Ops:
  0.6 30.4 %copy-start = (bf16[512,1536]{1,0:T(8,128)(2,1)S(1)}, bf16[512,1536]{1,0:T(8,128)(2,1)}, u32[]{:S(2)}) copy-start(bf16[512,1536]{1,0:T(8,128)(2,1)} %local_w.3) | copy-start | bytes 4718596
  0.6 30.4 %copy-start.13 = (bf16[8,16,512]{2,1,0:T(8,128)(2,1)S(1)}, bf16[8,16,512]{2,1,0:T(8,128)(2,1)}, u32[]{:S(2)}) copy-start(bf16[8,16,512]{2,1,0:T(8,128)(2,1)} %param.11) | copy-start | bytes 393220
  3.2 0.9 copy-start.28
  4.1 0.7 copy-start.31
  5.7 0.7 copy-start.29
  31.1 1.0 copy-start.3
  32.1 1.0 copy-start.5
  33.2 1.0 copy-start.7
  40.8 1.7 copy-start.1
  42.5 1.2 copy-start.9
  43.6 0.7 copy-start.22
  44.3 0.7 copy-start.14
  44.3 10.7 %copy-start.20 = (bf16[128,512]{1,0:T(8,128)(2,1)}, bf16[128,512]{1,0:T(8,128)(2,1)S(1)}, u32[]{:S(2)}) copy-start(bf16[128,512]{1,0:T(8,128)(2,1)S(1)} %get-tuple-element.49.query) | copy-start | bytes 393220
  44.3 23.4 %copy-start.11 = (bf16[512,512]{1,0:T(8,128)(2,1)S(1)}, bf16[512,512]{1,0:T(8,128)(2,1)}, u32[]{:S(2)}) copy-start(bf16[512,512]{1,0:T(8,128)(2,1)} %merge_w.1) | copy-start | bytes 1572868
  44.3 23.4 %copy-start.12 = (bf16[8,16,512]{2,1,0:T(8,128)(2,1)S(1)}, bf16[8,16,512]{2,1,0:T(8,128)(2,1)}, u32[]{:S(2)}) copy-start(bf16[8,16,512]{2,1,0:T(8,128)(2,1)} %param.21) | copy-start | bytes 393220
  45.0 8.0 %collective-permute-start.1 = (bf16[96,1024]{1,0:T(8,128)(2,1)S(1)}, bf16[96,1024]{1,0:T(8,128)(2,1)S(1)}, u32[]{:S(2)}, u32[]{:S(2)}) collective-permute-start(bf16[96,1024]{1,0:T(8,128)(2,1)S(1)} %get-tuple-element.76), channel_id=1, source_target_pairs={{16,0},{32,16},{48,32},{64,48},{80,64},{96,80},{112,96},{17,1},{33... | collective-permute-start | bytes 589832 | tf_op jit(solution)/shard_map/ppermute | solution.py:456
  46.3 7.6 %collective-permute-start = (bf16[96,1024]{1,0:T(8,128)(2,1)S(1)}, bf16[96,1024]{1,0:T(8,128)(2,1)S(1)}, u32[]{:S(2)}, u32[]{:S(2)}) collective-permute-start(bf16[96,1024]{1,0:T(8,128)(2,1)S(1)} %get-tuple-element.77), channel_id=1, source_target_pairs={{0,16},{16,32},{32,48},{48,64},{64,80},{80,96},{96,112},{1,17},{17... | collective-permute-start | bytes 589832 | tf_op jit(solution)/shard_map/ppermute | solution.py:455
  55.0 5.9 %collective-permute-start.2 = (bf16[128,1024]{1,0:T(8,128)(2,1)}, bf16[128,1024]{1,0:T(8,128)(2,1)S(1)}, u32[]{:S(2)}, u32[]{:S(2)}) collective-permute-start(bf16[128,1024]{1,0:T(8,128)(2,1)} %get-tuple-element.45), channel_id=1, source_target_pairs={{0,1},{1,2},{2,3},{3,4},{4,5},{5,6},{6,7},{7,8},{8,9},{9,10},{10,1... | collective-permute-start | bytes 786440 | tf_op jit(solution)/shard_map/ppermute | solution.py:462
  57.3 10.4 %collective-permute-start.3 = (bf16[128,1024]{1,0:T(8,128)(2,1)}, bf16[128,1024]{1,0:T(8,128)(2,1)}, u32[]{:S(2)}, u32[]{:S(2)}) collective-permute-start(bf16[128,1024]{1,0:T(8,128)(2,1)} %get-tuple-element.46), channel_id=1, source_target_pairs={{1,0},{2,1},{3,2},{4,3},{5,4},{6,5},{7,6},{8,7},{9,8},{10,9},{11,1... | collective-permute-start | bytes 786440 | tf_op jit(solution)/shard_map/ppermute | solution.py:463
  60.9 0.7 copy-start.16
  67.7 1.0 copy-start.17
  68.7 0.9 copy-start.23
  78.2 11.4 %copy-start.24 = (bf16[128,512]{1,0:T(8,128)(2,1)}, bf16[128,512]{1,0:T(8,128)(2,1)S(1)}, u32[]{:S(2)}) copy-start(bf16[128,512]{1,0:T(8,128)(2,1)S(1)} %get-tuple-element.60.local_att) | copy-start | bytes 393220
  78.2 24.3 %copy-start.4 = (bf16[512,512]{1,0:T(8,128)(2,1)S(1)}, bf16[512,512]{1,0:T(8,128)(2,1)}, u32[]{:S(2)}) copy-start(bf16[512,512]{1,0:T(8,128)(2,1)} %cross_w.3) | copy-start | bytes 1572868
  78.2 6.1 %collective-permute-start.4 = (bf16[128,1024]{1,0:T(8,128)(2,1)S(1)}, bf16[128,1024]{1,0:T(8,128)(2,1)S(1)}, u32[]{:S(2)}, u32[]{:S(2)}) collective-permute-start(bf16[128,1024]{1,0:T(8,128)(2,1)S(1)} %get-tuple-element.54), channel_id=1, source_target_pairs={{0,1},{1,2},{2,3},{3,4},{4,5},{5,6},{6,7},{7,8},{8,9},{9,10},{10,1... | collective-permute-start | bytes 786440 | tf_op jit(solution)/shard_map/ppermute | solution.py:483
  78.2 10.2 %collective-permute-start.5 = (bf16[128,1024]{1,0:T(8,128)(2,1)S(1)}, bf16[128,1024]{1,0:T(8,128)(2,1)S(1)}, u32[]{:S(2)}, u32[]{:S(2)}) collective-permute-start(bf16[128,1024]{1,0:T(8,128)(2,1)S(1)} %get-tuple-element.55), channel_id=1, source_target_pairs={{1,0},{2,1},{3,2},{4,3},{5,4},{6,5},{7,6},{8,7},{9,8},{10,9},{11,1... | collective-permute-start | bytes 786440 | tf_op jit(solution)/shard_map/ppermute | solution.py:482
  89.6 8.2 %collective-permute-start.6 = (bf16[96,1024]{1,0:T(8,128)(2,1)}, bf16[96,1024]{1,0:T(8,128)(2,1)}, u32[]{:S(2)}, u32[]{:S(2)}) collective-permute-start(bf16[96,1024]{1,0:T(8,128)(2,1)} %get-tuple-element.57), channel_id=1, source_target_pairs={{0,16},{16,32},{32,48},{48,64},{64,80},{80,96},{96,112},{1,17},{17... | collective-permute-start | bytes 589832 | tf_op jit(solution)/shard_map/ppermute | solution.py:490
  94.4 8.2 %collective-permute-start.7 = (bf16[96,1024]{1,0:T(8,128)(2,1)}, bf16[96,1024]{1,0:T(8,128)(2,1)}, u32[]{:S(2)}, u32[]{:S(2)}) collective-permute-start(bf16[96,1024]{1,0:T(8,128)(2,1)} %get-tuple-element.58), channel_id=1, source_target_pairs={{16,0},{32,16},{48,32},{64,48},{80,64},{96,80},{112,96},{17,1},{33... | collective-permute-start | bytes 589832 | tf_op jit(solution)/shard_map/ppermute | solution.py:489
  102.6 0.9 copy-start.25
  106.2 3.5 %copy-start.18 = (f32[128,512]{1,0:T(8,128)}, f32[128,512]{1,0:T(8,128)S(1)}, u32[]{:S(2)}) copy-start(f32[128,512]{1,0:T(8,128)S(1)} %get-tuple-element.63.grad_mixed) | copy-start | bytes 786436
  106.2 3.5 %copy-start.26 = (bf16[128,512]{1,0:T(8,128)(2,1)}, bf16[128,512]{1,0:T(8,128)(2,1)S(1)}, u32[]{:S(2)}) copy-start(bf16[128,512]{1,0:T(8,128)(2,1)S(1)} %get-tuple-element.61.grad_att) | copy-start | bytes 393220
  106.2 3.1 %collective-permute-start.10 = (bf16[5120,128]{1,0:T(8,128)(2,1)S(1)}, bf16[5120,128]{1,0:T(8,128)(2,1)S(1)}, u32[]{:S(2)}, u32[]{:S(2)}) collective-permute-start(bf16[5120,128]{1,0:T(8,128)(2,1)S(1)} %get-tuple-element.72), channel_id=1, source_target_pairs={{0,1},{1,0},{2,3},{3,2},{4,5},{5,4},{6,7},{7,6},{8,9},{9,8},{10,11... | collective-permute-start | bytes 3932168 | tf_op jit(solution)/shard_map/ppermute | solution.py:402
  142.5 5.4 %copy-start.6 = (bf16[512,512]{1,0:T(8,128)(2,1)S(1)}, bf16[512,512]{1,0:T(8,128)(2,1)}, u32[]{:S(2)}) copy-start(bf16[512,512]{1,0:T(8,128)(2,1)} %query_w.3) | copy-start | bytes 1572868
  142.5 5.5 %copy-start.8 = (bf16[256,1024]{1,0:T(8,128)(2,1)S(1)}, bf16[256,1024]{1,0:T(8,128)(2,1)}, u32[]{:S(2)}) copy-start(bf16[256,1024]{1,0:T(8,128)(2,1)} %sensor_w.3) | copy-start | bytes 1572868
  142.5 5.5 %copy-start.19 = (f32[128,512]{1,0:T(8,128)S(1)}, f32[128,512]{1,0:T(8,128)}, u32[]{:S(2)}) copy-start(f32[128,512]{1,0:T(8,128)} %copy-done.18) | copy-start | bytes 786436
  142.5 5.5 %copy-start.21 = (bf16[128,512]{1,0:T(8,128)(2,1)S(1)}, bf16[128,512]{1,0:T(8,128)(2,1)}, u32[]{:S(2)}) copy-start(bf16[128,512]{1,0:T(8,128)(2,1)} %copy-done.20) | copy-start | bytes 393220
  142.5 5.5 %copy-start.27 = (bf16[128,512]{1,0:T(8,128)(2,1)S(1)}, bf16[128,512]{1,0:T(8,128)(2,1)}, u32[]{:S(2)}) copy-start(bf16[128,512]{1,0:T(8,128)(2,1)} %copy-done.26) | copy-start | bytes 393220
  142.5 24.2 %all-to-all-start.5 = ((bf16[64,80,128]{2,1,0:T(8,128)(2,1)}), bf16[64,80,128]{2,1,0:T(8,128)(2,1)S(1)}, u32[]{:S(2)}, u32[]{:S(2)}) async-start(bf16[64,80,128]{2,1,0:T(8,128)(2,1)} %broadcast_in_dim.5), calls=%async_computation.5 | async-start | bytes 2621440 | tf_op jit(solution)/shard_map/all_to_all | solution.py:414
  148.0 1.9 copy-start.2
  149.9 1.4 copy-start.10
  151.3 1.0 copy-start.15
  161.3 3.1 %collective-permute-start.8 = (bf16[2048,128]{1,0:T(8,128)(2,1)S(1)}, bf16[2048,128]{1,0:T(8,128)(2,1)S(1)}, u32[]{:S(2)}, u32[]{:S(2)}) collective-permute-start(bf16[2048,128]{1,0:T(8,128)(2,1)S(1)} %get-tuple-element.68), channel_id=1, source_target_pairs={{0,1},{1,0},{2,3},{3,2},{4,5},{5,4},{6,7},{7,6},{8,9},{9,8},{10,11... | collective-permute-start | bytes 1572872 | tf_op jit(solution)/shard_map/ppermute | solution.py:402
  166.8 20.8 %all-to-all-start.2 = ((bf16[64,32,128]{2,1,0:T(8,128)(2,1)}), bf16[64,32,128]{2,1,0:T(8,128)(2,1)}, u32[]{:S(2)}, u32[]{:S(2)}) async-start(bf16[64,32,128]{2,1,0:T(8,128)(2,1)} %bitcast.13), calls=%async_computation.2 | async-start | bytes 1048576 | tf_op jit(solution)/shard_map/all_to_all | solution.py:405
  175.5 51.4 %collective-permute-start.11 = (bf16[5120,128]{1,0:T(8,128)(2,1)S(1)}, bf16[5120,128]{1,0:T(8,128)(2,1)S(1)}, u32[]{:S(2)}, u32[]{:S(2)}) collective-permute-start(bf16[5120,128]{1,0:T(8,128)(2,1)S(1)} %bitcast.17), channel_id=1, source_target_pairs={{0,1},{1,0},{2,3},{3,2},{4,5},{5,4},{6,7},{7,6},{8,9},{9,8},{10,11... | collective-permute-start | bytes 3932168 | tf_op jit(solution)/shard_map/ppermute | solution.py:415
  188.7 35.6 %copy-start.30 = (s32[256,1]{1,0:T(8,128)S(1)}, s32[256,1]{1,0:T(8,128)}, u32[]{:S(2)}) copy-start(s32[256,1]{1,0:T(8,128)} %copy-done.29) | copy-start | bytes 3076
  204.2 21.1 %collective-permute-start.9 = (bf16[2048,128]{1,0:T(8,128)(2,1)S(1)}, bf16[2048,128]{1,0:T(8,128)(2,1)S(1)}, u32[]{:S(2)}, u32[]{:S(2)}) collective-permute-start(bf16[2048,128]{1,0:T(8,128)(2,1)S(1)} %bitcast.19), channel_id=1, source_target_pairs={{0,1},{1,0},{2,3},{3,2},{4,5},{5,4},{6,7},{7,6},{8,9},{9,8},{10,11... | collective-permute-start | bytes 1572872 | tf_op jit(solution)/shard_map/ppermute | solution.py:415

commit v2 on v1

--- a/solution.py
+++ b/solution.py
@@ -1,4 +1,3 @@
-import functools
 import math
 
 import jax
@@ -35,14 +34,16 @@
 SCALE = 1.0 / math.sqrt(WIDTH)
 LOG2E = math.log2(math.e)
 LANES = GROUP * CELLS
-ROWS_A = 5120
-ROWS_B = 2048
-VMEM_LIMIT = 44 * 1024 * 1024
+SIDE_COUNT = 8
+RING = 4
+ROWS_CELLS = 5120
+ROWS_LATE = 2048
 
 ALL = ("zlo", "x", "y", "zhi", "core")
-CHIPS = ("zlo", "x", "y", "zhi")
 LAT = ("zlo", "x")
+DEPTH = ("zlo", "zhi")
 LON = ("y", "zhi", "core")
+SECTOR = ("y", "zhi")
 
 
 def dot(a, b):
@@ -65,21 +66,78 @@
     return lax.shift_right_logical(index * 10923, 16)
 
 
-def call(kernel, outs, args, scratch=(), scalars=0):
+class Arriving:
+    def __init__(self, source, buffer, semaphore):
+        self.copy = pltpu.make_async_copy(source, buffer, semaphore)
+        self.copy.start()
+        self.buffer = buffer
+
+    def __call__(self):
+        self.copy.wait()
+        return self.buffer
+
+
+def call(
+    kernel, outs, args, scratch=(), scalars=0, micros=1, after=(), loads=(), saves=(), raw=(),
+    raw_outs=(), megabytes=16,
+):
     vmem = pl.BlockSpec(memory_space=pltpu.VMEM)
     smem = pl.BlockSpec(memory_space=pltpu.SMEM)
+    hbm = pl.BlockSpec(memory_space=pltpu.HBM)
+    count, late, given, own = len(args), len(after), len(outs), len(scratch)
+
+    def body(*refs):
+        ins = list(refs[:count])
+        results = list(refs[count + late : count + late + given])
+        rest = refs[count + late + given :]
+        held, rest = rest[:own], rest[own:]
+        buffers, rest = rest[: len(loads) + len(saves)], rest[len(loads) + len(saves) :]
+        semaphores = rest[0] if rest else None
+        for k, i in enumerate(loads):
+            ins[i] = Arriving(ins[i], buffers[k], semaphores.at[k])
+        targets = list(results)
+        for k, i in enumerate(saves):
+            results[i] = buffers[len(loads) + k]
+        kernel(*ins, *results, *held)
+        leaving = [
+            pltpu.make_async_copy(results[i], targets[i], semaphores.at[len(loads) + k])
+            for k, i in enumerate(saves)
+        ]
+        for copy in leaving:
+            copy.start()
+        for copy in leaving:
+            copy.wait()
+
+    def spec_in(i):
+        if i < scalars:
+            return smem
+        return hbm if i in loads or i in raw else vmem
+
+    extra = [pltpu.VMEM(args[i].shape, args[i].dtype) for i in loads]
+    extra += [pltpu.VMEM(*outs[i]) for i in saves]
+    if extra:
+        extra.append(pltpu.SemaphoreType.DMA((len(extra),)))
     return pl.pallas_call(
-        kernel,
+        body,
         out_shape=tuple(jax.ShapeDtypeStruct(s, d) for s, d in outs),
-        in_specs=[smem] * scalars + [vmem] * (len(args) - scalars),
-        out_specs=tuple(vmem for _ in outs),
-        scratch_shapes=list(scratch),
-        compiler_params=pltpu.CompilerParams(vmem_limit_bytes=VMEM_LIMIT),
-    )(*args)
-
-
-def route_kernel(obs, tile_row, tile_col, cell_col, accept_col, out, slot):
-    tcol, trow = tile_col[...], tile_row[...]
+        in_specs=[spec_in(i) for i in range(count)]
+        + [pl.BlockSpec(memory_space=pl.ANY)] * late,
+        out_specs=tuple(hbm if i in saves or i in raw_outs else vmem for i in range(given)),
+        scratch_shapes=list(scratch) + extra,
+        compiler_params=pltpu.CompilerParams(vmem_limit_bytes=megabytes * 1024 * 1024),
+        cost_estimate=pl.CostEstimate(
+            flops=int(micros * 1e9), bytes_accessed=0, transcendentals=0
+        ),
+    )(*args, *after)
+
+
+def as_column(row):
+    return jnp.broadcast_to(row.astype(F32), (128, OBS)).T[:, :1].astype(jnp.int32)
+
+
+def route_kernel(obs, tile_row, cell_row, accept_row, out, slot):
+    trow = tile_row[...]
+    tcol = as_column(trow)
     hits = jnp.where(tcol == iota((OBS, TILES), 1), 1.0, 0.0)
     before = one_hot(iota((OBS, OBS), 0) > iota((OBS, OBS), 1))
     rank_col = jnp.sum(dot(before, hits.astype(B16)) * hits, axis=1, keepdims=True).astype(jnp.int32)
@@ -88,8 +146,8 @@
     rank_row = jnp.sum(dot(hits_t.astype(B16), after) * hits_t, axis=0, keepdims=True).astype(jnp.int32)
     slot[...] = tcol * PITCH + rank_col
     lane = iota((OBS, F), 1)
-    cell = cell_col[...]
-    row_code = ((lax.shift_right_logical(cell, 4) + 1) * accept_col[...]).astype(F32)
+    cell = as_column(cell_row[...])
+    row_code = ((lax.shift_right_logical(cell, 4) + 1) * as_column(accept_row[...])).astype(F32)
     col_code = (cell & (TW - 1)).astype(F32)
     codes = (
         jnp.where(lane == rank_col, row_code, 0.0) + jnp.where(lane == rank_col + 8, col_code, 0.0)
@@ -265,7 +323,7 @@
                     p * (grad_prob[r : r + step, cols] - delta)
                 ).astype(B16)
         att[:, lanes] = head_blocks(dot(values.T, prob[...])).astype(B16)
-        grad_query[:, lanes] = head_blocks(dot(keys.T, grad_score[...])) * SCALE
+        grad_query[:, lanes] = (head_blocks(dot(keys.T, grad_score[...])) * SCALE).astype(B16)
         grad_key = dot(grad_score[...], heads_query) * SCALE
         grad_value = dot(prob[...], heads_grad)
         for part, where_to in ((grad_key, lanes), (grad_value, upper)):
@@ -311,30 +369,34 @@
 
 
 def mixed_kernel(
-    core_index, grad_query, grad_kv, from_above, from_below, cotangent, local_w, after, cross_att,
-    cross_w, local_att,
+    core_index, grad_query, grad_kv, from_above, from_below, local_att, cotangent_in, local_in,
+    after_in, cross_att_in, cross_in,
     mine, send, grad_mixed, grad_cross_att,
     staged, keyval,
 ):
     keyval[...] = grad_kv[...]
     keyval[0:EDGE] = keyval[0:EDGE] + from_above[...].astype(F32)
     keyval[CELLS - EDGE :] = keyval[CELLS - EDGE :] + from_below[...].astype(F32)
-    grad_qkv = jnp.concatenate([grad_query[...].astype(B16), keyval[...].astype(B16)], axis=1)
+    grad_qkv = jnp.concatenate([grad_query[...], keyval[...].astype(B16)], axis=1)
+    cotangent = cotangent_in()
     put_blocks(staged, 0, dot(local_att[...].T, cotangent[...]))
-    put_blocks(staged, 4 * C, dot(after[...].T, grad_qkv))
-    mixed = cotangent[...].astype(F32) + dot_nt(grad_qkv, local_w[...])
+    put_blocks(staged, 4 * C, dot(after_in()[...].T, grad_qkv))
+    mixed = cotangent[...].astype(F32) + dot_nt(grad_qkv, local_in()[...])
     grad_mixed[...] = mixed
     rounded = mixed.astype(B16)
-    put_blocks(staged, 16 * C, dot(cross_att[...].T, rounded))
-    grad_cross_att[...] = dot_nt(rounded, cross_w[...]).astype(B16)
+    put_blocks(staged, 16 * C, dot(cross_att_in()[...].T, rounded))
+    grad_cross_att[...] = dot_nt(rounded, cross_in()[...]).astype(B16)
     split_halves(core_index[0], staged, mine, send)
 
 
 def cross_back_kernel(
-    core_index, query, keyval, prob, grad_att, grid, query_w, sensor_w, slots, grad_mixed,
+    core_index, query_in, keyval_in, prob_in, grad_att, grid, query_w, sensor_w, slots, grad_mixed,
     mine, send, grad_grid, grad_wire,
-    staged, grad_prob, grad_score, grad_query, grad_keyval,
+    staged, grad_prob, grad_score, grad_query, grad_keyval, prob, prob_came,
 ):
+    for g in range(GROUPS):
+        pltpu.make_async_copy(prob_in.at[g], prob.at[g], prob_came.at[g]).start()
+    query, keyval = query_in(), keyval_in()
     step = 96
 
     def one_group(g, carry):
@@ -344,6 +406,7 @@
         heads_query = masked_heads(query[:, lanes])
         heads_grad = masked_heads(grad_att[:, lanes])
         grad_prob[...] = dot_nt(values, heads_grad)
+        pltpu.make_async_copy(prob_in.at[g], prob.at[g], prob_came.at[g]).wait()
         for h in range(GROUP):
             cols = slice(h * CELLS, (h + 1) * CELLS)
             delta = jnp.zeros((8, CELLS), F32)
@@ -362,13 +425,13 @@
         return carry
 
     lax.fori_loop(0, GROUPS, one_group, 0)
-    grad_slots = dot_nt(grad_keyval[...], sensor_w[...]).astype(B16)
+    grad_slots = dot_nt(grad_keyval[...], sensor_w()[...]).astype(B16)
     wire, slot = iota((WIRE, SLOTS), 0), iota((WIRE, SLOTS), 1)
     source = sixth(slot)
     grad_wire[...] = dot(one_hot(wire == slot + 2 * source), grad_slots).astype(B16)
-    put_blocks(staged, 0, dot(grid[...].T, grad_query[...]))
-    put_blocks(staged, ROWS_B, dot(slots[...].T, grad_keyval[...]))
-    grad_grid[...] = grad_mixed[...] + dot_nt(grad_query[...], query_w[...])
+    put_blocks(staged, 0, dot(grid()[...].T, grad_query[...]))
+    put_blocks(staged, ROWS_LATE, dot(slots()[...].T, grad_keyval[...]))
+    grad_grid[...] = grad_mixed()[...] + dot_nt(grad_query[...], query_w()[...])
     split_halves(core_index[0], staged, mine, send)
 
 
@@ -385,34 +448,128 @@
         out[:, i * 128 : (i + 1) * 128] = halves[half][row : row + height].astype(F32)
 
 
-def unpack_kernel(starts, core_index, mine, other, *outs):
-    for core in range(2):
-
-        @pl.when(core_index[0] == core)
-        def _(core=core):
-            halves = (mine, other) if core == 0 else (other, mine)
-            for start, out in zip(starts, outs, strict=True):
-                take_blocks(halves, start, out)
+def either_core(core, pairs, write):
+    for index in range(2):
+
+        @pl.when(core == index)
+        def _(index=index):
+            write(*[(mine, other) if index == 0 else (other, mine) for mine, other in pairs])
+
+
+def unpack_cells_kernel(core_index, mine, other, merge, local, cross):
+    def write(halves):
+        take_blocks(halves, 0, merge)
+        take_blocks(halves, 4 * C, local)
+        take_blocks(halves, 16 * C, cross)
+
+    either_core(core_index[0], ((mine, other),), write)
+
+
+def unpack_late_kernel(core_index, mine, other, query, sensor):
+    def write(halves):
+        take_blocks(halves, 0, query)
+        take_blocks(halves, ROWS_LATE, sensor)
+
+    either_core(core_index[0], ((mine, other),), write)
+
+
+def summed_parts(parts):
+    total = parts[0].astype(F32)
+    for i in range(1, SIDE_COUNT):
+        total = total + parts[i].astype(F32)
+    return total.astype(B16)
+
+
+def spread_kernel(at, *refs):
+    parts, spread = refs[:RING], refs[RING]
+    rows = parts[0].shape[0]
+    for shift, part in enumerate(parts):
+        block = part[...]
+        for i in range(SIDE_COUNT):
+            spread[i, chunk(ring_place(at[0], -shift), rows)] = block
+
+
+def hold_kernel(block, same):
+    same[...] = block[...]
+
+
+def ring_place(at, shift):
+    return (at + shift) & (RING - 1)
+
+
+def chunk(index, rows):
+    return pl.ds(pl.multiple_of(index * rows, rows), rows)
+
+
+def first_kernel(at, mine, partner, *pieces):
+    rows = pieces[0].shape[0]
+    for shift, piece in enumerate(pieces):
+        block = chunk(ring_place(at[0], shift), rows)
+        piece[...] = (mine[block].astype(F32) + partner[block].astype(F32)).astype(B16)
+
+
+def band_kernel(at, bands, *refs):
+    pieces, band = refs[:RING], refs[RING]
+    band[...] = summed_parts(bands)
+    rows = pieces[0].shape[0]
+    for shift, piece in enumerate(pieces):
+        piece[...] = band[chunk(ring_place(at[0], shift), rows)]
+
+
+def summed(parts):
+    total = parts[0][...].astype(F32)
+    for part in parts[1:]:
+        total = total + part[...].astype(F32)
+    return total
+
+
+def next_kernel(at, *refs):
+    parts, pieces, total = refs[:RING], refs[RING : 2 * RING], refs[-1]
+    total[...] = summed(parts)
+    rows = pieces[0].shape[0]
+    for shift, piece in enumerate(pieces):
+        piece[...] = total[chunk(ring_place(at[0], shift), rows)].astype(B16)
+
+
+def sum_kernel(*refs):
+    refs[-1][...] = summed(refs[:-1]).astype(B16)
+
+
+def ordered_sum_kernel(at, *refs):
+    parts, out, held = refs[:RING], refs[RING], refs[RING + 1]
+    for shift, part in enumerate(parts):
+        held[ring_place(at[0], -shift)] = part[...].astype(F32)
+    out[...] = (((held[0] + held[1]) + held[2]) + held[3]).astype(B16)
+
+
+def joined_kernel(at, *refs):
+    parts, out = refs[:RING], refs[RING]
+    rows = parts[0].shape[0]
+    for shift, part in enumerate(parts):
+        out[chunk(ring_place(at[0], -shift), rows)] = part[...]
+
+
+def ring_sends(axis, pieces):
+    return [pieces[0]] + [
+        lax.ppermute(piece, axis, [(i, (i + shift) % RING) for i in range(RING)])
+        for shift, piece in enumerate(pieces)
+        if shift
+    ]
+
+
+def spot(axis):
+    return lax.axis_index(axis).astype(jnp.int32).reshape(1)
+
+
+def some(rows, count):
+    return [((rows, 128), B16)] * count
 
 
 CORE_PAIRS = ((0, 1), (1, 0))
 
 
-def reduced_share(mine, send):
-    partner = lax.ppermute(send, "core", CORE_PAIRS)
-    pair = (mine.astype(F32) + partner.astype(F32)).astype(B16)
-    chips = 64
-    parts = lax.all_to_all(
-        pair.reshape(chips, -1, 128), CHIPS, split_axis=0, concat_axis=0, tiled=True
-    )
-    return jnp.sum(parts.astype(F32), axis=0).astype(B16)
-
-
-def gathered_halves(share):
-    chips = 64
-    spread = jnp.broadcast_to(share[None], (chips,) + share.shape)
-    mine = lax.all_to_all(spread, CHIPS, split_axis=0, concat_axis=0, tiled=True).reshape(-1, 128)
-    return mine, lax.ppermute(mine, "core", CORE_PAIRS)
+def swapped_parts(blocks, axes):
+    return lax.all_to_all(blocks, axes, split_axis=0, concat_axis=0, tiled=True)
 
 
 def on_device(
@@ -433,8 +590,8 @@
         route_kernel,
         [((WIRE, F), B16), ((OBS, 1), jnp.int32)],
         (
-            observations, target_tile.reshape(1, OBS), target_tile,
-            target_cell.reshape(OBS, 1), accepted.reshape(OBS, 1),
+            observations, target_tile.reshape(1, OBS), target_cell.reshape(1, OBS),
+            accepted.reshape(1, OBS),
         ),
     )
     arrived = lax.all_to_all(
@@ -450,6 +607,7 @@
         ],
         (arrived, grid, query_weight, sensor_weight, cross_weight, local_weight),
         scratch=[pltpu.VMEM((SLOTS, CELLS), F32), pltpu.VMEM((SLOTS, LANES), F32)],
+        micros=7,
     )
 
     top = lax.ppermute(local_kv[CELLS - EDGE :], LAT, down)
@@ -465,7 +623,7 @@
     updated, local_att, grad_query, grad_region, grad_left, grad_right = call(
         local_kernel,
         [
-            ((CELLS, C), B16), ((CELLS, C), B16), ((CELLS, C), F32),
+            ((CELLS, C), B16), ((CELLS, C), B16), ((CELLS, C), B16),
             ((REGION, 2 * C), F32), ((SIDE, 2 * C), B16), ((SIDE, 2 * C), B16),
         ],
         (
@@ -478,9 +636,11 @@
             pltpu.VMEM((CELLS, C), B16),
         ],
         scalars=1,
+        micros=9,
     )
     back_right = lax.ppermute(grad_left, LON, west)
     back_left = lax.ppermute(grad_right, LON, east)
+    half = lambda rows: [((rows, 128), B16), ((rows, 128), B16)]
     grad_top, grad_own, grad_bottom = call(
         gather_kernel,
         [((EDGE, 2 * C), B16), ((CELLS, 2 * C), F32), ((EDGE, 2 * C), B16)],
@@ -489,51 +649,104 @@
     from_below = lax.ppermute(grad_top, LAT, up)
     from_above = lax.ppermute(grad_bottom, LAT, down)
 
-    mine_a, send_a, grad_mixed, grad_cross_att = call(
+    mine, send, grad_mixed, grad_cross_att = call(
         mixed_kernel,
-        [
-            ((ROWS_A, 128), B16), ((ROWS_A, 128), B16), ((CELLS, C), F32), ((CELLS, C), B16),
-        ],
+        half(ROWS_CELLS) + [((CELLS, C), F32), ((CELLS, C), B16)],
         (
-            core, grad_query, grad_own, from_above, from_below, grad_rows, local_weight, after,
-            cross_att, cross_weight, local_att,
+            core, grad_query, grad_own, from_above, from_below, local_att, grad_rows,
+            local_weight, after, cross_att, cross_weight,
         ),
-        scratch=[pltpu.VMEM((2, ROWS_A, 128), B16), pltpu.VMEM((CELLS, 2 * C), F32)],
+        scratch=[pltpu.VMEM((2, ROWS_CELLS, 128), B16), pltpu.VMEM((CELLS, 2 * C), F32)],
         scalars=1,
-    )
-    mine_b, send_b, grad_grid, grad_wire = call(
+        micros=3,
+        loads=(6, 8, 7, 9, 10),
+    )
+    cells_mine, cells_partner = mine, lax.ppermute(send, "core", CORE_PAIRS)
+    mine, send, grad_grid, grad_wire = call(
         cross_back_kernel,
-        [
-            ((ROWS_B, 128), B16), ((ROWS_B, 128), B16), ((CELLS, C), F32), ((WIRE, F), B16),
-        ],
+        half(ROWS_LATE) + [((CELLS, C), F32), ((WIRE, F), B16)],
         (
             core, query, keyval, prob, grad_cross_att, grid, query_weight, sensor_weight, slots,
             grad_mixed,
         ),
         scratch=[
-            pltpu.VMEM((2, ROWS_B, 128), B16), pltpu.VMEM((SLOTS, LANES), F32),
+            pltpu.VMEM((2, ROWS_LATE, 128), B16), pltpu.VMEM((SLOTS, LANES), F32),
             pltpu.VMEM((SLOTS, LANES), B16), pltpu.VMEM((CELLS, C), B16),
-            pltpu.VMEM((SLOTS, 2 * C), B16),
+            pltpu.VMEM((SLOTS, 2 * C), B16), pltpu.VMEM((GROUPS, SLOTS, LANES), B16),
+            pltpu.SemaphoreType.DMA((GROUPS,)),
         ],
         scalars=1,
-    )
-    share_a = reduced_share(mine_a, send_a)
+        micros=9,
+        loads=(1, 2, 5, 6, 7, 8, 9),
+        raw=(3,),
+        megabytes=20,
+    )
+    (pair,) = call(
+        sum_kernel, some(ROWS_CELLS, 1), (cells_mine, cells_partner), after=(grad_wire,)
+    )
+    parts = swapped_parts(pair.reshape(SIDE_COUNT, -1, 128), LAT)
     returned = lax.all_to_all(
         grad_wire.reshape(TILES, PITCH, F), ALL, split_axis=0, concat_axis=0, tiled=True
     ).reshape(WIRE, F)
-    share_b = reduced_share(mine_b, send_b)
-    (grad_obs,) = call(return_kernel, [((OBS, F), B16)], (slot, returned))
+    band = ROWS_CELLS // SIDE_COUNT
+    thin = band // RING
+    rows = ROWS_LATE // RING
+    pieces = call(
+        first_kernel, some(rows, RING),
+        (spot("y"), mine, lax.ppermute(send, "core", CORE_PAIRS)), scalars=1,
+    )
+    late_parts = ring_sends("y", pieces)
+    pieces = call(
+        next_kernel, some(rows // RING, RING), (spot("x"), *late_parts),
+        scratch=[pltpu.VMEM((rows, 128), F32)], scalars=1,
+    )
+    late_parts = ring_sends("x", pieces)
+    (share,) = call(sum_kernel, some(rows // RING, 1), late_parts)
+    bands = call(
+        band_kernel, some(thin, RING), (spot("y"), parts),
+        scratch=[pltpu.VMEM((band, 128), B16)], scalars=1, after=(share,),
+    )
+    late_parts = ring_sends(DEPTH, [share] * RING)
+    (share,) = call(
+        ordered_sum_kernel, some(rows // RING, 1), (spot(DEPTH), *late_parts),
+        scratch=[pltpu.VMEM((RING, rows // RING, 128), F32)], scalars=1,
+    )
+    (inner,) = call(sum_kernel, some(thin, 1), ring_sends("y", bands), after=(share,))
+    late_parts = ring_sends("x", [share] * RING)
+    (share,) = call(joined_kernel, some(rows, 1), (spot("x"), *late_parts), scalars=1)
+    (inner,) = call(
+        sum_kernel, some(thin, 1), (inner, lax.ppermute(inner, "zhi", CORE_PAIRS)),
+        after=(share,),
+    )
+    (grad_obs,) = call(
+        return_kernel, [((OBS, F), B16)], (slot, returned), after=(inner,)
+    )
+    (spread,) = call(
+        spread_kernel, [((SIDE_COUNT, band, 128), B16)],
+        (spot("y"), *ring_sends("y", [inner] * RING)), scalars=1, after=(grad_obs,),
+    )
+    gathered = lax.all_to_all(spread, LAT, split_axis=0, concat_axis=0, tiled=True)
+    late_parts = ring_sends("y", [share] * RING)
+    (share,) = call(
+        joined_kernel, some(ROWS_LATE, 1), (spot("y"), *late_parts), scalars=1, after=(spread,)
+    )
+    (gathered,) = call(
+        hold_kernel, some(ROWS_CELLS, 1), (gathered.reshape(-1, 128),), after=(share,)
+    )
+    late = (share, lax.ppermute(share, "core", CORE_PAIRS))
     grad_merge, grad_local, grad_cross = call(
-        functools.partial(unpack_kernel, (0, 4 * C, 16 * C)),
+        unpack_cells_kernel,
         [((C, C), F32), ((C, 3 * C), F32), ((C, C), F32)],
-        (core, *gathered_halves(share_a)),
+        (core, gathered, lax.ppermute(gathered, "core", CORE_PAIRS)),
         scalars=1,
+        micros=3,
     )
     grad_query_w, grad_sensor = call(
-        functools.partial(unpack_kernel, (0, ROWS_B)),
+        unpack_late_kernel,
         [((C, C), F32), ((F, 2 * C), F32)],
-        (core, *gathered_halves(share_b)),
+        (core, *late),
         scalars=1,
+        micros=2,
     )
     return (
         updated.reshape(TH, TW, C), grad_grid.reshape(TH, TW, C), grad_obs,

time: 231 us -> 212 us (0.918)
  blocking collectives: 88.2 us -> 24.8 us
  starting transfers between devices: 34 us -> 61.9 us
  waiting for transfers between devices: 47.1 us -> 63.9 us
  Pallas kernels: 35.8 us -> 42.1 us
  local copies, waits for them, and re-layouts: 21.2 us -> 17.9 us
  other arithmetic: 2.62 us -> 0 us
    all_to_all x3 -> x0, blocking collectives: 63.5 us -> none  [the longest x1 31.4 us: reduced_share(): lax.all_to_all(pair.reshape(chips, -1, 128), CHIPS, split_axis=0, concat_...]
    ppermute x4 -> x26, starting transfers between devices: 5.79 us -> 35.3 us  [the longest x21 32.3 us: ring_sends(): lax.ppermute(piece, axis, [(i, (i + shift) % RING) for i in range(RING)])]
    ppermute x4 -> x26, waiting for transfers between devices: 4.49 us -> 20.4 us  [the longest x21 13.1 us: ring_sends(): lax.ppermute(piece, axis, [(i, (i + shift) % RING) for i in range(RING)])]
    pallas_call x10 -> x22, Pallas kernels: 35.8 us -> 42.1 us  [call(): pl.pallas_call(body, out_shape=tuple((jax.ShapeDtypeStruct(s, d) for s, d...]
    ppermute x1, starting transfers between devices: 4 us -> 1.37 us  [on_device(): top = lax.ppermute(local_kv[CELLS - EDGE:], LAT, down)]
    all_to_all x2 -> x3, starting transfers between devices: 14.1 us -> 16 us  [the longest x1 7.6 us: swapped_parts(): return lax.all_to_all(blocks, axes, split_axis=0, concat_axis=0, tiled=True)]
    all_to_all x2 -> x3, waiting for transfers between devices: 12.7 us -> 11.6 us  [the longest x1 10 us: on_device(): lax.all_to_all(spread, LAT, split_axis=0, concat_axis=0, tiled=True)]
    unnamed x65 -> x86, local copies, waits for them, and re-layouts: 18.2 us -> 17.8 us
  transfers between devices with their start and end apart: 14 -> 37, of which waited for: 12 -> 21; matrix products, arithmetic and copies ran while one was open for 1% -> 0% of each run, Pallas kernels for 5% -> 7%
where the time goes in v2:
time: 212 us
  waiting for transfers between devices  63.9 us (30%)
  starting transfers between devices  61.9 us (29%)
  Pallas kernels  42.1 us (20%)
  blocking collectives  24.8 us (12%)
  local copies, waits for them, and re-layouts  17.9 us (8%)
    pallas_call x22, Pallas kernels, call(): pl.pallas_call(body, out_shape=tuple((jax.ShapeDtypeStruct(s, d) for s, d...  42.1 us
    ppermute x21, starting transfers between devices, ring_sends(): lax.ppermute(piece, axis, [(i, (i + shift) % RING) for i in range(RING)])  32.3 us
    all_to_all x1, blocking collectives, on_device(): lax.all_to_all(outgoing.reshape(TILES, PITCH, F), ALL, split_axis=0, conc...  24.8 us
    unnamed x86, local copies, waits for them, and re-layouts  17.8 us
    ppermute x21, waiting for transfers between devices, ring_sends(): lax.ppermute(piece, axis, [(i, (i + shift) % RING) for i in range(RING)])  13.1 us
    all_to_all x1, waiting for transfers between devices, on_device(): lax.all_to_all(spread, LAT, split_axis=0, concat_axis=0, tiled=True)  10 us
    all_to_all x1, starting transfers between devices, swapped_parts(): return lax.all_to_all(blocks, axes, split_axis=0, concat_axis=0, tiled=True)  7.6 us
    ppermute x1, waiting for transfers between devices, on_device(): right = lax.ppermute(send_left, LON, west)  6.78 us
  transfers between devices with their start and end apart: 37, of which 21 were waited for; matrix products, arithmetic and copies ran while one was open for 0% of the time, Pallas kernels for 7%

profile of v2, /device:TPU:1, one launch (start us, length us, event | category | flops | bytes accessed | tf_op | source)
XLA Modules:
  0.0 211.6 jit_solution(3069208160250556240)
XLA Ops:
  4.5 24.8 %all_to_all.20 = bf16[128,8,256]{2,1,0:T(8,128)(2,1)S(1)} all-to-all(bf16[128,8,256]{2,1,0:T(8,128)(2,1)S(1)} %bitcast.21), channel_id=1, replica_groups=mesh['zlo'=2,'x'=4,'y'=4,'zhi'=2,'core'=2] {'zlo','x','y','zhi','core'}, dimensions={0} | all-to-all | bytes 1048576 | tf_op jit(solution)/shard_map/all_to_all | solution.py:597
  29.3 6.6 %shard_map.171 = (bf16[768,256]{1,0:T(8,128)(2,1)S(1)}, bf16[768,1024]{1,0:T(8,128)(2,1)S(1)}, bf16[128,512]{1,0:T(8,128)(2,1)S(1)}, bf16[4,768,512]{2,1,0:T(8,1...) custom-call(bf16[1024,256]{1,0:T(8,128)(2,1)S(1)} %bitcast.20, ...), custom_call_target="tpu_custom_call" | custom-call | flops 7000000000 | tf_op jit(solution)/shard_map/pallas_call | solution.py:120
  37.9 1.4 collective-permute-start
  39.3 1.4 collective-permute-start.1
  40.7 2.6 %collective-permute-done.refs_0_.refs_2_ = bf16[96,1024]{1,0:T(8,128)(2,1)S(1)} collective-permute-done((bf16[96,1024]{1,0:T(8,128)(2,1)S(1)}, bf16[96,1024]{1,0:T(8,128)(2,1)S(1)}, u32[]{:S(2)}, u32[]{:S(2)}) %collective-permute-start) | collective-permute-done | bytes 196640 | tf_op jit(solution)/shard_map/ppermute | solution.py:613
  43.3 4.0 %collective-permute-done.1.refs_2_.refs_4_ = bf16[96,1024]{1,0:T(8,128)(2,1)S(1)} collective-permute-done((bf16[96,1024]{1,0:T(8,128)(2,1)S(1)}, bf16[96,1024]{1,0:T(8,128)(2,1)S(1)}, u32[]{:S(2)}, u32[]{:S(2)}) %collective-permute-start.1) | collective-permute-done | bytes 196640 | tf_op jit(solution)/shard_map/ppermute | solution.py:614
  48.4 2.9 %collective-permute-start.2 = (bf16[128,1024]{1,0:T(8,128)(2,1)}, bf16[128,1024]{1,0:T(8,128)(2,1)}, u32[]{:S(2)}, u32[]{:S(2)}) collective-permute-start(bf16[128,1024]{1,0:T(8,128)(2,1)} %get-tuple-element.57), channel_id=1, source_target_pairs={{0,1},{1,2},{2,3},{3,4},{4,5},{5,6},{6,7},{7,8},{8,9},{9,10},{10,1... | collective-permute-start | bytes 786440 | tf_op jit(solution)/shard_map/ppermute | solution.py:620
  51.3 3.6 %collective-permute-done.2.refs_5_ = bf16[128,1024]{1,0:T(8,128)(2,1)} collective-permute-done((bf16[128,1024]{1,0:T(8,128)(2,1)}, bf16[128,1024]{1,0:T(8,128)(2,1)}, u32[]{:S(2)}, u32[]{:S(2)}) %collective-permute-start.2) | collective-permute-done | bytes 262176 | tf_op jit(solution)/shard_map/ppermute | solution.py:620
  55.0 6.8 %collective-permute-done.3.refs_6_ = bf16[128,1024]{1,0:T(8,128)(2,1)} collective-permute-done((bf16[128,1024]{1,0:T(8,128)(2,1)}, bf16[128,1024]{1,0:T(8,128)(2,1)}, u32[]{:S(2)}, u32[]{:S(2)}) %collective-permute-start.3) | collective-permute-done | bytes 262176 | tf_op jit(solution)/shard_map/ppermute | solution.py:621
  65.4 8.7 %shard_map.173 = (bf16[128,512]{1,0:T(8,128)(2,1)}, bf16[128,512]{1,0:T(8,128)(2,1)S(1)}, bf16[128,512]{1,0:T(8,128)(2,1)S(1)}, f32[320,1024]{1,0:T(8,128)S(1)},...) custom-call(s32[1]{0:T(128)} %bitcast.refs_0_, bf16[128,512]{1,0:T(8,128)(2,1)S(1)} %copy-done.42, ...), custom_call_target="tpu_custom_call" | custom-call | flops 8999999488 | tf_op jit(solution)/shard_map/pallas_call | solution.py:120
  76.0 5.6 %collective-permute-done.4.refs_1_ = bf16[128,1024]{1,0:T(8,128)(2,1)S(1)} collective-permute-done((bf16[128,1024]{1,0:T(8,128)(2,1)S(1)}, bf16[128,1024]{1,0:T(8,128)(2,1)S(1)}, u32[]{:S(2)}, u32[]{:S(2)}) %collective-permute-start.4) | collective-permute-done | bytes 262176 | tf_op jit(solution)/shard_map/ppermute | solution.py:642
  81.6 3.4 %collective-permute-done.5.refs_2_ = bf16[128,1024]{1,0:T(8,128)(2,1)S(1)} collective-permute-done((bf16[128,1024]{1,0:T(8,128)(2,1)S(1)}, bf16[128,1024]{1,0:T(8,128)(2,1)S(1)}, u32[]{:S(2)}, u32[]{:S(2)}) %collective-permute-start.5) | collective-permute-done | bytes 262176 | tf_op jit(solution)/shard_map/ppermute | solution.py:641
  85.0 1.2 shard_map.174
  86.9 3.1 %collective-permute-start.6 = (bf16[96,1024]{1,0:T(8,128)(2,1)}, bf16[96,1024]{1,0:T(8,128)(2,1)S(1)}, u32[]{:S(2)}, u32[]{:S(2)}) collective-permute-start(bf16[96,1024]{1,0:T(8,128)(2,1)} %get-tuple-element.69), channel_id=1, source_target_pairs={{0,16},{16,32},{32,48},{48,64},{64,80},{80,96},{96,112},{1,17},{17... | collective-permute-start | bytes 589832 | tf_op jit(solution)/shard_map/ppermute | solution.py:650
  90.0 1.3 collective-permute-start.7
  91.3 2.2 %collective-permute-done.6.refs_3_ = bf16[96,1024]{1,0:T(8,128)(2,1)S(1)} collective-permute-done((bf16[96,1024]{1,0:T(8,128)(2,1)}, bf16[96,1024]{1,0:T(8,128)(2,1)S(1)}, u32[]{:S(2)}, u32[]{:S(2)}) %collective-permute-start.6) | collective-permute-done | bytes 196640 | tf_op jit(solution)/shard_map/ppermute | solution.py:650
  93.5 3.8 %collective-permute-done.7.refs_4_ = bf16[96,1024]{1,0:T(8,128)(2,1)S(1)} collective-permute-done((bf16[96,1024]{1,0:T(8,128)(2,1)S(1)}, bf16[96,1024]{1,0:T(8,128)(2,1)S(1)}, u32[]{:S(2)}, u32[]{:S(2)}) %collective-permute-start.7) | collective-permute-done | bytes 196640 | tf_op jit(solution)/shard_map/ppermute | solution.py:649
  103.6 3.2 %shard_map.175 = (bf16[5120,128]{1,0:T(8,128)(2,1)S(1)}, bf16[5120,128]{1,0:T(8,128)(2,1)S(1)}, f32[128,512]{1,0:T(8,128)S(1)}, bf16[128,512]{1,0:T(8,128)(2,1)S(1)}) custom-call(s32[1]{0:T(128)} %bitcast.9.refs_0_, bf16[128,512]{1,0:T(8,128)(2,1)S(1)} %copy-done.36, f32[128,1024]{1,0:T(8,128)S(1)} %copy-done.21, ...), custom_call_target="tpu_custom_call" | custom-call | flops 3000000000 | tf_op jit(solution)/shard_map/pallas_call | solution.py:120
  107.1 11.4 %shard_map.176 = (bf16[2048,128]{1,0:T(8,128)(2,1)S(1)}, bf16[2048,128]{1,0:T(8,128)(2,1)S(1)}, f32[128,512]{1,0:T(8,128)}, bf16[1024,256]{1,0:T(8,128)(2,1)}) custom-call(s32[1]{0:T(128)} %bitcast.9.refs_0_, bf16[128,512]{1,0:T(8,128)(2,1)S(1)} %copy-done.40, bf16[768,1024]{1,0:T(8,128)(2,1)S(1)} %copy-done.27, bf16[4,768,512]{2,1,0:T(8,128)(2,1)S(1)} %copy-done.25, ...), custom_call_target="tpu_custom_call" | custom-call | flops 8999999488 | tf_op jit(solution)/shard_map/pallas_call | solution.py:120
  118.5 1.4 shard_map.177
  119.9 7.6 %all-to-all-start.2 = ((bf16[8,640,128]{2,1,0:T(8,128)(2,1)}), bf16[8,640,128]{2,1,0:T(8,128)(2,1)S(1)}, u32[]{:S(2)}, u32[]{:S(2)}) async-start(bf16[8,640,128]{2,1,0:T(8,128)(2,1)} %bitcast.14), calls=%async_computation.2 | async-start | bytes 2621440 | tf_op jit(solution)/shard_map/all_to_all | solution.py:572
  128.2 1.5 collective-permute-done.9.refs_2_
  130.1 2.6 %collective-permute-start.12 = (bf16[512,128]{1,0:T(8,128)(2,1)S(1)}, bf16[512,128]{1,0:T(8,128)(2,1)S(1)}, u32[]{:S(2)}, u32[]{:S(2)}) collective-permute-start(bf16[512,128]{1,0:T(8,128)(2,1)S(1)} %get-tuple-element.86), channel_id=1, source_target_pairs={{0,12},{4,0},{8,4},{12,8},{1,13},{5,1},{9,5},{13,9},{2,14},{6,2},{... | collective-permute-start | bytes 393224 | tf_op jit(solution)/shard_map/ppermute | solution.py:554
  132.6 6.4 %collective-permute-done.10.refs_2_ = bf16[512,128]{1,0:T(8,128)(2,1)S(1)} collective-permute-done((bf16[512,128]{1,0:T(8,128)(2,1)S(1)}, bf16[512,128]{1,0:T(8,128)(2,1)S(1)}, u32[]{:S(2)}, u32[]{:S(2)}) %collective-permute-start.10) | collective-permute-done | bytes 131104 | tf_op jit(solution)/shard_map/ppermute | solution.py:554
  139.2 1.8 collective-permute-start.13
  141.0 2.4 %collective-permute-start.14 = (bf16[128,128]{1,0:T(8,128)(2,1)S(1)}, bf16[128,128]{1,0:T(8,128)(2,1)S(1)}, u32[]{:S(2)}, u32[]{:S(2)}) collective-permute-start(bf16[128,128]{1,0:T(8,128)(2,1)S(1)} %get-tuple-element.89), channel_id=1, source_target_pairs={{0,32},{16,48},{32,0},{48,16},{1,33},{17,49},{33,1},{49,17},{2,34}... | collective-permute-start | bytes 98312 | tf_op jit(solution)/shard_map/ppermute | solution.py:554
  143.4 1.2 collective-permute-start.15
  144.5 1.6 all-to-all-done.2.refs_1_
  146.1 4.8 %all-to-all-start.1 = ((bf16[128,8,256]{2,1,0:T(8,128)(2,1)}), bf16[128,8,256]{2,1,0:T(8,128)(2,1)S(1)}, u32[]{:S(2)}, u32[]{:S(2)}) async-start(bf16[128,8,256]{2,1,0:T(8,128)(2,1)} %bitcast.11), calls=%async_computation.1 | async-start | bytes 1048576 | tf_op jit(solution)/shard_map/all_to_all | solution.py:688
  151.0 3.5 %collective-permute-start.19 = (bf16[128,128]{1,0:T(8,128)(2,1)S(1)}, bf16[128,128]{1,0:T(8,128)(2,1)S(1)}, u32[]{:S(2)}, u32[]{:S(2)}) collective-permute-start(bf16[128,128]{1,0:T(8,128)(2,1)S(1)} %shard_map.180.refs_2_.refs_1_), channel_id=1, source_target_pairs={{0,2},{2,64},{64,66},{66,0},{1,3},{3,65},{65,67},{67,1},{4,6},{6,6... | collective-permute-start | bytes 98312 | tf_op jit(solution)/shard_map/ppermute | solution.py:554
  155.3 1.3 collective-permute-start.16
  156.7 2.5 %collective-permute-start.17 = (bf16[160,128]{1,0:T(8,128)(2,1)S(1)}, bf16[160,128]{1,0:T(8,128)(2,1)S(1)}, u32[]{:S(2)}, u32[]{:S(2)}) collective-permute-start(bf16[160,128]{1,0:T(8,128)(2,1)S(1)} %get-tuple-element.93), channel_id=1, source_target_pairs={{0,8},{4,12},{8,0},{12,4},{1,9},{5,13},{9,1},{13,5},{2,10},{6,14},... | collective-permute-start | bytes 122888 | tf_op jit(solution)/shard_map/ppermute | solution.py:554
  159.2 2.7 %collective-permute-start.18 = (bf16[160,128]{1,0:T(8,128)(2,1)S(1)}, bf16[160,128]{1,0:T(8,128)(2,1)S(1)}, u32[]{:S(2)}, u32[]{:S(2)}) collective-permute-start(bf16[160,128]{1,0:T(8,128)(2,1)S(1)} %get-tuple-element.94), channel_id=1, source_target_pairs={{0,12},{4,0},{8,4},{12,8},{1,13},{5,1},{9,5},{13,9},{2,14},{6,2},{... | collective-permute-start | bytes 122888 | tf_op jit(solution)/shard_map/ppermute | solution.py:554
  161.9 2.9 %collective-permute-start.23 = (bf16[128,128]{1,0:T(8,128)(2,1)S(1)}, bf16[128,128]{1,0:T(8,128)(2,1)S(1)}, u32[]{:S(2)}, u32[]{:S(2)}) collective-permute-start(bf16[128,128]{1,0:T(8,128)(2,1)S(1)} %shard_map.182.refs_4_.refs_1_), channel_id=1, source_target_pairs={{0,16},{16,32},{32,48},{48,0},{1,17},{17,33},{33,49},{49,1},{2,18}... | collective-permute-start | bytes 98312 | tf_op jit(solution)/shard_map/ppermute | solution.py:554
  164.8 2.6 %collective-permute-start.24 = (bf16[128,128]{1,0:T(8,128)(2,1)S(1)}, bf16[128,128]{1,0:T(8,128)(2,1)S(1)}, u32[]{:S(2)}, u32[]{:S(2)}) collective-permute-start(bf16[128,128]{1,0:T(8,128)(2,1)S(1)} %shard_map.182.refs_4_.refs_1_), channel_id=1, source_target_pairs={{0,32},{16,48},{32,0},{48,16},{1,33},{17,49},{33,1},{49,17},{2,34}... | collective-permute-start | bytes 98312 | tf_op jit(solution)/shard_map/ppermute | solution.py:554
  169.0 1.4 collective-permute-done.25.refs_4_
  170.5 2.5 %collective-permute-done.22.refs_1_ = bf16[160,128]{1,0:T(8,128)(2,1)S(1)} collective-permute-done((bf16[160,128]{1,0:T(8,128)(2,1)S(1)}, bf16[160,128]{1,0:T(8,128)(2,1)S(1)}, u32[]{:S(2)}, u32[]{:S(2)}) %collective-permute-start.22) | collective-permute-done | bytes 40992 | tf_op jit(solution)/shard_map/ppermute | solution.py:718
  173.1 2.2 %collective-permute-start.30 = (bf16[160,128]{1,0:T(8,128)(2,1)S(1)}, bf16[160,128]{1,0:T(8,128)(2,1)S(1)}, u32[]{:S(2)}, u32[]{:S(2)}) collective-permute-start(bf16[160,128]{1,0:T(8,128)(2,1)S(1)} %shard_map.185.refs_2_.refs_1_), channel_id=1, source_target_pairs={{0,8},{4,12},{8,0},{12,4},{1,9},{5,13},{9,1},{13,5},{2,10},{6,14},... | collective-permute-start | bytes 122888 | tf_op jit(solution)/shard_map/ppermute | solution.py:554
  179.0 1.2 shard_map.187.refs_5_
  180.3 3.6 %all-to-all-start.3 = ((bf16[8,640,128]{2,1,0:T(8,128)(2,1)}), bf16[8,640,128]{2,1,0:T(8,128)(2,1)S(1)}, u32[]{:S(2)}, u32[]{:S(2)}) async-start(bf16[8,640,128]{2,1,0:T(8,128)(2,1)} %shard_map.187.refs_5_), calls=%async_computation.3 | async-start | bytes 2621440 | tf_op jit(solution)/shard_map/all_to_all | solution.py:728
  185.0 2.5 %collective-permute-start.27 = (bf16[512,128]{1,0:T(8,128)(2,1)S(1)}, bf16[512,128]{1,0:T(8,128)(2,1)S(1)}, u32[]{:S(2)}, u32[]{:S(2)}) collective-permute-start(bf16[512,128]{1,0:T(8,128)(2,1)S(1)} %shard_map.184.refs_2_.refs_1_), channel_id=1, source_target_pairs={{0,8},{4,12},{8,0},{12,4},{1,9},{5,13},{9,1},{13,5},{2,10},{6,14},... | collective-permute-start | bytes 393224 | tf_op jit(solution)/shard_map/ppermute | solution.py:554
  187.5 1.4 collective-permute-done.26.refs_2_
  188.9 2.3 %collective-permute-done.27.refs_3_ = bf16[512,128]{1,0:T(8,128)(2,1)S(1)} collective-permute-done((bf16[512,128]{1,0:T(8,128)(2,1)S(1)}, bf16[512,128]{1,0:T(8,128)(2,1)S(1)}, u32[]{:S(2)}, u32[]{:S(2)}) %collective-permute-start.27) | collective-permute-done | bytes 131104 | tf_op jit(solution)/shard_map/ppermute | solution.py:554
  191.6 10.0 %all-to-all-done.3 = bf16[8,640,128]{2,1,0:T(8,128)(2,1)S(1)} async-done(((bf16[8,640,128]{2,1,0:T(8,128)(2,1)}), bf16[8,640,128]{2,1,0:T(8,128)(2,1)S(1)}, u32[]{:S(2)}, u32[]{:S(2)}) %all-to-all-start.3) | async-done | bytes 1310752 | tf_op jit(solution)/shard_map/all_to_all | solution.py:728
  201.8 1.8 collective-permute-start.33
  203.6 3.3 %collective-permute-done.32.refs_2_ = bf16[2048,128]{1,0:T(8,128)(2,1)S(1)} collective-permute-done((bf16[2048,128]{1,0:T(8,128)(2,1)S(1)}, bf16[2048,128]{1,0:T(8,128)(2,1)S(1)}, u32[]{:S(2)}, u32[]{:S(2)}) %collective-permute-start.32) | collective-permute-done | bytes 524320 | tf_op jit(solution)/shard_map/ppermute | solution.py:736
  207.0 1.6 shard_map.189
  208.5 3.0 %shard_map.191 = (f32[512,512]{1,0:T(8,128)}, f32[512,1536]{1,0:T(8,128)}, f32[512,512]{1,0:T(8,128)}) custom-call(s32[1]{0:T(128)} %bitcast.9.refs_0_, bf16[5120,128]{1,0:T(8,128)(2,1)S(1)} %shard_map.190.refs_1_, bf16[5120,128]{1,0:T(8,128)(2,1)S(1)} %collective-permute-done.33.refs_2_), custom_call_target="tpu_custom_call" | custom-call | flops 3000000000 | tf_op jit(solution)/shard_map/pallas_call | solution.py:120
  (136 shorter events, 29.1 us)
Async XLA Ops:
  3.6 25.7 %copy-start = (bf16[512,1536]{1,0:T(8,128)(2,1)S(1)}, bf16[512,1536]{1,0:T(8,128)(2,1)}, u32[]{:S(2)}) copy-start(bf16[512,1536]{1,0:T(8,128)(2,1)} %refs_7_.2) | copy-start | bytes 4718596
  3.6 25.7 %copy-start.2 = (bf16[512,512]{1,0:T(8,128)(2,1)S(1)}, bf16[512,512]{1,0:T(8,128)(2,1)}, u32[]{:S(2)}) copy-start(bf16[512,512]{1,0:T(8,128)(2,1)} %refs_10_.1) | copy-start | bytes 1572868
  3.6 25.7 %copy-start.3 = (bf16[512,512]{1,0:T(8,128)(2,1)S(1)}, bf16[512,512]{1,0:T(8,128)(2,1)}, u32[]{:S(2)}) copy-start(bf16[512,512]{1,0:T(8,128)(2,1)} %refs_6_.1) | copy-start | bytes 1572868
  3.6 25.7 %copy-start.4 = (bf16[256,1024]{1,0:T(8,128)(2,1)S(1)}, bf16[256,1024]{1,0:T(8,128)(2,1)}, u32[]{:S(2)}) copy-start(bf16[256,1024]{1,0:T(8,128)(2,1)} %refs_7_.3) | copy-start | bytes 1572868
  3.6 25.7 %copy-start.14 = (bf16[8,16,512]{2,1,0:T(8,128)(2,1)S(1)}, bf16[8,16,512]{2,1,0:T(8,128)(2,1)}, u32[]{:S(2)}) copy-start(bf16[8,16,512]{2,1,0:T(8,128)(2,1)} %param.11) | copy-start | bytes 393220
  4.5 31.4 %copy-start.22 = (s32[256,1]{1,0:T(8,128)}, s32[256,1]{1,0:T(8,128)S(1)}, u32[]{:S(2)}) copy-start(s32[256,1]{1,0:T(8,128)S(1)} %get-tuple-element.77.refs_0_) | copy-start | bytes 3076
  37.8 10.6 %copy-start.30 = (bf16[128,512]{1,0:T(8,128)(2,1)}, bf16[128,512]{1,0:T(8,128)(2,1)S(1)}, u32[]{:S(2)}) copy-start(bf16[128,512]{1,0:T(8,128)(2,1)S(1)} %get-tuple-element.59.refs_9_.refs_8_) | copy-start | bytes 393220
  37.8 10.6 %copy-start.39 = (bf16[128,512]{1,0:T(8,128)(2,1)}, bf16[128,512]{1,0:T(8,128)(2,1)S(1)}, u32[]{:S(2)}) copy-start(bf16[128,512]{1,0:T(8,128)(2,1)S(1)} %get-tuple-element.61.refs_1_) | copy-start | bytes 393220
  37.8 10.6 %copy-start.41 = (bf16[128,512]{1,0:T(8,128)(2,1)}, bf16[128,512]{1,0:T(8,128)(2,1)S(1)}, u32[]{:S(2)}) copy-start(bf16[128,512]{1,0:T(8,128)(2,1)S(1)} %get-tuple-element.55.refs_1_) | copy-start | bytes 393220
  37.9 5.4 %collective-permute-start = (bf16[96,1024]{1,0:T(8,128)(2,1)S(1)}, bf16[96,1024]{1,0:T(8,128)(2,1)S(1)}, u32[]{:S(2)}, u32[]{:S(2)}) collective-permute-start(bf16[96,1024]{1,0:T(8,128)(2,1)S(1)} %get-tuple-element.101), channel_id=1, source_target_pairs={{0,16},{16,32},{32,48},{48,64},{64,80},{80,96},{96,112},{1,17},{17... | collective-permute-start | bytes 589832 | tf_op jit(solution)/shard_map/ppermute | solution.py:613
  39.3 22.5 %copy-start.1 = (bf16[512,512]{1,0:T(8,128)(2,1)S(1)}, bf16[512,512]{1,0:T(8,128)(2,1)}, u32[]{:S(2)}) copy-start(bf16[512,512]{1,0:T(8,128)(2,1)} %refs_8_.1) | copy-start | bytes 1572868
  39.3 22.5 %copy-start.13 = (bf16[8,16,512]{2,1,0:T(8,128)(2,1)S(1)}, bf16[8,16,512]{2,1,0:T(8,128)(2,1)}, u32[]{:S(2)}) copy-start(bf16[8,16,512]{2,1,0:T(8,128)(2,1)} %param.21) | copy-start | bytes 393220
  39.3 7.9 %collective-permute-start.1 = (bf16[96,1024]{1,0:T(8,128)(2,1)S(1)}, bf16[96,1024]{1,0:T(8,128)(2,1)S(1)}, u32[]{:S(2)}, u32[]{:S(2)}) collective-permute-start(bf16[96,1024]{1,0:T(8,128)(2,1)S(1)} %get-tuple-element.100), channel_id=1, source_target_pairs={{16,0},{32,16},{48,32},{64,48},{80,64},{96,80},{112,96},{17,1},{33... | collective-permute-start | bytes 589832 | tf_op jit(solution)/shard_map/ppermute | solution.py:614
  48.4 6.5 %collective-permute-start.2 = (bf16[128,1024]{1,0:T(8,128)(2,1)}, bf16[128,1024]{1,0:T(8,128)(2,1)}, u32[]{:S(2)}, u32[]{:S(2)}) collective-permute-start(bf16[128,1024]{1,0:T(8,128)(2,1)} %get-tuple-element.57), channel_id=1, source_target_pairs={{0,1},{1,2},{2,3},{3,4},{4,5},{5,6},{6,7},{7,8},{8,9},{9,10},{10,1... | collective-permute-start | bytes 786440 | tf_op jit(solution)/shard_map/ppermute | solution.py:620
  51.3 10.4 %collective-permute-start.3 = (bf16[128,1024]{1,0:T(8,128)(2,1)}, bf16[128,1024]{1,0:T(8,128)(2,1)}, u32[]{:S(2)}, u32[]{:S(2)}) collective-permute-start(bf16[128,1024]{1,0:T(8,128)(2,1)} %get-tuple-element.58), channel_id=1, source_target_pairs={{1,0},{2,1},{3,2},{4,3},{5,4},{6,5},{7,6},{8,7},{9,8},{10,9},{11,1... | collective-permute-start | bytes 786440 | tf_op jit(solution)/shard_map/ppermute | solution.py:621
  75.5 6.1 %collective-permute-start.4 = (bf16[128,1024]{1,0:T(8,128)(2,1)S(1)}, bf16[128,1024]{1,0:T(8,128)(2,1)S(1)}, u32[]{:S(2)}, u32[]{:S(2)}) collective-permute-start(bf16[128,1024]{1,0:T(8,128)(2,1)S(1)} %get-tuple-element.66), channel_id=1, source_target_pairs={{0,1},{1,2},{2,3},{3,4},{4,5},{5,6},{6,7},{7,8},{8,9},{9,10},{10,1... | collective-permute-start | bytes 786440 | tf_op jit(solution)/shard_map/ppermute | solution.py:642
  75.5 9.5 %collective-permute-start.5 = (bf16[128,1024]{1,0:T(8,128)(2,1)S(1)}, bf16[128,1024]{1,0:T(8,128)(2,1)S(1)}, u32[]{:S(2)}, u32[]{:S(2)}) collective-permute-start(bf16[128,1024]{1,0:T(8,128)(2,1)S(1)} %get-tuple-element.67), channel_id=1, source_target_pairs={{1,0},{2,1},{3,2},{4,3},{5,4},{6,5},{7,6},{8,7},{9,8},{10,9},{11,1... | collective-permute-start | bytes 786440 | tf_op jit(solution)/shard_map/ppermute | solution.py:641
  86.9 6.5 %collective-permute-start.6 = (bf16[96,1024]{1,0:T(8,128)(2,1)}, bf16[96,1024]{1,0:T(8,128)(2,1)S(1)}, u32[]{:S(2)}, u32[]{:S(2)}) collective-permute-start(bf16[96,1024]{1,0:T(8,128)(2,1)} %get-tuple-element.69), channel_id=1, source_target_pairs={{0,16},{16,32},{32,48},{48,64},{64,80},{80,96},{96,112},{1,17},{17... | collective-permute-start | bytes 589832 | tf_op jit(solution)/shard_map/ppermute | solution.py:650
  90.0 7.2 %collective-permute-start.7 = (bf16[96,1024]{1,0:T(8,128)(2,1)S(1)}, bf16[96,1024]{1,0:T(8,128)(2,1)S(1)}, u32[]{:S(2)}, u32[]{:S(2)}) collective-permute-start(bf16[96,1024]{1,0:T(8,128)(2,1)S(1)} %get-tuple-element.70), channel_id=1, source_target_pairs={{16,0},{32,16},{48,32},{64,48},{80,64},{96,80},{112,96},{17,1},{33... | collective-permute-start | bytes 589832 | tf_op jit(solution)/shard_map/ppermute | solution.py:649
  106.8 11.8 %collective-permute-start.8 = (bf16[5120,128]{1,0:T(8,128)(2,1)S(1)}, bf16[5120,128]{1,0:T(8,128)(2,1)S(1)}, u32[]{:S(2)}, u32[]{:S(2)}) collective-permute-start(bf16[5120,128]{1,0:T(8,128)(2,1)S(1)} %get-tuple-element.80), channel_id=1, source_target_pairs={{0,1},{1,0},{2,3},{3,2},{4,5},{5,4},{6,7},{7,6},{8,9},{9,8},{10,11... | collective-permute-start | bytes 3932168 | tf_op jit(solution)/shard_map/ppermute | solution.py:664
  119.9 26.3 %all-to-all-start.2 = ((bf16[8,640,128]{2,1,0:T(8,128)(2,1)}), bf16[8,640,128]{2,1,0:T(8,128)(2,1)S(1)}, u32[]{:S(2)}, u32[]{:S(2)}) async-start(bf16[8,640,128]{2,1,0:T(8,128)(2,1)} %bitcast.14), calls=%async_computation.2 | async-start | bytes 2621440 | tf_op jit(solution)/shard_map/all_to_all | solution.py:572
  127.5 2.3 %collective-permute-start.9 = (bf16[2048,128]{1,0:T(8,128)(2,1)S(1)}, bf16[2048,128]{1,0:T(8,128)(2,1)S(1)}, u32[]{:S(2)}, u32[]{:S(2)}) collective-permute-start(bf16[2048,128]{1,0:T(8,128)(2,1)S(1)} %get-tuple-element.82), channel_id=1, source_target_pairs={{0,1},{1,0},{2,3},{3,2},{4,5},{5,4},{6,7},{7,6},{8,9},{9,8},{10,11... | collective-permute-start | bytes 1572872 | tf_op jit(solution)/shard_map/ppermute | solution.py:696
  129.9 9.1 %collective-permute-start.10 = (bf16[512,128]{1,0:T(8,128)(2,1)S(1)}, bf16[512,128]{1,0:T(8,128)(2,1)S(1)}, u32[]{:S(2)}, u32[]{:S(2)}) collective-permute-start(bf16[512,128]{1,0:T(8,128)(2,1)S(1)} %get-tuple-element.84), channel_id=1, source_target_pairs={{0,4},{4,8},{8,12},{12,0},{1,5},{5,9},{9,13},{13,1},{2,6},{6,10},{... | collective-permute-start | bytes 393224 | tf_op jit(solution)/shard_map/ppermute | solution.py:554
  130.0 9.1 %collective-permute-start.11 = (bf16[512,128]{1,0:T(8,128)(2,1)S(1)}, bf16[512,128]{1,0:T(8,128)(2,1)S(1)}, u32[]{:S(2)}, u32[]{:S(2)}) collective-permute-start(bf16[512,128]{1,0:T(8,128)(2,1)S(1)} %get-tuple-element.85), channel_id=1, source_target_pairs={{0,8},{4,12},{8,0},{12,4},{1,9},{5,13},{9,1},{13,5},{2,10},{6,14},... | collective-permute-start | bytes 393224 | tf_op jit(solution)/shard_map/ppermute | solution.py:554
  130.1 9.0 %collective-permute-start.12 = (bf16[512,128]{1,0:T(8,128)(2,1)S(1)}, bf16[512,128]{1,0:T(8,128)(2,1)S(1)}, u32[]{:S(2)}, u32[]{:S(2)}) collective-permute-start(bf16[512,128]{1,0:T(8,128)(2,1)S(1)} %get-tuple-element.86), channel_id=1, source_target_pairs={{0,12},{4,0},{8,4},{12,8},{1,13},{5,1},{9,5},{13,9},{2,14},{6,2},{... | collective-permute-start | bytes 393224 | tf_op jit(solution)/shard_map/ppermute | solution.py:554
  139.2 11.8 %collective-permute-start.13 = (bf16[128,128]{1,0:T(8,128)(2,1)S(1)}, bf16[128,128]{1,0:T(8,128)(2,1)S(1)}, u32[]{:S(2)}, u32[]{:S(2)}) collective-permute-start(bf16[128,128]{1,0:T(8,128)(2,1)S(1)} %get-tuple-element.88), channel_id=1, source_target_pairs={{0,16},{16,32},{32,48},{48,0},{1,17},{17,33},{33,49},{49,1},{2,18}... | collective-permute-start | bytes 98312 | tf_op jit(solution)/shard_map/ppermute | solution.py:554
  141.0 10.0 %collective-permute-start.14 = (bf16[128,128]{1,0:T(8,128)(2,1)S(1)}, bf16[128,128]{1,0:T(8,128)(2,1)S(1)}, u32[]{:S(2)}, u32[]{:S(2)}) collective-permute-start(bf16[128,128]{1,0:T(8,128)(2,1)S(1)} %get-tuple-element.89), channel_id=1, source_target_pairs={{0,32},{16,48},{32,0},{48,16},{1,33},{17,49},{33,1},{49,17},{2,34}... | collective-permute-start | bytes 98312 | tf_op jit(solution)/shard_map/ppermute | solution.py:554
  143.4 7.6 %collective-permute-start.15 = (bf16[128,128]{1,0:T(8,128)(2,1)S(1)}, bf16[128,128]{1,0:T(8,128)(2,1)S(1)}, u32[]{:S(2)}, u32[]{:S(2)}) collective-permute-start(bf16[128,128]{1,0:T(8,128)(2,1)S(1)} %get-tuple-element.90), channel_id=1, source_target_pairs={{0,48},{16,0},{32,16},{48,32},{1,49},{17,1},{33,17},{49,33},{2,50}... | collective-permute-start | bytes 98312 | tf_op jit(solution)/shard_map/ppermute | solution.py:554
  146.1 30.2 %all-to-all-start.1 = ((bf16[128,8,256]{2,1,0:T(8,128)(2,1)}), bf16[128,8,256]{2,1,0:T(8,128)(2,1)S(1)}, u32[]{:S(2)}, u32[]{:S(2)}) async-start(bf16[128,8,256]{2,1,0:T(8,128)(2,1)} %bitcast.11), calls=%async_computation.1 | async-start | bytes 1048576 | tf_op jit(solution)/shard_map/all_to_all | solution.py:688
  151.0 8.2 %collective-permute-start.19 = (bf16[128,128]{1,0:T(8,128)(2,1)S(1)}, bf16[128,128]{1,0:T(8,128)(2,1)S(1)}, u32[]{:S(2)}, u32[]{:S(2)}) collective-permute-start(bf16[128,128]{1,0:T(8,128)(2,1)S(1)} %shard_map.180.refs_2_.refs_1_), channel_id=1, source_target_pairs={{0,2},{2,64},{64,66},{66,0},{1,3},{3,65},{65,67},{67,1},{4,6},{6,6... | collective-permute-start | bytes 98312 | tf_op jit(solution)/shard_map/ppermute | solution.py:554
  154.5 7.3 %collective-permute-start.20 = (bf16[128,128]{1,0:T(8,128)(2,1)S(1)}, bf16[128,128]{1,0:T(8,128)(2,1)S(1)}, u32[]{:S(2)}, u32[]{:S(2)}) collective-permute-start(bf16[128,128]{1,0:T(8,128)(2,1)S(1)} %shard_map.180.refs_2_.refs_1_), channel_id=1, source_target_pairs={{0,64},{2,66},{64,0},{66,2},{1,65},{3,67},{65,1},{67,3},{4,68},{6,... | collective-permute-start | bytes 98312 | tf_op jit(solution)/shard_map/ppermute | solution.py:554
  155.1 6.8 %collective-permute-start.21 = (bf16[128,128]{1,0:T(8,128)(2,1)S(1)}, bf16[128,128]{1,0:T(8,128)(2,1)S(1)}, u32[]{:S(2)}, u32[]{:S(2)}) collective-permute-start(bf16[128,128]{1,0:T(8,128)(2,1)S(1)} %shard_map.180.refs_2_.refs_1_), channel_id=1, source_target_pairs={{0,66},{2,0},{64,2},{66,64},{1,67},{3,1},{65,3},{67,65},{4,70},{6,... | collective-permute-start | bytes 98312 | tf_op jit(solution)/shard_map/ppermute | solution.py:554
  155.3 12.1 %collective-permute-start.16 = (bf16[160,128]{1,0:T(8,128)(2,1)S(1)}, bf16[160,128]{1,0:T(8,128)(2,1)S(1)}, u32[]{:S(2)}, u32[]{:S(2)}) collective-permute-start(bf16[160,128]{1,0:T(8,128)(2,1)S(1)} %get-tuple-element.92), channel_id=1, source_target_pairs={{0,4},{4,8},{8,12},{12,0},{1,5},{5,9},{9,13},{13,1},{2,6},{6,10},{... | collective-permute-start | bytes 122888 | tf_op jit(solution)/shard_map/ppermute | solution.py:554
  156.7 11.8 %collective-permute-start.17 = (bf16[160,128]{1,0:T(8,128)(2,1)S(1)}, bf16[160,128]{1,0:T(8,128)(2,1)S(1)}, u32[]{:S(2)}, u32[]{:S(2)}) collective-permute-start(bf16[160,128]{1,0:T(8,128)(2,1)S(1)} %get-tuple-element.93), channel_id=1, source_target_pairs={{0,8},{4,12},{8,0},{12,4},{1,9},{5,13},{9,1},{13,5},{2,10},{6,14},... | collective-permute-start | bytes 122888 | tf_op jit(solution)/shard_map/ppermute | solution.py:554
  159.2 9.3 %collective-permute-start.18 = (bf16[160,128]{1,0:T(8,128)(2,1)S(1)}, bf16[160,128]{1,0:T(8,128)(2,1)S(1)}, u32[]{:S(2)}, u32[]{:S(2)}) collective-permute-start(bf16[160,128]{1,0:T(8,128)(2,1)S(1)} %get-tuple-element.94), channel_id=1, source_target_pairs={{0,12},{4,0},{8,4},{12,8},{1,13},{5,1},{9,5},{13,9},{2,14},{6,2},{... | collective-permute-start | bytes 122888 | tf_op jit(solution)/shard_map/ppermute | solution.py:554
  161.9 6.8 %collective-permute-start.23 = (bf16[128,128]{1,0:T(8,128)(2,1)S(1)}, bf16[128,128]{1,0:T(8,128)(2,1)S(1)}, u32[]{:S(2)}, u32[]{:S(2)}) collective-permute-start(bf16[128,128]{1,0:T(8,128)(2,1)S(1)} %shard_map.182.refs_4_.refs_1_), channel_id=1, source_target_pairs={{0,16},{16,32},{32,48},{48,0},{1,17},{17,33},{33,49},{49,1},{2,18}... | collective-permute-start | bytes 98312 | tf_op jit(solution)/shard_map/ppermute | solution.py:554
  164.8 4.3 %collective-permute-start.24 = (bf16[128,128]{1,0:T(8,128)(2,1)S(1)}, bf16[128,128]{1,0:T(8,128)(2,1)S(1)}, u32[]{:S(2)}, u32[]{:S(2)}) collective-permute-start(bf16[128,128]{1,0:T(8,128)(2,1)S(1)} %shard_map.182.refs_4_.refs_1_), channel_id=1, source_target_pairs={{0,32},{16,48},{32,0},{48,16},{1,33},{17,49},{33,1},{49,17},{2,34}... | collective-permute-start | bytes 98312 | tf_op jit(solution)/shard_map/ppermute | solution.py:554
  167.4 3.1 %collective-permute-start.25 = (bf16[128,128]{1,0:T(8,128)(2,1)S(1)}, bf16[128,128]{1,0:T(8,128)(2,1)S(1)}, u32[]{:S(2)}, u32[]{:S(2)}) collective-permute-start(bf16[128,128]{1,0:T(8,128)(2,1)S(1)} %shard_map.182.refs_4_.refs_1_), channel_id=1, source_target_pairs={{0,48},{16,0},{32,16},{48,32},{1,49},{17,1},{33,17},{49,33},{2,50}... | collective-permute-start | bytes 98312 | tf_op jit(solution)/shard_map/ppermute | solution.py:554
  168.5 4.4 %collective-permute-start.22 = (bf16[160,128]{1,0:T(8,128)(2,1)S(1)}, bf16[160,128]{1,0:T(8,128)(2,1)S(1)}, u32[]{:S(2)}, u32[]{:S(2)}) collective-permute-start(bf16[160,128]{1,0:T(8,128)(2,1)S(1)} %shard_map.183.refs_0_), channel_id=1, source_target_pairs={{0,2},{2,0},{1,3},{3,1},{4,6},{6,4},{5,7},{7,5},{8,10},{10,8},{9,1... | collective-permute-start | bytes 122888 | tf_op jit(solution)/shard_map/ppermute | solution.py:718
  173.0 4.4 %collective-permute-start.29 = (bf16[160,128]{1,0:T(8,128)(2,1)S(1)}, bf16[160,128]{1,0:T(8,128)(2,1)S(1)}, u32[]{:S(2)}, u32[]{:S(2)}) collective-permute-start(bf16[160,128]{1,0:T(8,128)(2,1)S(1)} %shard_map.185.refs_2_.refs_1_), channel_id=1, source_target_pairs={{0,4},{4,8},{8,12},{12,0},{1,5},{5,9},{9,13},{13,1},{2,6},{6,10},{... | collective-permute-start | bytes 122888 | tf_op jit(solution)/shard_map/ppermute | solution.py:554
  173.1 4.5 %collective-permute-start.30 = (bf16[160,128]{1,0:T(8,128)(2,1)S(1)}, bf16[160,128]{1,0:T(8,128)(2,1)S(1)}, u32[]{:S(2)}, u32[]{:S(2)}) collective-permute-start(bf16[160,128]{1,0:T(8,128)(2,1)S(1)} %shard_map.185.refs_2_.refs_1_), channel_id=1, source_target_pairs={{0,8},{4,12},{8,0},{12,4},{1,9},{5,13},{9,1},{13,5},{2,10},{6,14},... | collective-permute-start | bytes 122888 | tf_op jit(solution)/shard_map/ppermute | solution.py:554
  175.2 2.9 %collective-permute-start.31 = (bf16[160,128]{1,0:T(8,128)(2,1)S(1)}, bf16[160,128]{1,0:T(8,128)(2,1)S(1)}, u32[]{:S(2)}, u32[]{:S(2)}) collective-permute-start(bf16[160,128]{1,0:T(8,128)(2,1)S(1)} %shard_map.185.refs_2_.refs_1_), channel_id=1, source_target_pairs={{0,12},{4,0},{8,4},{12,8},{1,13},{5,1},{9,5},{13,9},{2,14},{6,2},{... | collective-permute-start | bytes 122888 | tf_op jit(solution)/shard_map/ppermute | solution.py:554
  180.3 21.4 %all-to-all-start.3 = ((bf16[8,640,128]{2,1,0:T(8,128)(2,1)}), bf16[8,640,128]{2,1,0:T(8,128)(2,1)S(1)}, u32[]{:S(2)}, u32[]{:S(2)}) async-start(bf16[8,640,128]{2,1,0:T(8,128)(2,1)} %shard_map.187.refs_5_), calls=%async_computation.3 | async-start | bytes 2621440 | tf_op jit(solution)/shard_map/all_to_all | solution.py:728
  183.8 5.1 %collective-permute-start.26 = (bf16[512,128]{1,0:T(8,128)(2,1)S(1)}, bf16[512,128]{1,0:T(8,128)(2,1)S(1)}, u32[]{:S(2)}, u32[]{:S(2)}) collective-permute-start(bf16[512,128]{1,0:T(8,128)(2,1)S(1)} %shard_map.184.refs_2_.refs_1_), channel_id=1, source_target_pairs={{0,4},{4,8},{8,12},{12,0},{1,5},{5,9},{9,13},{13,1},{2,6},{6,10},{... | collective-permute-start | bytes 393224 | tf_op jit(solution)/shard_map/ppermute | solution.py:554
  185.0 6.3 %collective-permute-start.27 = (bf16[512,128]{1,0:T(8,128)(2,1)S(1)}, bf16[512,128]{1,0:T(8,128)(2,1)S(1)}, u32[]{:S(2)}, u32[]{:S(2)}) collective-permute-start(bf16[512,128]{1,0:T(8,128)(2,1)S(1)} %shard_map.184.refs_2_.refs_1_), channel_id=1, source_target_pairs={{0,8},{4,12},{8,0},{12,4},{1,9},{5,13},{9,1},{13,5},{2,10},{6,14},... | collective-permute-start | bytes 393224 | tf_op jit(solution)/shard_map/ppermute | solution.py:554
  187.5 4.1 %collective-permute-start.28 = (bf16[512,128]{1,0:T(8,128)(2,1)S(1)}, bf16[512,128]{1,0:T(8,128)(2,1)S(1)}, u32[]{:S(2)}, u32[]{:S(2)}) collective-permute-start(bf16[512,128]{1,0:T(8,128)(2,1)S(1)} %shard_map.184.refs_2_.refs_1_), channel_id=1, source_target_pairs={{0,12},{4,0},{8,4},{12,8},{1,13},{5,1},{9,5},{13,9},{2,14},{6,2},{... | collective-permute-start | bytes 393224 | tf_op jit(solution)/shard_map/ppermute | solution.py:554
  201.8 6.8 %collective-permute-start.33 = (bf16[5120,128]{1,0:T(8,128)(2,1)S(1)}, bf16[5120,128]{1,0:T(8,128)(2,1)S(1)}, u32[]{:S(2)}, u32[]{:S(2)}) collective-permute-start(bf16[5120,128]{1,0:T(8,128)(2,1)S(1)} %shard_map.190.refs_1_), channel_id=1, source_target_pairs={{0,1},{1,0},{2,3},{3,2},{4,5},{5,4},{6,7},{7,6},{8,9},{9,8},{10,11... | collective-permute-start | bytes 3932168 | tf_op jit(solution)/shard_map/ppermute | solution.py:740
  203.6 3.4 %collective-permute-start.32 = (bf16[2048,128]{1,0:T(8,128)(2,1)S(1)}, bf16[2048,128]{1,0:T(8,128)(2,1)S(1)}, u32[]{:S(2)}, u32[]{:S(2)}) collective-permute-start(bf16[2048,128]{1,0:T(8,128)(2,1)S(1)} %shard_map.188.refs_1_), channel_id=1, source_target_pairs={{0,1},{1,0},{2,3},{3,2},{4,5},{5,4},{6,7},{7,6},{8,9},{9,8},{10,11... | collective-permute-start | bytes 1572872 | tf_op jit(solution)/shard_map/ppermute | solution.py:736
  (32 other events, 72.3 us)

commit v3 on v2

--- a/solution.py
+++ b/solution.py
@@ -181,7 +181,7 @@
 
 def cross_kernel(
     arrived, grid, query_w, sensor_w, cross_w, local_w,
-    slots_out, keyval, query, prob, att, after, local_q, local_kv,
+    keyval, query, prob, cells, local_kv,
     gap, scores,
 ):
     slot = iota((SLOTS, WIRE), 0)
@@ -190,8 +190,8 @@
     rows = arrived[...]
     picked = dot(one_hot(wire == slot + 2 * source), rows).astype(B16)
     codes = dot(one_hot(wire == source * PITCH + CAP), rows[:, :128])
-    slots_out[...] = picked
-    keyval[...] = dot(picked, sensor_w[...]).astype(B16)
+    keyval[:, 2 * C :] = picked
+    keyval[:, : 2 * C] = dot(picked, sensor_w[...]).astype(B16)
     query[...] = dot(grid[...], query_w[...]).astype(B16)
 
     index = iota((SLOTS, 128), 0)
@@ -229,14 +229,15 @@
             inverse = 1.0 / total
             for r in range(0, SLOTS, step):
                 prob[g, r : r + step, cols] = (scores[r : r + step, cols] * inverse).astype(B16)
-        att[:, lanes] = head_blocks(dot(values.T, prob[g])).astype(B16)
+        out_lanes = pl.ds(pl.multiple_of(2 * C + g * 128, 128), 128)
+        cells[:, out_lanes] = head_blocks(dot(values.T, prob[g])).astype(B16)
         return carry
 
     lax.fori_loop(0, GROUPS, one_group, 0)
-    mixed = (grid[...].astype(F32) + dot(att[...], cross_w[...])).astype(B16)
-    after[...] = mixed
+    mixed = (grid[...].astype(F32) + dot(cells[:, 2 * C :], cross_w[...])).astype(B16)
+    cells[:, :C] = mixed
     qkv = dot(mixed, local_w[...]).astype(B16)
-    local_q[...] = qkv[:, :C]
+    cells[:, C : 2 * C] = qkv[:, :C]
     local_kv[...] = qkv[:, C:]
 
 
@@ -247,8 +248,9 @@
     return (iota(shape, 1 - key_dim) == wanted) & (key < (TH + 2 * RADIUS) * RADIUS)
 
 
-def edges_kernel(top, own, bottom, left, right):
+def edges_kernel(top, own, bottom, left, right, kept):
     region = jnp.concatenate([top[...], own[...], bottom[...]], axis=0)
+    kept[...] = region
     shape = (SIDE, REGION)
     left[...] = dot(one_hot(side_rows(shape, 0, 0)), region).astype(B16)
     right[...] = dot(one_hot(side_rows(shape, 0, TW - RADIUS)), region).astype(B16)
@@ -265,14 +267,12 @@
 
 
 def local_kernel(
-    lat_index, query, top, own, bottom, left, right, cotangent, merge_w, after,
-    updated, att, grad_query, grad_region, grad_left, grad_right,
+    lat_index, cells, region, left, right, cotangent, merge_w,
+    updated, results, grad_region, grad_left, grad_right,
     keyval, bias, scores, grad_prob, prob, grad_score, grad_att,
 ):
     lat = lat_index[0]
-    keyval[0:EDGE] = top[...]
-    keyval[EDGE : EDGE + CELLS] = own[...]
-    keyval[EDGE + CELLS : REGION] = bottom[...]
+    keyval[0:REGION] = region[...]
     keyval[REGION : REGION + SIDE] = left[...]
     keyval[REGION + SIDE : KEYS] = right[...]
     grad_att[...] = dot_nt(cotangent[...], merge_w[...]).astype(B16)
@@ -295,7 +295,7 @@
         lanes = pl.ds(pl.multiple_of(g * 128, 128), 128)
         upper = pl.ds(pl.multiple_of(C + g * 128, 128), 128)
         keys, values = keyval[:, lanes], keyval[:, upper]
-        heads_query = masked_heads(query[:, lanes])
+        heads_query = masked_heads(cells[:, upper])
         heads_grad = masked_heads(grad_att[:, lanes])
         scores[...] = dot_nt(keys, heads_query)
         grad_prob[...] = dot_nt(values, heads_grad)
@@ -322,8 +322,8 @@
                 grad_score[r : r + step, cols] = (
                     p * (grad_prob[r : r + step, cols] - delta)
                 ).astype(B16)
-        att[:, lanes] = head_blocks(dot(values.T, prob[...])).astype(B16)
-        grad_query[:, lanes] = (head_blocks(dot(keys.T, grad_score[...])) * SCALE).astype(B16)
+        results[:, lanes] = head_blocks(dot(values.T, prob[...])).astype(B16)
+        results[:, upper] = (head_blocks(dot(keys.T, grad_score[...])) * SCALE).astype(B16)
         grad_key = dot(grad_score[...], heads_query) * SCALE
         grad_value = dot(prob[...], heads_grad)
         for part, where_to in ((grad_key, lanes), (grad_value, upper)):
@@ -333,7 +333,11 @@
         return carry
 
     lax.fori_loop(0, GROUPS, one_group, 0)
-    updated[...] = (after[...].astype(F32) + dot(att[...], merge_w[...])).astype(B16)
+    updated[...] = (
+        cells[:, :C].astype(F32) + dot(results[:, :C], merge_w[...])
+    ).astype(B16)
+    results[:, 2 * C : 3 * C] = cells[:, :C]
+    results[:, 3 * C :] = cells[:, 2 * C :]
 
 
 def gather_kernel(grad_region, from_left, from_right, top, own, bottom):
@@ -369,28 +373,27 @@
 
 
 def mixed_kernel(
-    core_index, grad_query, grad_kv, from_above, from_below, local_att, cotangent_in, local_in,
-    after_in, cross_att_in, cross_in,
+    core_index, results, grad_kv, from_above, from_below, cotangent_in, local_in, cross_in,
     mine, send, grad_mixed, grad_cross_att,
     staged, keyval,
 ):
     keyval[...] = grad_kv[...]
     keyval[0:EDGE] = keyval[0:EDGE] + from_above[...].astype(F32)
     keyval[CELLS - EDGE :] = keyval[CELLS - EDGE :] + from_below[...].astype(F32)
-    grad_qkv = jnp.concatenate([grad_query[...], keyval[...].astype(B16)], axis=1)
+    grad_qkv = jnp.concatenate([results[:, C : 2 * C], keyval[...].astype(B16)], axis=1)
     cotangent = cotangent_in()
-    put_blocks(staged, 0, dot(local_att[...].T, cotangent[...]))
-    put_blocks(staged, 4 * C, dot(after_in()[...].T, grad_qkv))
+    put_blocks(staged, 0, dot(results[:, :C].T, cotangent[...]))
+    put_blocks(staged, 4 * C, dot(results[:, 2 * C : 3 * C].T, grad_qkv))
     mixed = cotangent[...].astype(F32) + dot_nt(grad_qkv, local_in()[...])
     grad_mixed[...] = mixed
     rounded = mixed.astype(B16)
-    put_blocks(staged, 16 * C, dot(cross_att_in()[...].T, rounded))
+    put_blocks(staged, 16 * C, dot(results[:, 3 * C :].T, rounded))
     grad_cross_att[...] = dot_nt(rounded, cross_in()[...]).astype(B16)
     split_halves(core_index[0], staged, mine, send)
 
 
 def cross_back_kernel(
-    core_index, query_in, keyval_in, prob_in, grad_att, grid, query_w, sensor_w, slots, grad_mixed,
+    core_index, query_in, keyval_in, prob_in, grad_att, grid, query_w, sensor_w, grad_mixed,
     mine, send, grad_grid, grad_wire,
     staged, grad_prob, grad_score, grad_query, grad_keyval, prob, prob_came,
 ):
@@ -430,7 +433,7 @@
     source = sixth(slot)
     grad_wire[...] = dot(one_hot(wire == slot + 2 * source), grad_slots).astype(B16)
     put_blocks(staged, 0, dot(grid()[...].T, grad_query[...]))
-    put_blocks(staged, ROWS_LATE, dot(slots()[...].T, grad_keyval[...]))
+    put_blocks(staged, ROWS_LATE, dot(keyval[:, 2 * C :].T, grad_keyval[...]))
     grad_grid[...] = grad_mixed()[...] + dot_nt(grad_query[...], query_w()[...])
     split_halves(core_index[0], staged, mine, send)
 
@@ -598,12 +601,11 @@
         outgoing.reshape(TILES, PITCH, F), ALL, split_axis=0, concat_axis=0, tiled=True
     ).reshape(WIRE, F)
 
-    slots, keyval, query, prob, cross_att, after, local_q, local_kv = call(
+    keyval, query, prob, cells, local_kv = call(
         cross_kernel,
         [
-            ((SLOTS, F), B16), ((SLOTS, 2 * C), B16), ((CELLS, C), B16),
-            ((GROUPS, SLOTS, LANES), B16), ((CELLS, C), B16), ((CELLS, C), B16),
-            ((CELLS, C), B16), ((CELLS, 2 * C), B16),
+            ((SLOTS, 2 * C + F), B16), ((CELLS, C), B16),
+            ((GROUPS, SLOTS, LANES), B16), ((CELLS, 3 * C), B16), ((CELLS, 2 * C), B16),
         ],
         (arrived, grid, query_weight, sensor_weight, cross_weight, local_weight),
         scratch=[pltpu.VMEM((SLOTS, CELLS), F32), pltpu.VMEM((SLOTS, LANES), F32)],
@@ -612,22 +614,22 @@
 
     top = lax.ppermute(local_kv[CELLS - EDGE :], LAT, down)
     bottom = lax.ppermute(local_kv[:EDGE], LAT, up)
-    send_left, send_right = call(
+    send_left, send_right, region = call(
         edges_kernel,
-        [((SIDE, 2 * C), B16), ((SIDE, 2 * C), B16)],
+        [((SIDE, 2 * C), B16), ((SIDE, 2 * C), B16), ((REGION, 2 * C), B16)],
         (top, local_kv, bottom),
     )
     left = lax.ppermute(send_right, LON, east)
     right = lax.ppermute(send_left, LON, west)
 
-    updated, local_att, grad_query, grad_region, grad_left, grad_right = call(
+    updated, results, grad_region, grad_left, grad_right = call(
         local_kernel,
         [
-            ((CELLS, C), B16), ((CELLS, C), B16), ((CELLS, C), B16),
+            ((CELLS, C), B16), ((CELLS, 4 * C), B16),
             ((REGION, 2 * C), F32), ((SIDE, 2 * C), B16), ((SIDE, 2 * C), B16),
         ],
         (
-            lat, local_q, top, local_kv, bottom, left, right, grad_rows, merge_weight, after,
+            lat, cells, region, left, right, grad_rows, merge_weight,
         ),
         scratch=[
             pltpu.VMEM((KEYS, 2 * C), B16), pltpu.VMEM((KEYS, CELLS), F32),
@@ -653,20 +655,20 @@
         mixed_kernel,
         half(ROWS_CELLS) + [((CELLS, C), F32), ((CELLS, C), B16)],
         (
-            core, grad_query, grad_own, from_above, from_below, local_att, grad_rows,
-            local_weight, after, cross_att, cross_weight,
+            core, results, grad_own, from_above, from_below, grad_rows, local_weight,
+            cross_weight,
         ),
         scratch=[pltpu.VMEM((2, ROWS_CELLS, 128), B16), pltpu.VMEM((CELLS, 2 * C), F32)],
         scalars=1,
         micros=3,
-        loads=(6, 8, 7, 9, 10),
+        loads=(5, 6, 7),
     )
     cells_mine, cells_partner = mine, lax.ppermute(send, "core", CORE_PAIRS)
     mine, send, grad_grid, grad_wire = call(
         cross_back_kernel,
         half(ROWS_LATE) + [((CELLS, C), F32), ((WIRE, F), B16)],
         (
-            core, query, keyval, prob, grad_cross_att, grid, query_weight, sensor_weight, slots,
+            core, query, keyval, prob, grad_cross_att, grid, query_weight, sensor_weight,
             grad_mixed,
         ),
         scratch=[
@@ -677,7 +679,7 @@
         ],
         scalars=1,
         micros=9,
-        loads=(1, 2, 5, 6, 7, 8, 9),
+        loads=(1, 2, 5, 6, 7, 8),
         raw=(3,),
         megabytes=20,
     )

time: 212 us -> 207 us (0.976)
  local copies, waits for them, and re-layouts: 17.9 us -> 13.5 us
    unnamed x86 -> x70, local copies, waits for them, and re-layouts: 17.8 us -> 13.5 us
where the time goes in v3:
time: 207 us; the launch traced here: 206 us
  waiting for transfers between devices  63.8 us (31%)
  starting transfers between devices  61.9 us (30%)
  Pallas kernels  41.2 us (20%)
  blocking collectives  24.8 us (12%)
  local copies, waits for them, and re-layouts  13.5 us (7%)
    pallas_call x22, Pallas kernels, call(): pl.pallas_call(body, out_shape=tuple((jax.ShapeDtypeStruct(s, d) for s, d...  41.2 us
    ppermute x21, starting transfers between devices, ring_sends(): lax.ppermute(piece, axis, [(i, (i + shift) % RING) for i in range(RING)])  32.3 us
    all_to_all x1, blocking collectives, on_device(): lax.all_to_all(outgoing.reshape(TILES, PITCH, F), ALL, split_axis=0, conc...  24.8 us
    unnamed x70, local copies, waits for them, and re-layouts  13.5 us
    ppermute x21, waiting for transfers between devices, ring_sends(): lax.ppermute(piece, axis, [(i, (i + shift) % RING) for i in range(RING)])  13.1 us
    all_to_all x1, waiting for transfers between devices, on_device(): lax.all_to_all(spread, LAT, split_axis=0, concat_axis=0, tiled=True)  10 us
    all_to_all x1, starting transfers between devices, swapped_parts(): return lax.all_to_all(blocks, axes, split_axis=0, concat_axis=0, tiled=True)  7.69 us
    ppermute x1, waiting for transfers between devices, on_device(): right = lax.ppermute(send_left, LON, west)  6.79 us
  transfers between devices with their start and end apart: 37, of which 21 were waited for; matrix products, arithmetic and copies ran while one was open for 0% of the time, Pallas kernels for 7%

profile of v3, /device:TPU:1, one launch (start us, length us, event | category | flops | bytes accessed | tf_op | source)
XLA Modules:
  0.0 206.1 jit_solution(1629452880872269545)
XLA Ops:
  4.5 24.8 %all_to_all.20 = bf16[128,8,256]{2,1,0:T(8,128)(2,1)S(1)} all-to-all(bf16[128,8,256]{2,1,0:T(8,128)(2,1)S(1)} %bitcast.21), channel_id=1, replica_groups=mesh['zlo'=2,'x'=4,'y'=4,'zhi'=2,'core'=2] {'zlo','x','y','zhi','core'}, dimensions={0} | all-to-all | bytes 1048576 | tf_op jit(solution)/shard_map/all_to_all | solution.py:600
  29.3 6.6 %shard_map.171 = (bf16[768,1280]{1,0:T(8,128)(2,1)S(1)}, bf16[128,512]{1,0:T(8,128)(2,1)S(1)}, bf16[4,768,512]{2,1,0:T(8,128)(2,1)S(1)}, bf16[128,1536]{1,0:T(8,128)(2,1)S(1)}, bf16[128,1024]{1,0:T(8,128)(2,1)S(1)}) custom-call(bf16[1024,256]{1,0:T(8,128)(2,1)S(1)} %bitcast.20, bf16[128,512]{1,0:T(8,128)(2,1)S(1)} %bitcast.24, ...), custom_call_target="tpu_custom_call" | custom-call | flops 7000000000 | tf_op jit(solution)/shard_map/pallas_call | solution.py:120
  35.9 1.2 copy-done.29
  37.2 1.4 collective-permute-start
  38.6 1.4 collective-permute-start.1
  40.0 2.5 %collective-permute-done.refs_0_ = bf16[96,1024]{1,0:T(8,128)(2,1)S(1)} collective-permute-done((bf16[96,1024]{1,0:T(8,128)(2,1)S(1)}, bf16[96,1024]{1,0:T(8,128)(2,1)S(1)}, u32[]{:S(2)}, u32[]{:S(2)}) %collective-permute-start) | collective-permute-done | bytes 196640 | tf_op jit(solution)/shard_map/ppermute | solution.py:615
  42.6 4.0 %collective-permute-done.1.refs_2_ = bf16[96,1024]{1,0:T(8,128)(2,1)S(1)} collective-permute-done((bf16[96,1024]{1,0:T(8,128)(2,1)S(1)}, bf16[96,1024]{1,0:T(8,128)(2,1)S(1)}, u32[]{:S(2)}, u32[]{:S(2)}) %collective-permute-start.1) | collective-permute-done | bytes 196640 | tf_op jit(solution)/shard_map/ppermute | solution.py:616
  46.6 1.2 shard_map.172
  48.6 2.8 %collective-permute-start.2 = (bf16[128,1024]{1,0:T(8,128)(2,1)}, bf16[128,1024]{1,0:T(8,128)(2,1)S(1)}, u32[]{:S(2)}, u32[]{:S(2)}) collective-permute-start(bf16[128,1024]{1,0:T(8,128)(2,1)} %get-tuple-element.55), channel_id=1, source_target_pairs={{0,1},{1,2},{2,3},{3,4},{4,5},{5,6},{6,7},{7,8},{8,9},{9,10},{10,1... | collective-permute-start | bytes 786440 | tf_op jit(solution)/shard_map/ppermute | solution.py:622
  51.4 3.6 %collective-permute-done.2.refs_3_ = bf16[128,1024]{1,0:T(8,128)(2,1)S(1)} collective-permute-done((bf16[128,1024]{1,0:T(8,128)(2,1)}, bf16[128,1024]{1,0:T(8,128)(2,1)S(1)}, u32[]{:S(2)}, u32[]{:S(2)}) %collective-permute-start.2) | collective-permute-done | bytes 262176 | tf_op jit(solution)/shard_map/ppermute | solution.py:622
  55.1 6.8 %collective-permute-done.3.refs_4_ = bf16[128,1024]{1,0:T(8,128)(2,1)} collective-permute-done((bf16[128,1024]{1,0:T(8,128)(2,1)}, bf16[128,1024]{1,0:T(8,128)(2,1)}, u32[]{:S(2)}, u32[]{:S(2)}) %collective-permute-start.3) | collective-permute-done | bytes 262176 | tf_op jit(solution)/shard_map/ppermute | solution.py:623
  63.9 8.7 %shard_map.173 = (bf16[128,512]{1,0:T(8,128)(2,1)}, bf16[128,2048]{1,0:T(8,128)(2,1)S(1)}, f32[320,1024]{1,0:T(8,128)S(1)}, bf16[128,1024]{1,0:T(8,128)(2,1)S(1)}, bf16[128,1024]{1,0:T(8,128)(2,1)S(1)}) custom-call(s32[1]{0:T(128)} %bitcast.refs_0_, bf16[128,1536]{1,0:T(8,128)(2,1)S(1)} %copy-done.32, bf16[320,1024]{1,0:T(8,128)(2,1)S(1)} %copy-done.22, ...), custom_call_target="tpu_custom_call" | custom-call | flops 8999999488 | tf_op jit(solution)/shard_map/pallas_call | solution.py:120
  73.1 5.6 %collective-permute-done.4.refs_1_ = bf16[128,1024]{1,0:T(8,128)(2,1)S(1)} collective-permute-done((bf16[128,1024]{1,0:T(8,128)(2,1)S(1)}, bf16[128,1024]{1,0:T(8,128)(2,1)S(1)}, u32[]{:S(2)}, u32[]{:S(2)}) %collective-permute-start.4) | collective-permute-done | bytes 262176 | tf_op jit(solution)/shard_map/ppermute | solution.py:644
  78.7 3.3 %collective-permute-done.5.refs_2_ = bf16[128,1024]{1,0:T(8,128)(2,1)S(1)} collective-permute-done((bf16[128,1024]{1,0:T(8,128)(2,1)S(1)}, bf16[128,1024]{1,0:T(8,128)(2,1)S(1)}, u32[]{:S(2)}, u32[]{:S(2)}) %collective-permute-start.5) | collective-permute-done | bytes 262176 | tf_op jit(solution)/shard_map/ppermute | solution.py:643
  84.0 3.1 %collective-permute-start.6 = (bf16[96,1024]{1,0:T(8,128)(2,1)}, bf16[96,1024]{1,0:T(8,128)(2,1)S(1)}, u32[]{:S(2)}, u32[]{:S(2)}) collective-permute-start(bf16[96,1024]{1,0:T(8,128)(2,1)} %get-tuple-element.66), channel_id=1, source_target_pairs={{0,16},{16,32},{32,48},{48,64},{64,80},{80,96},{96,112},{1,17},{17... | collective-permute-start | bytes 589832 | tf_op jit(solution)/shard_map/ppermute | solution.py:652
  87.1 1.3 collective-permute-start.7
  88.4 2.1 %collective-permute-done.6.refs_3_ = bf16[96,1024]{1,0:T(8,128)(2,1)S(1)} collective-permute-done((bf16[96,1024]{1,0:T(8,128)(2,1)}, bf16[96,1024]{1,0:T(8,128)(2,1)S(1)}, u32[]{:S(2)}, u32[]{:S(2)}) %collective-permute-start.6) | collective-permute-done | bytes 196640 | tf_op jit(solution)/shard_map/ppermute | solution.py:652
  90.5 3.8 %collective-permute-done.7.refs_4_ = bf16[96,1024]{1,0:T(8,128)(2,1)S(1)} collective-permute-done((bf16[96,1024]{1,0:T(8,128)(2,1)S(1)}, bf16[96,1024]{1,0:T(8,128)(2,1)S(1)}, u32[]{:S(2)}, u32[]{:S(2)}) %collective-permute-start.7) | collective-permute-done | bytes 196640 | tf_op jit(solution)/shard_map/ppermute | solution.py:651
  98.9 2.6 %shard_map.175 = (bf16[5120,128]{1,0:T(8,128)(2,1)S(1)}, bf16[5120,128]{1,0:T(8,128)(2,1)S(1)}, f32[128,512]{1,0:T(8,128)S(1)}, bf16[128,512]{1,0:T(8,128)(2,1)S(1)}) custom-call(s32[1]{0:T(128)} %bitcast.9.refs_0_, bf16[128,2048]{1,0:T(8,128)(2,1)S(1)} %copy-done.26, f32[128,1024]{1,0:T(8,128)S(1)} %copy-done.18, ...), custom_call_target="tpu_custom_call" | custom-call | flops 3000000000 | tf_op jit(solution)/shard_map/pallas_call | solution.py:120
  101.8 11.1 %shard_map.176 = (bf16[2048,128]{1,0:T(8,128)(2,1)S(1)}, bf16[2048,128]{1,0:T(8,128)(2,1)S(1)}, f32[128,512]{1,0:T(8,128)}, bf16[1024,256]{1,0:T(8,128)(2,1)}) custom-call(s32[1]{0:T(128)} %bitcast.9.refs_0_, bf16[128,512]{1,0:T(8,128)(2,1)S(1)} %copy-done.34, bf16[768,1280]{1,0:T(8,128)(2,1)S(1)} %copy-done.30, bf16[4,768,512]{2,1,0:T(8,128)(2,1)S(1)} %copy-done.28, ...), custom_call_target="tpu_custom_call" | custom-call | flops 8999999488 | tf_op jit(solution)/shard_map/pallas_call | solution.py:120
  113.0 1.4 shard_map.177
  114.4 7.7 %all-to-all-start.2 = ((bf16[8,640,128]{2,1,0:T(8,128)(2,1)}), bf16[8,640,128]{2,1,0:T(8,128)(2,1)S(1)}, u32[]{:S(2)}, u32[]{:S(2)}) async-start(bf16[8,640,128]{2,1,0:T(8,128)(2,1)} %bitcast.14), calls=%async_computation.2 | async-start | bytes 2621440 | tf_op jit(solution)/shard_map/all_to_all | solution.py:575
  122.8 1.5 collective-permute-done.9.refs_2_
  124.7 2.6 %collective-permute-start.12 = (bf16[512,128]{1,0:T(8,128)(2,1)S(1)}, bf16[512,128]{1,0:T(8,128)(2,1)S(1)}, u32[]{:S(2)}, u32[]{:S(2)}) collective-permute-start(bf16[512,128]{1,0:T(8,128)(2,1)S(1)} %get-tuple-element.80), channel_id=1, source_target_pairs={{0,12},{4,0},{8,4},{12,8},{1,13},{5,1},{9,5},{13,9},{2,14},{6,2},{... | collective-permute-start | bytes 393224 | tf_op jit(solution)/shard_map/ppermute | solution.py:557
  127.2 6.4 %collective-permute-done.10.refs_2_ = bf16[512,128]{1,0:T(8,128)(2,1)S(1)} collective-permute-done((bf16[512,128]{1,0:T(8,128)(2,1)S(1)}, bf16[512,128]{1,0:T(8,128)(2,1)S(1)}, u32[]{:S(2)}, u32[]{:S(2)}) %collective-permute-start.10) | collective-permute-done | bytes 131104 | tf_op jit(solution)/shard_map/ppermute | solution.py:557
  133.7 1.8 collective-permute-start.13
  135.5 2.4 %collective-permute-start.14 = (bf16[128,128]{1,0:T(8,128)(2,1)S(1)}, bf16[128,128]{1,0:T(8,128)(2,1)S(1)}, u32[]{:S(2)}, u32[]{:S(2)}) collective-permute-start(bf16[128,128]{1,0:T(8,128)(2,1)S(1)} %get-tuple-element.83), channel_id=1, source_target_pairs={{0,32},{16,48},{32,0},{48,16},{1,33},{17,49},{33,1},{49,17},{2,34}... | collective-permute-start | bytes 98312 | tf_op jit(solution)/shard_map/ppermute | solution.py:557
  139.1 1.6 all-to-all-done.2.refs_1_
  140.7 4.8 %all-to-all-start.1 = ((bf16[128,8,256]{2,1,0:T(8,128)(2,1)}), bf16[128,8,256]{2,1,0:T(8,128)(2,1)S(1)}, u32[]{:S(2)}, u32[]{:S(2)}) async-start(bf16[128,8,256]{2,1,0:T(8,128)(2,1)} %bitcast.11), calls=%async_computation.1 | async-start | bytes 1048576 | tf_op jit(solution)/shard_map/all_to_all | solution.py:690
  145.6 3.5 %collective-permute-start.19 = (bf16[128,128]{1,0:T(8,128)(2,1)S(1)}, bf16[128,128]{1,0:T(8,128)(2,1)S(1)}, u32[]{:S(2)}, u32[]{:S(2)}) collective-permute-start(bf16[128,128]{1,0:T(8,128)(2,1)S(1)} %shard_map.180.refs_2_.refs_1_), channel_id=1, source_target_pairs={{0,2},{2,64},{64,66},{66,0},{1,3},{3,65},{65,67},{67,1},{4,6},{6,6... | collective-permute-start | bytes 98312 | tf_op jit(solution)/shard_map/ppermute | solution.py:557
  149.9 1.3 collective-permute-start.16
  151.2 2.5 %collective-permute-start.17 = (bf16[160,128]{1,0:T(8,128)(2,1)S(1)}, bf16[160,128]{1,0:T(8,128)(2,1)S(1)}, u32[]{:S(2)}, u32[]{:S(2)}) collective-permute-start(bf16[160,128]{1,0:T(8,128)(2,1)S(1)} %get-tuple-element.87), channel_id=1, source_target_pairs={{0,8},{4,12},{8,0},{12,4},{1,9},{5,13},{9,1},{13,5},{2,10},{6,14},... | collective-permute-start | bytes 122888 | tf_op jit(solution)/shard_map/ppermute | solution.py:557
  153.8 2.7 %collective-permute-start.18 = (bf16[160,128]{1,0:T(8,128)(2,1)S(1)}, bf16[160,128]{1,0:T(8,128)(2,1)S(1)}, u32[]{:S(2)}, u32[]{:S(2)}) collective-permute-start(bf16[160,128]{1,0:T(8,128)(2,1)S(1)} %get-tuple-element.88), channel_id=1, source_target_pairs={{0,12},{4,0},{8,4},{12,8},{1,13},{5,1},{9,5},{13,9},{2,14},{6,2},{... | collective-permute-start | bytes 122888 | tf_op jit(solution)/shard_map/ppermute | solution.py:557
  156.5 2.9 %collective-permute-start.23 = (bf16[128,128]{1,0:T(8,128)(2,1)S(1)}, bf16[128,128]{1,0:T(8,128)(2,1)S(1)}, u32[]{:S(2)}, u32[]{:S(2)}) collective-permute-start(bf16[128,128]{1,0:T(8,128)(2,1)S(1)} %shard_map.182.refs_4_.refs_1_), channel_id=1, source_target_pairs={{0,16},{16,32},{32,48},{48,0},{1,17},{17,33},{33,49},{49,1},{2,18}... | collective-permute-start | bytes 98312 | tf_op jit(solution)/shard_map/ppermute | solution.py:557
  159.3 2.6 %collective-permute-start.24 = (bf16[128,128]{1,0:T(8,128)(2,1)S(1)}, bf16[128,128]{1,0:T(8,128)(2,1)S(1)}, u32[]{:S(2)}, u32[]{:S(2)}) collective-permute-start(bf16[128,128]{1,0:T(8,128)(2,1)S(1)} %shard_map.182.refs_4_.refs_1_), channel_id=1, source_target_pairs={{0,32},{16,48},{32,0},{48,16},{1,33},{17,49},{33,1},{49,17},{2,34}... | collective-permute-start | bytes 98312 | tf_op jit(solution)/shard_map/ppermute | solution.py:557
  163.6 1.4 collective-permute-done.25.refs_4_
  165.1 2.5 %collective-permute-done.22.refs_1_ = bf16[160,128]{1,0:T(8,128)(2,1)S(1)} collective-permute-done((bf16[160,128]{1,0:T(8,128)(2,1)S(1)}, bf16[160,128]{1,0:T(8,128)(2,1)S(1)}, u32[]{:S(2)}, u32[]{:S(2)}) %collective-permute-start.22) | collective-permute-done | bytes 40992 | tf_op jit(solution)/shard_map/ppermute | solution.py:720
  167.6 2.2 %collective-permute-start.30 = (bf16[160,128]{1,0:T(8,128)(2,1)S(1)}, bf16[160,128]{1,0:T(8,128)(2,1)S(1)}, u32[]{:S(2)}, u32[]{:S(2)}) collective-permute-start(bf16[160,128]{1,0:T(8,128)(2,1)S(1)} %shard_map.185.refs_2_.refs_1_), channel_id=1, source_target_pairs={{0,8},{4,12},{8,0},{12,4},{1,9},{5,13},{9,1},{13,5},{2,10},{6,14},... | collective-permute-start | bytes 122888 | tf_op jit(solution)/shard_map/ppermute | solution.py:557
  173.6 1.2 shard_map.187.refs_5_
  174.8 3.6 %all-to-all-start.3 = ((bf16[8,640,128]{2,1,0:T(8,128)(2,1)}), bf16[8,640,128]{2,1,0:T(8,128)(2,1)S(1)}, u32[]{:S(2)}, u32[]{:S(2)}) async-start(bf16[8,640,128]{2,1,0:T(8,128)(2,1)} %shard_map.187.refs_5_), calls=%async_computation.3 | async-start | bytes 2621440 | tf_op jit(solution)/shard_map/all_to_all | solution.py:730
  179.5 2.5 %collective-permute-start.27 = (bf16[512,128]{1,0:T(8,128)(2,1)S(1)}, bf16[512,128]{1,0:T(8,128)(2,1)S(1)}, u32[]{:S(2)}, u32[]{:S(2)}) collective-permute-start(bf16[512,128]{1,0:T(8,128)(2,1)S(1)} %shard_map.184.refs_2_.refs_1_), channel_id=1, source_target_pairs={{0,8},{4,12},{8,0},{12,4},{1,9},{5,13},{9,1},{13,5},{2,10},{6,14},... | collective-permute-start | bytes 393224 | tf_op jit(solution)/shard_map/ppermute | solution.py:557
  182.1 1.4 collective-permute-done.26.refs_2_
  183.5 2.3 %collective-permute-done.27.refs_3_ = bf16[512,128]{1,0:T(8,128)(2,1)S(1)} collective-permute-done((bf16[512,128]{1,0:T(8,128)(2,1)S(1)}, bf16[512,128]{1,0:T(8,128)(2,1)S(1)}, u32[]{:S(2)}, u32[]{:S(2)}) %collective-permute-start.27) | collective-permute-done | bytes 131104 | tf_op jit(solution)/shard_map/ppermute | solution.py:557
  186.2 10.0 %all-to-all-done.3 = bf16[8,640,128]{2,1,0:T(8,128)(2,1)S(1)} async-done(((bf16[8,640,128]{2,1,0:T(8,128)(2,1)}), bf16[8,640,128]{2,1,0:T(8,128)(2,1)S(1)}, u32[]{:S(2)}, u32[]{:S(2)}) %all-to-all-start.3) | async-done | bytes 1310752 | tf_op jit(solution)/shard_map/all_to_all | solution.py:730
  196.4 1.8 collective-permute-start.33
  198.2 3.3 %collective-permute-done.32.refs_2_ = bf16[2048,128]{1,0:T(8,128)(2,1)S(1)} collective-permute-done((bf16[2048,128]{1,0:T(8,128)(2,1)S(1)}, bf16[2048,128]{1,0:T(8,128)(2,1)S(1)}, u32[]{:S(2)}, u32[]{:S(2)}) %collective-permute-start.32) | collective-permute-done | bytes 524320 | tf_op jit(solution)/shard_map/ppermute | solution.py:738
  201.5 1.6 shard_map.189
  203.1 3.0 %shard_map.191 = (f32[512,512]{1,0:T(8,128)}, f32[512,1536]{1,0:T(8,128)}, f32[512,512]{1,0:T(8,128)}) custom-call(s32[1]{0:T(128)} %bitcast.9.refs_0_, bf16[5120,128]{1,0:T(8,128)(2,1)S(1)} %shard_map.190.refs_1_, bf16[5120,128]{1,0:T(8,128)(2,1)S(1)} %collective-permute-done.33.refs_2_), custom_call_target="tpu_custom_call" | custom-call | flops 3000000000 | tf_op jit(solution)/shard_map/pallas_call | solution.py:120
  (120 shorter events, 24.6 us)
Async XLA Ops:
  3.6 25.7 %copy-start = (bf16[512,1536]{1,0:T(8,128)(2,1)S(1)}, bf16[512,1536]{1,0:T(8,128)(2,1)}, u32[]{:S(2)}) copy-start(bf16[512,1536]{1,0:T(8,128)(2,1)} %refs_6_.4) | copy-start | bytes 4718596
  3.6 25.7 %copy-start.2 = (bf16[512,512]{1,0:T(8,128)(2,1)S(1)}, bf16[512,512]{1,0:T(8,128)(2,1)}, u32[]{:S(2)}) copy-start(bf16[512,512]{1,0:T(8,128)(2,1)} %refs_7_.2) | copy-start | bytes 1572868
  3.6 25.7 %copy-start.3 = (bf16[512,512]{1,0:T(8,128)(2,1)S(1)}, bf16[512,512]{1,0:T(8,128)(2,1)}, u32[]{:S(2)}) copy-start(bf16[512,512]{1,0:T(8,128)(2,1)} %refs_6_.5) | copy-start | bytes 1572868
  3.6 25.7 %copy-start.4 = (bf16[256,1024]{1,0:T(8,128)(2,1)S(1)}, bf16[256,1024]{1,0:T(8,128)(2,1)}, u32[]{:S(2)}) copy-start(bf16[256,1024]{1,0:T(8,128)(2,1)} %refs_7_.3) | copy-start | bytes 1572868
  3.6 25.7 %copy-start.11 = (bf16[8,16,512]{2,1,0:T(8,128)(2,1)S(1)}, bf16[8,16,512]{2,1,0:T(8,128)(2,1)}, u32[]{:S(2)}) copy-start(bf16[8,16,512]{2,1,0:T(8,128)(2,1)} %param.11) | copy-start | bytes 393220
  4.5 31.4 %copy-start.23 = (s32[256,1]{1,0:T(8,128)}, s32[256,1]{1,0:T(8,128)S(1)}, u32[]{:S(2)}) copy-start(s32[256,1]{1,0:T(8,128)S(1)} %get-tuple-element.71.refs_0_) | copy-start | bytes 3076
  37.2 10.6 %copy-start.31 = (bf16[128,1536]{1,0:T(8,128)(2,1)}, bf16[128,1536]{1,0:T(8,128)(2,1)S(1)}, u32[]{:S(2)}) copy-start(bf16[128,1536]{1,0:T(8,128)(2,1)S(1)} %get-tuple-element.52.refs_1_) | copy-start | bytes 1179652
  37.2 10.6 %copy-start.33 = (bf16[128,512]{1,0:T(8,128)(2,1)}, bf16[128,512]{1,0:T(8,128)(2,1)S(1)}, u32[]{:S(2)}) copy-start(bf16[128,512]{1,0:T(8,128)(2,1)S(1)} %get-tuple-element.58.refs_1_) | copy-start | bytes 393220
  37.2 5.4 %collective-permute-start = (bf16[96,1024]{1,0:T(8,128)(2,1)S(1)}, bf16[96,1024]{1,0:T(8,128)(2,1)S(1)}, u32[]{:S(2)}, u32[]{:S(2)}) collective-permute-start(bf16[96,1024]{1,0:T(8,128)(2,1)S(1)} %get-tuple-element.95), channel_id=1, source_target_pairs={{0,16},{16,32},{32,48},{48,64},{64,80},{80,96},{96,112},{1,17},{17... | collective-permute-start | bytes 589832 | tf_op jit(solution)/shard_map/ppermute | solution.py:615
  38.6 23.3 %copy-start.1 = (bf16[512,512]{1,0:T(8,128)(2,1)S(1)}, bf16[512,512]{1,0:T(8,128)(2,1)}, u32[]{:S(2)}) copy-start(bf16[512,512]{1,0:T(8,128)(2,1)} %refs_6_.3) | copy-start | bytes 1572868
  38.6 23.2 %copy-start.9 = (bf16[8,16,512]{2,1,0:T(8,128)(2,1)S(1)}, bf16[8,16,512]{2,1,0:T(8,128)(2,1)}, u32[]{:S(2)}) copy-start(bf16[8,16,512]{2,1,0:T(8,128)(2,1)} %param.21) | copy-start | bytes 393220
  38.6 7.9 %collective-permute-start.1 = (bf16[96,1024]{1,0:T(8,128)(2,1)S(1)}, bf16[96,1024]{1,0:T(8,128)(2,1)S(1)}, u32[]{:S(2)}, u32[]{:S(2)}) collective-permute-start(bf16[96,1024]{1,0:T(8,128)(2,1)S(1)} %get-tuple-element.94), channel_id=1, source_target_pairs={{16,0},{32,16},{48,32},{64,48},{80,64},{96,80},{112,96},{17,1},{33... | collective-permute-start | bytes 589832 | tf_op jit(solution)/shard_map/ppermute | solution.py:616
  48.6 6.5 %collective-permute-start.2 = (bf16[128,1024]{1,0:T(8,128)(2,1)}, bf16[128,1024]{1,0:T(8,128)(2,1)S(1)}, u32[]{:S(2)}, u32[]{:S(2)}) collective-permute-start(bf16[128,1024]{1,0:T(8,128)(2,1)} %get-tuple-element.55), channel_id=1, source_target_pairs={{0,1},{1,2},{2,3},{3,4},{4,5},{5,6},{6,7},{7,8},{8,9},{9,10},{10,1... | collective-permute-start | bytes 786440 | tf_op jit(solution)/shard_map/ppermute | solution.py:622
  51.4 10.4 %collective-permute-start.3 = (bf16[128,1024]{1,0:T(8,128)(2,1)}, bf16[128,1024]{1,0:T(8,128)(2,1)}, u32[]{:S(2)}, u32[]{:S(2)}) collective-permute-start(bf16[128,1024]{1,0:T(8,128)(2,1)} %get-tuple-element.56), channel_id=1, source_target_pairs={{1,0},{2,1},{3,2},{4,3},{5,4},{6,5},{7,6},{8,7},{9,8},{10,9},{11,1... | collective-permute-start | bytes 786440 | tf_op jit(solution)/shard_map/ppermute | solution.py:623
  72.6 10.6 %copy-start.25 = (bf16[128,2048]{1,0:T(8,128)(2,1)}, bf16[128,2048]{1,0:T(8,128)(2,1)S(1)}, u32[]{:S(2)}) copy-start(bf16[128,2048]{1,0:T(8,128)(2,1)S(1)} %get-tuple-element.61.refs_1_) | copy-start | bytes 1572868
  72.6 6.1 %collective-permute-start.4 = (bf16[128,1024]{1,0:T(8,128)(2,1)S(1)}, bf16[128,1024]{1,0:T(8,128)(2,1)S(1)}, u32[]{:S(2)}, u32[]{:S(2)}) collective-permute-start(bf16[128,1024]{1,0:T(8,128)(2,1)S(1)} %get-tuple-element.63), channel_id=1, source_target_pairs={{0,1},{1,2},{2,3},{3,4},{4,5},{5,6},{6,7},{7,8},{8,9},{9,10},{10,1... | collective-permute-start | bytes 786440 | tf_op jit(solution)/shard_map/ppermute | solution.py:644
  72.6 9.4 %collective-permute-start.5 = (bf16[128,1024]{1,0:T(8,128)(2,1)S(1)}, bf16[128,1024]{1,0:T(8,128)(2,1)S(1)}, u32[]{:S(2)}, u32[]{:S(2)}) collective-permute-start(bf16[128,1024]{1,0:T(8,128)(2,1)S(1)} %get-tuple-element.64), channel_id=1, source_target_pairs={{1,0},{2,1},{3,2},{4,3},{5,4},{6,5},{7,6},{8,7},{9,8},{10,9},{11,1... | collective-permute-start | bytes 786440 | tf_op jit(solution)/shard_map/ppermute | solution.py:643
  84.0 6.5 %collective-permute-start.6 = (bf16[96,1024]{1,0:T(8,128)(2,1)}, bf16[96,1024]{1,0:T(8,128)(2,1)S(1)}, u32[]{:S(2)}, u32[]{:S(2)}) collective-permute-start(bf16[96,1024]{1,0:T(8,128)(2,1)} %get-tuple-element.66), channel_id=1, source_target_pairs={{0,16},{16,32},{32,48},{48,64},{64,80},{80,96},{96,112},{1,17},{17... | collective-permute-start | bytes 589832 | tf_op jit(solution)/shard_map/ppermute | solution.py:652
  87.1 7.2 %collective-permute-start.7 = (bf16[96,1024]{1,0:T(8,128)(2,1)S(1)}, bf16[96,1024]{1,0:T(8,128)(2,1)S(1)}, u32[]{:S(2)}, u32[]{:S(2)}) collective-permute-start(bf16[96,1024]{1,0:T(8,128)(2,1)S(1)} %get-tuple-element.67), channel_id=1, source_target_pairs={{16,0},{32,16},{48,32},{64,48},{80,64},{96,80},{112,96},{17,1},{33... | collective-permute-start | bytes 589832 | tf_op jit(solution)/shard_map/ppermute | solution.py:651
  101.5 11.5 %collective-permute-start.8 = (bf16[5120,128]{1,0:T(8,128)(2,1)S(1)}, bf16[5120,128]{1,0:T(8,128)(2,1)S(1)}, u32[]{:S(2)}, u32[]{:S(2)}) collective-permute-start(bf16[5120,128]{1,0:T(8,128)(2,1)S(1)} %get-tuple-element.74), channel_id=1, source_target_pairs={{0,1},{1,0},{2,3},{3,2},{4,5},{5,4},{6,7},{7,6},{8,9},{9,8},{10,11... | collective-permute-start | bytes 3932168 | tf_op jit(solution)/shard_map/ppermute | solution.py:666
  114.4 26.3 %all-to-all-start.2 = ((bf16[8,640,128]{2,1,0:T(8,128)(2,1)}), bf16[8,640,128]{2,1,0:T(8,128)(2,1)S(1)}, u32[]{:S(2)}, u32[]{:S(2)}) async-start(bf16[8,640,128]{2,1,0:T(8,128)(2,1)} %bitcast.14), calls=%async_computation.2 | async-start | bytes 2621440 | tf_op jit(solution)/shard_map/all_to_all | solution.py:575
  122.1 2.3 %collective-permute-start.9 = (bf16[2048,128]{1,0:T(8,128)(2,1)S(1)}, bf16[2048,128]{1,0:T(8,128)(2,1)S(1)}, u32[]{:S(2)}, u32[]{:S(2)}) collective-permute-start(bf16[2048,128]{1,0:T(8,128)(2,1)S(1)} %get-tuple-element.76), channel_id=1, source_target_pairs={{0,1},{1,0},{2,3},{3,2},{4,5},{5,4},{6,7},{7,6},{8,9},{9,8},{10,11... | collective-permute-start | bytes 1572872 | tf_op jit(solution)/shard_map/ppermute | solution.py:698
  124.5 9.1 %collective-permute-start.10 = (bf16[512,128]{1,0:T(8,128)(2,1)S(1)}, bf16[512,128]{1,0:T(8,128)(2,1)S(1)}, u32[]{:S(2)}, u32[]{:S(2)}) collective-permute-start(bf16[512,128]{1,0:T(8,128)(2,1)S(1)} %get-tuple-element.78), channel_id=1, source_target_pairs={{0,4},{4,8},{8,12},{12,0},{1,5},{5,9},{9,13},{13,1},{2,6},{6,10},{... | collective-permute-start | bytes 393224 | tf_op jit(solution)/shard_map/ppermute | solution.py:557
  124.6 9.1 %collective-permute-start.11 = (bf16[512,128]{1,0:T(8,128)(2,1)S(1)}, bf16[512,128]{1,0:T(8,128)(2,1)S(1)}, u32[]{:S(2)}, u32[]{:S(2)}) collective-permute-start(bf16[512,128]{1,0:T(8,128)(2,1)S(1)} %get-tuple-element.79), channel_id=1, source_target_pairs={{0,8},{4,12},{8,0},{12,4},{1,9},{5,13},{9,1},{13,5},{2,10},{6,14},... | collective-permute-start | bytes 393224 | tf_op jit(solution)/shard_map/ppermute | solution.py:557
  124.7 9.0 %collective-permute-start.12 = (bf16[512,128]{1,0:T(8,128)(2,1)S(1)}, bf16[512,128]{1,0:T(8,128)(2,1)S(1)}, u32[]{:S(2)}, u32[]{:S(2)}) collective-permute-start(bf16[512,128]{1,0:T(8,128)(2,1)S(1)} %get-tuple-element.80), channel_id=1, source_target_pairs={{0,12},{4,0},{8,4},{12,8},{1,13},{5,1},{9,5},{13,9},{2,14},{6,2},{... | collective-permute-start | bytes 393224 | tf_op jit(solution)/shard_map/ppermute | solution.py:557
  133.7 11.8 %collective-permute-start.13 = (bf16[128,128]{1,0:T(8,128)(2,1)S(1)}, bf16[128,128]{1,0:T(8,128)(2,1)S(1)}, u32[]{:S(2)}, u32[]{:S(2)}) collective-permute-start(bf16[128,128]{1,0:T(8,128)(2,1)S(1)} %get-tuple-element.82), channel_id=1, source_target_pairs={{0,16},{16,32},{32,48},{48,0},{1,17},{17,33},{33,49},{49,1},{2,18}... | collective-permute-start | bytes 98312 | tf_op jit(solution)/shard_map/ppermute | solution.py:557
  135.5 10.0 %collective-permute-start.14 = (bf16[128,128]{1,0:T(8,128)(2,1)S(1)}, bf16[128,128]{1,0:T(8,128)(2,1)S(1)}, u32[]{:S(2)}, u32[]{:S(2)}) collective-permute-start(bf16[128,128]{1,0:T(8,128)(2,1)S(1)} %get-tuple-element.83), channel_id=1, source_target_pairs={{0,32},{16,48},{32,0},{48,16},{1,33},{17,49},{33,1},{49,17},{2,34}... | collective-permute-start | bytes 98312 | tf_op jit(solution)/shard_map/ppermute | solution.py:557
  137.9 7.6 %collective-permute-start.15 = (bf16[128,128]{1,0:T(8,128)(2,1)S(1)}, bf16[128,128]{1,0:T(8,128)(2,1)S(1)}, u32[]{:S(2)}, u32[]{:S(2)}) collective-permute-start(bf16[128,128]{1,0:T(8,128)(2,1)S(1)} %get-tuple-element.84), channel_id=1, source_target_pairs={{0,48},{16,0},{32,16},{48,32},{1,49},{17,1},{33,17},{49,33},{2,50}... | collective-permute-start | bytes 98312 | tf_op jit(solution)/shard_map/ppermute | solution.py:557
  140.7 30.2 %all-to-all-start.1 = ((bf16[128,8,256]{2,1,0:T(8,128)(2,1)}), bf16[128,8,256]{2,1,0:T(8,128)(2,1)S(1)}, u32[]{:S(2)}, u32[]{:S(2)}) async-start(bf16[128,8,256]{2,1,0:T(8,128)(2,1)} %bitcast.11), calls=%async_computation.1 | async-start | bytes 1048576 | tf_op jit(solution)/shard_map/all_to_all | solution.py:690
  145.6 8.2 %collective-permute-start.19 = (bf16[128,128]{1,0:T(8,128)(2,1)S(1)}, bf16[128,128]{1,0:T(8,128)(2,1)S(1)}, u32[]{:S(2)}, u32[]{:S(2)}) collective-permute-start(bf16[128,128]{1,0:T(8,128)(2,1)S(1)} %shard_map.180.refs_2_.refs_1_), channel_id=1, source_target_pairs={{0,2},{2,64},{64,66},{66,0},{1,3},{3,65},{65,67},{67,1},{4,6},{6,6... | collective-permute-start | bytes 98312 | tf_op jit(solution)/shard_map/ppermute | solution.py:557
  149.1 7.3 %collective-permute-start.20 = (bf16[128,128]{1,0:T(8,128)(2,1)S(1)}, bf16[128,128]{1,0:T(8,128)(2,1)S(1)}, u32[]{:S(2)}, u32[]{:S(2)}) collective-permute-start(bf16[128,128]{1,0:T(8,128)(2,1)S(1)} %shard_map.180.refs_2_.refs_1_), channel_id=1, source_target_pairs={{0,64},{2,66},{64,0},{66,2},{1,65},{3,67},{65,1},{67,3},{4,68},{6,... | collective-permute-start | bytes 98312 | tf_op jit(solution)/shard_map/ppermute | solution.py:557
  149.7 6.8 %collective-permute-start.21 = (bf16[128,128]{1,0:T(8,128)(2,1)S(1)}, bf16[128,128]{1,0:T(8,128)(2,1)S(1)}, u32[]{:S(2)}, u32[]{:S(2)}) collective-permute-start(bf16[128,128]{1,0:T(8,128)(2,1)S(1)} %shard_map.180.refs_2_.refs_1_), channel_id=1, source_target_pairs={{0,66},{2,0},{64,2},{66,64},{1,67},{3,1},{65,3},{67,65},{4,70},{6,... | collective-permute-start | bytes 98312 | tf_op jit(solution)/shard_map/ppermute | solution.py:557
  149.9 12.1 %collective-permute-start.16 = (bf16[160,128]{1,0:T(8,128)(2,1)S(1)}, bf16[160,128]{1,0:T(8,128)(2,1)S(1)}, u32[]{:S(2)}, u32[]{:S(2)}) collective-permute-start(bf16[160,128]{1,0:T(8,128)(2,1)S(1)} %get-tuple-element.86), channel_id=1, source_target_pairs={{0,4},{4,8},{8,12},{12,0},{1,5},{5,9},{9,13},{13,1},{2,6},{6,10},{... | collective-permute-start | bytes 122888 | tf_op jit(solution)/shard_map/ppermute | solution.py:557
  151.2 11.8 %collective-permute-start.17 = (bf16[160,128]{1,0:T(8,128)(2,1)S(1)}, bf16[160,128]{1,0:T(8,128)(2,1)S(1)}, u32[]{:S(2)}, u32[]{:S(2)}) collective-permute-start(bf16[160,128]{1,0:T(8,128)(2,1)S(1)} %get-tuple-element.87), channel_id=1, source_target_pairs={{0,8},{4,12},{8,0},{12,4},{1,9},{5,13},{9,1},{13,5},{2,10},{6,14},... | collective-permute-start | bytes 122888 | tf_op jit(solution)/shard_map/ppermute | solution.py:557
  153.8 9.3 %collective-permute-start.18 = (bf16[160,128]{1,0:T(8,128)(2,1)S(1)}, bf16[160,128]{1,0:T(8,128)(2,1)S(1)}, u32[]{:S(2)}, u32[]{:S(2)}) collective-permute-start(bf16[160,128]{1,0:T(8,128)(2,1)S(1)} %get-tuple-element.88), channel_id=1, source_target_pairs={{0,12},{4,0},{8,4},{12,8},{1,13},{5,1},{9,5},{13,9},{2,14},{6,2},{... | collective-permute-start | bytes 122888 | tf_op jit(solution)/shard_map/ppermute | solution.py:557
  156.5 6.8 %collective-permute-start.23 = (bf16[128,128]{1,0:T(8,128)(2,1)S(1)}, bf16[128,128]{1,0:T(8,128)(2,1)S(1)}, u32[]{:S(2)}, u32[]{:S(2)}) collective-permute-start(bf16[128,128]{1,0:T(8,128)(2,1)S(1)} %shard_map.182.refs_4_.refs_1_), channel_id=1, source_target_pairs={{0,16},{16,32},{32,48},{48,0},{1,17},{17,33},{33,49},{49,1},{2,18}... | collective-permute-start | bytes 98312 | tf_op jit(solution)/shard_map/ppermute | solution.py:557
  159.3 4.3 %collective-permute-start.24 = (bf16[128,128]{1,0:T(8,128)(2,1)S(1)}, bf16[128,128]{1,0:T(8,128)(2,1)S(1)}, u32[]{:S(2)}, u32[]{:S(2)}) collective-permute-start(bf16[128,128]{1,0:T(8,128)(2,1)S(1)} %shard_map.182.refs_4_.refs_1_), channel_id=1, source_target_pairs={{0,32},{16,48},{32,0},{48,16},{1,33},{17,49},{33,1},{49,17},{2,34}... | collective-permute-start | bytes 98312 | tf_op jit(solution)/shard_map/ppermute | solution.py:557
  162.0 3.1 %collective-permute-start.25 = (bf16[128,128]{1,0:T(8,128)(2,1)S(1)}, bf16[128,128]{1,0:T(8,128)(2,1)S(1)}, u32[]{:S(2)}, u32[]{:S(2)}) collective-permute-start(bf16[128,128]{1,0:T(8,128)(2,1)S(1)} %shard_map.182.refs_4_.refs_1_), channel_id=1, source_target_pairs={{0,48},{16,0},{32,16},{48,32},{1,49},{17,1},{33,17},{49,33},{2,50}... | collective-permute-start | bytes 98312 | tf_op jit(solution)/shard_map/ppermute | solution.py:557
  163.1 4.4 %collective-permute-start.22 = (bf16[160,128]{1,0:T(8,128)(2,1)S(1)}, bf16[160,128]{1,0:T(8,128)(2,1)S(1)}, u32[]{:S(2)}, u32[]{:S(2)}) collective-permute-start(bf16[160,128]{1,0:T(8,128)(2,1)S(1)} %shard_map.183.refs_0_), channel_id=1, source_target_pairs={{0,2},{2,0},{1,3},{3,1},{4,6},{6,4},{5,7},{7,5},{8,10},{10,8},{9,1... | collective-permute-start | bytes 122888 | tf_op jit(solution)/shard_map/ppermute | solution.py:720
  167.6 4.4 %collective-permute-start.29 = (bf16[160,128]{1,0:T(8,128)(2,1)S(1)}, bf16[160,128]{1,0:T(8,128)(2,1)S(1)}, u32[]{:S(2)}, u32[]{:S(2)}) collective-permute-start(bf16[160,128]{1,0:T(8,128)(2,1)S(1)} %shard_map.185.refs_2_.refs_1_), channel_id=1, source_target_pairs={{0,4},{4,8},{8,12},{12,0},{1,5},{5,9},{9,13},{13,1},{2,6},{6,10},{... | collective-permute-start | bytes 122888 | tf_op jit(solution)/shard_map/ppermute | solution.py:557
  167.6 4.5 %collective-permute-start.30 = (bf16[160,128]{1,0:T(8,128)(2,1)S(1)}, bf16[160,128]{1,0:T(8,128)(2,1)S(1)}, u32[]{:S(2)}, u32[]{:S(2)}) collective-permute-start(bf16[160,128]{1,0:T(8,128)(2,1)S(1)} %shard_map.185.refs_2_.refs_1_), channel_id=1, source_target_pairs={{0,8},{4,12},{8,0},{12,4},{1,9},{5,13},{9,1},{13,5},{2,10},{6,14},... | collective-permute-start | bytes 122888 | tf_op jit(solution)/shard_map/ppermute | solution.py:557
  169.8 2.9 %collective-permute-start.31 = (bf16[160,128]{1,0:T(8,128)(2,1)S(1)}, bf16[160,128]{1,0:T(8,128)(2,1)S(1)}, u32[]{:S(2)}, u32[]{:S(2)}) collective-permute-start(bf16[160,128]{1,0:T(8,128)(2,1)S(1)} %shard_map.185.refs_2_.refs_1_), channel_id=1, source_target_pairs={{0,12},{4,0},{8,4},{12,8},{1,13},{5,1},{9,5},{13,9},{2,14},{6,2},{... | collective-permute-start | bytes 122888 | tf_op jit(solution)/shard_map/ppermute | solution.py:557
  174.8 21.4 %all-to-all-start.3 = ((bf16[8,640,128]{2,1,0:T(8,128)(2,1)}), bf16[8,640,128]{2,1,0:T(8,128)(2,1)S(1)}, u32[]{:S(2)}, u32[]{:S(2)}) async-start(bf16[8,640,128]{2,1,0:T(8,128)(2,1)} %shard_map.187.refs_5_), calls=%async_computation.3 | async-start | bytes 2621440 | tf_op jit(solution)/shard_map/all_to_all | solution.py:730
  178.4 5.1 %collective-permute-start.26 = (bf16[512,128]{1,0:T(8,128)(2,1)S(1)}, bf16[512,128]{1,0:T(8,128)(2,1)S(1)}, u32[]{:S(2)}, u32[]{:S(2)}) collective-permute-start(bf16[512,128]{1,0:T(8,128)(2,1)S(1)} %shard_map.184.refs_2_.refs_1_), channel_id=1, source_target_pairs={{0,4},{4,8},{8,12},{12,0},{1,5},{5,9},{9,13},{13,1},{2,6},{6,10},{... | collective-permute-start | bytes 393224 | tf_op jit(solution)/shard_map/ppermute | solution.py:557
  179.5 6.3 %collective-permute-start.27 = (bf16[512,128]{1,0:T(8,128)(2,1)S(1)}, bf16[512,128]{1,0:T(8,128)(2,1)S(1)}, u32[]{:S(2)}, u32[]{:S(2)}) collective-permute-start(bf16[512,128]{1,0:T(8,128)(2,1)S(1)} %shard_map.184.refs_2_.refs_1_), channel_id=1, source_target_pairs={{0,8},{4,12},{8,0},{12,4},{1,9},{5,13},{9,1},{13,5},{2,10},{6,14},... | collective-permute-start | bytes 393224 | tf_op jit(solution)/shard_map/ppermute | solution.py:557
  182.1 4.1 %collective-permute-start.28 = (bf16[512,128]{1,0:T(8,128)(2,1)S(1)}, bf16[512,128]{1,0:T(8,128)(2,1)S(1)}, u32[]{:S(2)}, u32[]{:S(2)}) collective-permute-start(bf16[512,128]{1,0:T(8,128)(2,1)S(1)} %shard_map.184.refs_2_.refs_1_), channel_id=1, source_target_pairs={{0,12},{4,0},{8,4},{12,8},{1,13},{5,1},{9,5},{13,9},{2,14},{6,2},{... | collective-permute-start | bytes 393224 | tf_op jit(solution)/shard_map/ppermute | solution.py:557
  196.4 6.8 %collective-permute-start.33 = (bf16[5120,128]{1,0:T(8,128)(2,1)S(1)}, bf16[5120,128]{1,0:T(8,128)(2,1)S(1)}, u32[]{:S(2)}, u32[]{:S(2)}) collective-permute-start(bf16[5120,128]{1,0:T(8,128)(2,1)S(1)} %shard_map.190.refs_1_), channel_id=1, source_target_pairs={{0,1},{1,0},{2,3},{3,2},{4,5},{5,4},{6,7},{7,6},{8,9},{9,8},{10,11... | collective-permute-start | bytes 3932168 | tf_op jit(solution)/shard_map/ppermute | solution.py:742
  198.1 3.4 %collective-permute-start.32 = (bf16[2048,128]{1,0:T(8,128)(2,1)S(1)}, bf16[2048,128]{1,0:T(8,128)(2,1)S(1)}, u32[]{:S(2)}, u32[]{:S(2)}) collective-permute-start(bf16[2048,128]{1,0:T(8,128)(2,1)S(1)} %shard_map.188.refs_1_), channel_id=1, source_target_pairs={{0,1},{1,0},{2,3},{3,2},{4,5},{5,4},{6,7},{7,6},{8,9},{9,8},{10,11... | collective-permute-start | bytes 1572872 | tf_op jit(solution)/shard_map/ppermute | solution.py:738
  (24 other events, 55.8 us)

commit v4 on v3

--- a/solution.py
+++ b/solution.py
@@ -135,8 +135,8 @@
     return jnp.broadcast_to(row.astype(F32), (128, OBS)).T[:, :1].astype(jnp.int32)
 
 
-def route_kernel(obs, tile_row, cell_row, accept_row, out, slot):
-    trow = tile_row[...]
+def route_kernel(obs, marks, out, slot):
+    trow = marks[0:1]
     tcol = as_column(trow)
     hits = jnp.where(tcol == iota((OBS, TILES), 1), 1.0, 0.0)
     before = one_hot(iota((OBS, OBS), 0) > iota((OBS, OBS), 1))
@@ -146,8 +146,8 @@
     rank_row = jnp.sum(dot(hits_t.astype(B16), after) * hits_t, axis=0, keepdims=True).astype(jnp.int32)
     slot[...] = tcol * PITCH + rank_col
     lane = iota((OBS, F), 1)
-    cell = as_column(cell_row[...])
-    row_code = ((lax.shift_right_logical(cell, 4) + 1) * as_column(accept_row[...])).astype(F32)
+    cell = as_column(marks[1:2])
+    row_code = ((lax.shift_right_logical(cell, 4) + 1) * as_column(marks[2:3])).astype(F32)
     col_code = (cell & (TW - 1)).astype(F32)
     codes = (
         jnp.where(lane == rank_col, row_code, 0.0) + jnp.where(lane == rank_col + 8, col_code, 0.0)
@@ -593,8 +593,7 @@
         route_kernel,
         [((WIRE, F), B16), ((OBS, 1), jnp.int32)],
         (
-            observations, target_tile.reshape(1, OBS), target_cell.reshape(1, OBS),
-            accepted.reshape(1, OBS),
+            observations, jnp.stack([target_tile[:, 0], target_cell, accepted]),
         ),
     )
     arrived = lax.all_to_all(

time: 207 us -> 206 us (level)
    unnamed x70 -> x64, local copies, waits for them, and re-layouts: 13.5 us -> 11.5 us
where the time goes in v4:
time: 206 us; the launch traced here: 205 us
  waiting for transfers between devices  63.8 us (31%)
  starting transfers between devices  62 us (30%)
  Pallas kernels  41.2 us (20%)
  blocking collectives  24.8 us (12%)
  local copies, waits for them, and re-layouts  11.5 us (6%)
    pallas_call x22, Pallas kernels, call(): pl.pallas_call(body, out_shape=tuple((jax.ShapeDtypeStruct(s, d) for s, d...  41.2 us
    ppermute x21, starting transfers between devices, ring_sends(): lax.ppermute(piece, axis, [(i, (i + shift) % RING) for i in range(RING)])  32.2 us
    all_to_all x1, blocking collectives, on_device(): lax.all_to_all(outgoing.reshape(TILES, PITCH, F), ALL, split_axis=0, conc...  24.8 us
    ppermute x21, waiting for transfers between devices, ring_sends(): lax.ppermute(piece, axis, [(i, (i + shift) % RING) for i in range(RING)])  13 us
    unnamed x64, local copies, waits for them, and re-layouts  11.5 us
    all_to_all x1, waiting for transfers between devices, on_device(): lax.all_to_all(spread, LAT, split_axis=0, concat_axis=0, tiled=True)  10 us
    all_to_all x1, starting transfers between devices, swapped_parts(): return lax.all_to_all(blocks, axes, split_axis=0, concat_axis=0, tiled=True)  7.69 us
    ppermute x1, waiting for transfers between devices, on_device(): right = lax.ppermute(send_left, LON, west)  6.79 us
  transfers between devices with their start and end apart: 37, of which 21 were waited for; matrix products, arithmetic and copies ran while one was open for 0% of the time, Pallas kernels for 7%

profile of v4, /device:TPU:1, one launch (start us, length us, event | category | flops | bytes accessed | tf_op | source)
XLA Modules:
  0.0 205.0 jit_solution(11841704876067241662)
XLA Ops:
  3.2 24.8 %all_to_all.20 = bf16[128,8,256]{2,1,0:T(8,128)(2,1)S(1)} all-to-all(bf16[128,8,256]{2,1,0:T(8,128)(2,1)S(1)} %bitcast.21), channel_id=1, replica_groups=mesh['zlo'=2,'x'=4,'y'=4,'zhi'=2,'core'=2] {'zlo','x','y','zhi','core'}, dimensions={0} | all-to-all | bytes 1048576 | tf_op jit(solution)/shard_map/all_to_all | solution.py:599
  28.0 6.6 %shard_map.171 = (bf16[768,1280]{1,0:T(8,128)(2,1)S(1)}, bf16[128,512]{1,0:T(8,128)(2,1)S(1)}, bf16[4,768,512]{2,1,0:T(8,128)(2,1)S(1)}, bf16[128,1536]{1,0:T(8,128)(2,1)S(1)}, bf16[128,1024]{1,0:T(8,128)(2,1)S(1)}) custom-call(bf16[1024,256]{1,0:T(8,128)(2,1)S(1)} %bitcast.20, bf16[128,512]{1,0:T(8,128)(2,1)S(1)} %bitcast.24, ...), custom_call_target="tpu_custom_call" | custom-call | flops 7000000000 | tf_op jit(solution)/shard_map/pallas_call | solution.py:120
  34.6 1.3 copy-done.26
  35.9 1.4 collective-permute-start
  37.3 1.4 collective-permute-start.1
  38.8 2.6 %collective-permute-done.refs_0_ = bf16[96,1024]{1,0:T(8,128)(2,1)S(1)} collective-permute-done((bf16[96,1024]{1,0:T(8,128)(2,1)S(1)}, bf16[96,1024]{1,0:T(8,128)(2,1)S(1)}, u32[]{:S(2)}, u32[]{:S(2)}) %collective-permute-start) | collective-permute-done | bytes 196640 | tf_op jit(solution)/shard_map/ppermute | solution.py:614
  41.3 4.0 %collective-permute-done.1.refs_2_ = bf16[96,1024]{1,0:T(8,128)(2,1)S(1)} collective-permute-done((bf16[96,1024]{1,0:T(8,128)(2,1)S(1)}, bf16[96,1024]{1,0:T(8,128)(2,1)S(1)}, u32[]{:S(2)}, u32[]{:S(2)}) %collective-permute-start.1) | collective-permute-done | bytes 196640 | tf_op jit(solution)/shard_map/ppermute | solution.py:615
  45.3 1.2 shard_map.172
  47.3 2.8 %collective-permute-start.2 = (bf16[128,1024]{1,0:T(8,128)(2,1)}, bf16[128,1024]{1,0:T(8,128)(2,1)S(1)}, u32[]{:S(2)}, u32[]{:S(2)}) collective-permute-start(bf16[128,1024]{1,0:T(8,128)(2,1)} %get-tuple-element.55), channel_id=1, source_target_pairs={{0,1},{1,2},{2,3},{3,4},{4,5},{5,6},{6,7},{7,8},{8,9},{9,10},{10,1... | collective-permute-start | bytes 786440 | tf_op jit(solution)/shard_map/ppermute | solution.py:621
  50.1 3.6 %collective-permute-done.2.refs_3_ = bf16[128,1024]{1,0:T(8,128)(2,1)S(1)} collective-permute-done((bf16[128,1024]{1,0:T(8,128)(2,1)}, bf16[128,1024]{1,0:T(8,128)(2,1)S(1)}, u32[]{:S(2)}, u32[]{:S(2)}) %collective-permute-start.2) | collective-permute-done | bytes 262176 | tf_op jit(solution)/shard_map/ppermute | solution.py:621
  53.8 6.8 %collective-permute-done.3.refs_4_ = bf16[128,1024]{1,0:T(8,128)(2,1)} collective-permute-done((bf16[128,1024]{1,0:T(8,128)(2,1)}, bf16[128,1024]{1,0:T(8,128)(2,1)}, u32[]{:S(2)}, u32[]{:S(2)}) %collective-permute-start.3) | collective-permute-done | bytes 262176 | tf_op jit(solution)/shard_map/ppermute | solution.py:622
  62.7 8.7 %shard_map.173 = (bf16[128,512]{1,0:T(8,128)(2,1)}, bf16[128,2048]{1,0:T(8,128)(2,1)S(1)}, f32[320,1024]{1,0:T(8,128)S(1)}, bf16[128,1024]{1,0:T(8,128)(2,1)S(1)}, bf16[128,1024]{1,0:T(8,128)(2,1)S(1)}) custom-call(s32[1]{0:T(128)} %bitcast.refs_0_, bf16[128,1536]{1,0:T(8,128)(2,1)S(1)} %copy-done.29, bf16[320,1024]{1,0:T(8,128)(2,1)S(1)} %copy-done.19, ...), custom_call_target="tpu_custom_call" | custom-call | flops 8999999488 | tf_op jit(solution)/shard_map/pallas_call | solution.py:120
  71.8 5.6 %collective-permute-done.4.refs_1_ = bf16[128,1024]{1,0:T(8,128)(2,1)S(1)} collective-permute-done((bf16[128,1024]{1,0:T(8,128)(2,1)S(1)}, bf16[128,1024]{1,0:T(8,128)(2,1)S(1)}, u32[]{:S(2)}, u32[]{:S(2)}) %collective-permute-start.4) | collective-permute-done | bytes 262176 | tf_op jit(solution)/shard_map/ppermute | solution.py:643
  77.5 3.3 %collective-permute-done.5.refs_2_ = bf16[128,1024]{1,0:T(8,128)(2,1)S(1)} collective-permute-done((bf16[128,1024]{1,0:T(8,128)(2,1)S(1)}, bf16[128,1024]{1,0:T(8,128)(2,1)S(1)}, u32[]{:S(2)}, u32[]{:S(2)}) %collective-permute-start.5) | collective-permute-done | bytes 262176 | tf_op jit(solution)/shard_map/ppermute | solution.py:642
  82.7 3.1 %collective-permute-start.6 = (bf16[96,1024]{1,0:T(8,128)(2,1)}, bf16[96,1024]{1,0:T(8,128)(2,1)S(1)}, u32[]{:S(2)}, u32[]{:S(2)}) collective-permute-start(bf16[96,1024]{1,0:T(8,128)(2,1)} %get-tuple-element.66), channel_id=1, source_target_pairs={{0,16},{16,32},{32,48},{48,64},{64,80},{80,96},{96,112},{1,17},{17... | collective-permute-start | bytes 589832 | tf_op jit(solution)/shard_map/ppermute | solution.py:651
  85.8 1.3 collective-permute-start.7
  87.1 2.1 %collective-permute-done.6.refs_3_ = bf16[96,1024]{1,0:T(8,128)(2,1)S(1)} collective-permute-done((bf16[96,1024]{1,0:T(8,128)(2,1)}, bf16[96,1024]{1,0:T(8,128)(2,1)S(1)}, u32[]{:S(2)}, u32[]{:S(2)}) %collective-permute-start.6) | collective-permute-done | bytes 196640 | tf_op jit(solution)/shard_map/ppermute | solution.py:651
  89.2 3.8 %collective-permute-done.7.refs_4_ = bf16[96,1024]{1,0:T(8,128)(2,1)S(1)} collective-permute-done((bf16[96,1024]{1,0:T(8,128)(2,1)S(1)}, bf16[96,1024]{1,0:T(8,128)(2,1)S(1)}, u32[]{:S(2)}, u32[]{:S(2)}) %collective-permute-start.7) | collective-permute-done | bytes 196640 | tf_op jit(solution)/shard_map/ppermute | solution.py:650
  97.6 2.6 %shard_map.175 = (bf16[5120,128]{1,0:T(8,128)(2,1)S(1)}, bf16[5120,128]{1,0:T(8,128)(2,1)S(1)}, f32[128,512]{1,0:T(8,128)S(1)}, bf16[128,512]{1,0:T(8,128)(2,1)S(1)}) custom-call(s32[1]{0:T(128)} %bitcast.9.refs_0_, bf16[128,2048]{1,0:T(8,128)(2,1)S(1)} %copy-done.23, f32[128,1024]{1,0:T(8,128)S(1)} %copy-done.15, ...), custom_call_target="tpu_custom_call" | custom-call | flops 3000000000 | tf_op jit(solution)/shard_map/pallas_call | solution.py:120
  100.6 11.1 %shard_map.176 = (bf16[2048,128]{1,0:T(8,128)(2,1)S(1)}, bf16[2048,128]{1,0:T(8,128)(2,1)S(1)}, f32[128,512]{1,0:T(8,128)}, bf16[1024,256]{1,0:T(8,128)(2,1)}) custom-call(s32[1]{0:T(128)} %bitcast.9.refs_0_, bf16[128,512]{1,0:T(8,128)(2,1)S(1)} %copy-done.31, bf16[768,1280]{1,0:T(8,128)(2,1)S(1)} %copy-done.27, bf16[4,768,512]{2,1,0:T(8,128)(2,1)S(1)} %copy-done.25, ...), custom_call_target="tpu_custom_call" | custom-call | flops 8999999488 | tf_op jit(solution)/shard_map/pallas_call | solution.py:120
  111.7 1.4 shard_map.177
  113.1 7.7 %all-to-all-start.2 = ((bf16[8,640,128]{2,1,0:T(8,128)(2,1)}), bf16[8,640,128]{2,1,0:T(8,128)(2,1)S(1)}, u32[]{:S(2)}, u32[]{:S(2)}) async-start(bf16[8,640,128]{2,1,0:T(8,128)(2,1)} %bitcast.14), calls=%async_computation.2 | async-start | bytes 2621440 | tf_op jit(solution)/shard_map/all_to_all | solution.py:575
  121.5 1.5 collective-permute-done.9.refs_2_
  123.4 2.6 %collective-permute-start.12 = (bf16[512,128]{1,0:T(8,128)(2,1)S(1)}, bf16[512,128]{1,0:T(8,128)(2,1)S(1)}, u32[]{:S(2)}, u32[]{:S(2)}) collective-permute-start(bf16[512,128]{1,0:T(8,128)(2,1)S(1)} %get-tuple-element.80), channel_id=1, source_target_pairs={{0,12},{4,0},{8,4},{12,8},{1,13},{5,1},{9,5},{13,9},{2,14},{6,2},{... | collective-permute-start | bytes 393224 | tf_op jit(solution)/shard_map/ppermute | solution.py:557
  125.9 6.4 %collective-permute-done.10.refs_2_ = bf16[512,128]{1,0:T(8,128)(2,1)S(1)} collective-permute-done((bf16[512,128]{1,0:T(8,128)(2,1)S(1)}, bf16[512,128]{1,0:T(8,128)(2,1)S(1)}, u32[]{:S(2)}, u32[]{:S(2)}) %collective-permute-start.10) | collective-permute-done | bytes 131104 | tf_op jit(solution)/shard_map/ppermute | solution.py:557
  132.4 1.8 collective-permute-start.13
  134.3 2.4 %collective-permute-start.14 = (bf16[128,128]{1,0:T(8,128)(2,1)S(1)}, bf16[128,128]{1,0:T(8,128)(2,1)S(1)}, u32[]{:S(2)}, u32[]{:S(2)}) collective-permute-start(bf16[128,128]{1,0:T(8,128)(2,1)S(1)} %get-tuple-element.83), channel_id=1, source_target_pairs={{0,32},{16,48},{32,0},{48,16},{1,33},{17,49},{33,1},{49,17},{2,34}... | collective-permute-start | bytes 98312 | tf_op jit(solution)/shard_map/ppermute | solution.py:557
  137.8 1.6 all-to-all-done.2.refs_1_
  139.4 5.1 %all-to-all-start.1 = ((bf16[128,8,256]{2,1,0:T(8,128)(2,1)}), bf16[128,8,256]{2,1,0:T(8,128)(2,1)S(1)}, u32[]{:S(2)}, u32[]{:S(2)}) async-start(bf16[128,8,256]{2,1,0:T(8,128)(2,1)} %bitcast.11), calls=%async_computation.1 | async-start | bytes 1048576 | tf_op jit(solution)/shard_map/all_to_all | solution.py:689
  144.6 3.3 %collective-permute-start.19 = (bf16[128,128]{1,0:T(8,128)(2,1)S(1)}, bf16[128,128]{1,0:T(8,128)(2,1)S(1)}, u32[]{:S(2)}, u32[]{:S(2)}) collective-permute-start(bf16[128,128]{1,0:T(8,128)(2,1)S(1)} %shard_map.180.refs_2_.refs_1_), channel_id=1, source_target_pairs={{0,2},{2,64},{64,66},{66,0},{1,3},{3,65},{65,67},{67,1},{4,6},{6,6... | collective-permute-start | bytes 98312 | tf_op jit(solution)/shard_map/ppermute | solution.py:557
  148.7 1.3 collective-permute-start.16
  150.1 2.5 %collective-permute-start.17 = (bf16[160,128]{1,0:T(8,128)(2,1)S(1)}, bf16[160,128]{1,0:T(8,128)(2,1)S(1)}, u32[]{:S(2)}, u32[]{:S(2)}) collective-permute-start(bf16[160,128]{1,0:T(8,128)(2,1)S(1)} %get-tuple-element.87), channel_id=1, source_target_pairs={{0,8},{4,12},{8,0},{12,4},{1,9},{5,13},{9,1},{13,5},{2,10},{6,14},... | collective-permute-start | bytes 122888 | tf_op jit(solution)/shard_map/ppermute | solution.py:557
  152.6 2.7 %collective-permute-start.18 = (bf16[160,128]{1,0:T(8,128)(2,1)S(1)}, bf16[160,128]{1,0:T(8,128)(2,1)S(1)}, u32[]{:S(2)}, u32[]{:S(2)}) collective-permute-start(bf16[160,128]{1,0:T(8,128)(2,1)S(1)} %get-tuple-element.88), channel_id=1, source_target_pairs={{0,12},{4,0},{8,4},{12,8},{1,13},{5,1},{9,5},{13,9},{2,14},{6,2},{... | collective-permute-start | bytes 122888 | tf_op jit(solution)/shard_map/ppermute | solution.py:557
  155.3 2.9 %collective-permute-start.23 = (bf16[128,128]{1,0:T(8,128)(2,1)S(1)}, bf16[128,128]{1,0:T(8,128)(2,1)S(1)}, u32[]{:S(2)}, u32[]{:S(2)}) collective-permute-start(bf16[128,128]{1,0:T(8,128)(2,1)S(1)} %shard_map.182.refs_4_.refs_1_), channel_id=1, source_target_pairs={{0,16},{16,32},{32,48},{48,0},{1,17},{17,33},{33,49},{49,1},{2,18}... | collective-permute-start | bytes 98312 | tf_op jit(solution)/shard_map/ppermute | solution.py:557
  158.2 2.6 %collective-permute-start.24 = (bf16[128,128]{1,0:T(8,128)(2,1)S(1)}, bf16[128,128]{1,0:T(8,128)(2,1)S(1)}, u32[]{:S(2)}, u32[]{:S(2)}) collective-permute-start(bf16[128,128]{1,0:T(8,128)(2,1)S(1)} %shard_map.182.refs_4_.refs_1_), channel_id=1, source_target_pairs={{0,32},{16,48},{32,0},{48,16},{1,33},{17,49},{33,1},{49,17},{2,34}... | collective-permute-start | bytes 98312 | tf_op jit(solution)/shard_map/ppermute | solution.py:557
  162.4 1.4 collective-permute-done.25.refs_4_
  163.9 2.5 %collective-permute-done.22.refs_1_ = bf16[160,128]{1,0:T(8,128)(2,1)S(1)} collective-permute-done((bf16[160,128]{1,0:T(8,128)(2,1)S(1)}, bf16[160,128]{1,0:T(8,128)(2,1)S(1)}, u32[]{:S(2)}, u32[]{:S(2)}) %collective-permute-start.22) | collective-permute-done | bytes 40992 | tf_op jit(solution)/shard_map/ppermute | solution.py:719
  166.5 2.2 %collective-permute-start.30 = (bf16[160,128]{1,0:T(8,128)(2,1)S(1)}, bf16[160,128]{1,0:T(8,128)(2,1)S(1)}, u32[]{:S(2)}, u32[]{:S(2)}) collective-permute-start(bf16[160,128]{1,0:T(8,128)(2,1)S(1)} %shard_map.185.refs_2_.refs_1_), channel_id=1, source_target_pairs={{0,8},{4,12},{8,0},{12,4},{1,9},{5,13},{9,1},{13,5},{2,10},{6,14},... | collective-permute-start | bytes 122888 | tf_op jit(solution)/shard_map/ppermute | solution.py:557
  172.4 1.2 shard_map.187.refs_5_
  173.7 3.6 %all-to-all-start.3 = ((bf16[8,640,128]{2,1,0:T(8,128)(2,1)}), bf16[8,640,128]{2,1,0:T(8,128)(2,1)S(1)}, u32[]{:S(2)}, u32[]{:S(2)}) async-start(bf16[8,640,128]{2,1,0:T(8,128)(2,1)} %shard_map.187.refs_5_), calls=%async_computation.3 | async-start | bytes 2621440 | tf_op jit(solution)/shard_map/all_to_all | solution.py:729
  178.4 2.5 %collective-permute-start.27 = (bf16[512,128]{1,0:T(8,128)(2,1)S(1)}, bf16[512,128]{1,0:T(8,128)(2,1)S(1)}, u32[]{:S(2)}, u32[]{:S(2)}) collective-permute-start(bf16[512,128]{1,0:T(8,128)(2,1)S(1)} %shard_map.184.refs_2_.refs_1_), channel_id=1, source_target_pairs={{0,8},{4,12},{8,0},{12,4},{1,9},{5,13},{9,1},{13,5},{2,10},{6,14},... | collective-permute-start | bytes 393224 | tf_op jit(solution)/shard_map/ppermute | solution.py:557
  180.9 1.4 collective-permute-done.26.refs_2_
  182.3 2.3 %collective-permute-done.27.refs_3_ = bf16[512,128]{1,0:T(8,128)(2,1)S(1)} collective-permute-done((bf16[512,128]{1,0:T(8,128)(2,1)S(1)}, bf16[512,128]{1,0:T(8,128)(2,1)S(1)}, u32[]{:S(2)}, u32[]{:S(2)}) %collective-permute-start.27) | collective-permute-done | bytes 131104 | tf_op jit(solution)/shard_map/ppermute | solution.py:557
  185.0 10.0 %all-to-all-done.3 = bf16[8,640,128]{2,1,0:T(8,128)(2,1)S(1)} async-done(((bf16[8,640,128]{2,1,0:T(8,128)(2,1)}), bf16[8,640,128]{2,1,0:T(8,128)(2,1)S(1)}, u32[]{:S(2)}, u32[]{:S(2)}) %all-to-all-start.3) | async-done | bytes 1310752 | tf_op jit(solution)/shard_map/all_to_all | solution.py:729
  195.2 1.8 collective-permute-start.33
  197.0 3.3 %collective-permute-done.32.refs_2_ = bf16[2048,128]{1,0:T(8,128)(2,1)S(1)} collective-permute-done((bf16[2048,128]{1,0:T(8,128)(2,1)S(1)}, bf16[2048,128]{1,0:T(8,128)(2,1)S(1)}, u32[]{:S(2)}, u32[]{:S(2)}) %collective-permute-start.32) | collective-permute-done | bytes 524320 | tf_op jit(solution)/shard_map/ppermute | solution.py:737
  200.4 1.6 shard_map.189
  201.9 3.0 %shard_map.191 = (f32[512,512]{1,0:T(8,128)}, f32[512,1536]{1,0:T(8,128)}, f32[512,512]{1,0:T(8,128)}) custom-call(s32[1]{0:T(128)} %bitcast.9.refs_0_, bf16[5120,128]{1,0:T(8,128)(2,1)S(1)} %shard_map.190.refs_1_, bf16[5120,128]{1,0:T(8,128)(2,1)S(1)} %collective-permute-done.33.refs_2_), custom_call_target="tpu_custom_call" | custom-call | flops 3000000000 | tf_op jit(solution)/shard_map/pallas_call | solution.py:120
  (115 shorter events, 23.3 us)
Async XLA Ops:
  2.3 25.7 %copy-start = (bf16[512,1536]{1,0:T(8,128)(2,1)S(1)}, bf16[512,1536]{1,0:T(8,128)(2,1)}, u32[]{:S(2)}) copy-start(bf16[512,1536]{1,0:T(8,128)(2,1)} %refs_6_.4) | copy-start | bytes 4718596
  2.3 25.7 %copy-start.2 = (bf16[512,512]{1,0:T(8,128)(2,1)S(1)}, bf16[512,512]{1,0:T(8,128)(2,1)}, u32[]{:S(2)}) copy-start(bf16[512,512]{1,0:T(8,128)(2,1)} %refs_7_.2) | copy-start | bytes 1572868
  2.3 25.7 %copy-start.3 = (bf16[512,512]{1,0:T(8,128)(2,1)S(1)}, bf16[512,512]{1,0:T(8,128)(2,1)}, u32[]{:S(2)}) copy-start(bf16[512,512]{1,0:T(8,128)(2,1)} %refs_6_.5) | copy-start | bytes 1572868
  2.3 25.7 %copy-start.4 = (bf16[256,1024]{1,0:T(8,128)(2,1)S(1)}, bf16[256,1024]{1,0:T(8,128)(2,1)}, u32[]{:S(2)}) copy-start(bf16[256,1024]{1,0:T(8,128)(2,1)} %refs_7_.3) | copy-start | bytes 1572868
  2.3 25.7 %copy-start.11 = (bf16[8,16,512]{2,1,0:T(8,128)(2,1)S(1)}, bf16[8,16,512]{2,1,0:T(8,128)(2,1)}, u32[]{:S(2)}) copy-start(bf16[8,16,512]{2,1,0:T(8,128)(2,1)} %param.11) | copy-start | bytes 393220
  3.2 31.4 %copy-start.20 = (s32[256,1]{1,0:T(8,128)}, s32[256,1]{1,0:T(8,128)S(1)}, u32[]{:S(2)}) copy-start(s32[256,1]{1,0:T(8,128)S(1)} %get-tuple-element.71.refs_0_) | copy-start | bytes 3076
  35.9 10.6 %copy-start.24 = (bf16[4,768,512]{2,1,0:T(8,128)(2,1)}, bf16[4,768,512]{2,1,0:T(8,128)(2,1)S(1)}, u32[]{:S(2)}) copy-start(bf16[4,768,512]{2,1,0:T(8,128)(2,1)S(1)} %get-tuple-element.60.refs_3_) | copy-start | bytes 9437188
  35.9 10.6 %copy-start.28 = (bf16[128,1536]{1,0:T(8,128)(2,1)}, bf16[128,1536]{1,0:T(8,128)(2,1)S(1)}, u32[]{:S(2)}) copy-start(bf16[128,1536]{1,0:T(8,128)(2,1)S(1)} %get-tuple-element.52.refs_1_) | copy-start | bytes 1179652
  35.9 10.6 %copy-start.30 = (bf16[128,512]{1,0:T(8,128)(2,1)}, bf16[128,512]{1,0:T(8,128)(2,1)S(1)}, u32[]{:S(2)}) copy-start(bf16[128,512]{1,0:T(8,128)(2,1)S(1)} %get-tuple-element.58.refs_1_) | copy-start | bytes 393220
  35.9 5.4 %collective-permute-start = (bf16[96,1024]{1,0:T(8,128)(2,1)S(1)}, bf16[96,1024]{1,0:T(8,128)(2,1)S(1)}, u32[]{:S(2)}, u32[]{:S(2)}) collective-permute-start(bf16[96,1024]{1,0:T(8,128)(2,1)S(1)} %get-tuple-element.95), channel_id=1, source_target_pairs={{0,16},{16,32},{32,48},{48,64},{64,80},{80,96},{96,112},{1,17},{17... | collective-permute-start | bytes 589832 | tf_op jit(solution)/shard_map/ppermute | solution.py:614
  37.3 23.3 %copy-start.1 = (bf16[512,512]{1,0:T(8,128)(2,1)S(1)}, bf16[512,512]{1,0:T(8,128)(2,1)}, u32[]{:S(2)}) copy-start(bf16[512,512]{1,0:T(8,128)(2,1)} %refs_6_.3) | copy-start | bytes 1572868
  37.3 23.2 %copy-start.9 = (bf16[8,16,512]{2,1,0:T(8,128)(2,1)S(1)}, bf16[8,16,512]{2,1,0:T(8,128)(2,1)}, u32[]{:S(2)}) copy-start(bf16[8,16,512]{2,1,0:T(8,128)(2,1)} %param.21) | copy-start | bytes 393220
  37.3 8.0 %collective-permute-start.1 = (bf16[96,1024]{1,0:T(8,128)(2,1)S(1)}, bf16[96,1024]{1,0:T(8,128)(2,1)S(1)}, u32[]{:S(2)}, u32[]{:S(2)}) collective-permute-start(bf16[96,1024]{1,0:T(8,128)(2,1)S(1)} %get-tuple-element.94), channel_id=1, source_target_pairs={{16,0},{32,16},{48,32},{64,48},{80,64},{96,80},{112,96},{17,1},{33... | collective-permute-start | bytes 589832 | tf_op jit(solution)/shard_map/ppermute | solution.py:615
  47.3 6.4 %collective-permute-start.2 = (bf16[128,1024]{1,0:T(8,128)(2,1)}, bf16[128,1024]{1,0:T(8,128)(2,1)S(1)}, u32[]{:S(2)}, u32[]{:S(2)}) collective-permute-start(bf16[128,1024]{1,0:T(8,128)(2,1)} %get-tuple-element.55), channel_id=1, source_target_pairs={{0,1},{1,2},{2,3},{3,4},{4,5},{5,6},{6,7},{7,8},{8,9},{9,10},{10,1... | collective-permute-start | bytes 786440 | tf_op jit(solution)/shard_map/ppermute | solution.py:621
  50.1 10.4 %collective-permute-start.3 = (bf16[128,1024]{1,0:T(8,128)(2,1)}, bf16[128,1024]{1,0:T(8,128)(2,1)}, u32[]{:S(2)}, u32[]{:S(2)}) collective-permute-start(bf16[128,1024]{1,0:T(8,128)(2,1)} %get-tuple-element.56), channel_id=1, source_target_pairs={{1,0},{2,1},{3,2},{4,3},{5,4},{6,5},{7,6},{8,7},{9,8},{10,9},{11,1... | collective-permute-start | bytes 786440 | tf_op jit(solution)/shard_map/ppermute | solution.py:622
  71.3 6.1 %collective-permute-start.4 = (bf16[128,1024]{1,0:T(8,128)(2,1)S(1)}, bf16[128,1024]{1,0:T(8,128)(2,1)S(1)}, u32[]{:S(2)}, u32[]{:S(2)}) collective-permute-start(bf16[128,1024]{1,0:T(8,128)(2,1)S(1)} %get-tuple-element.63), channel_id=1, source_target_pairs={{0,1},{1,2},{2,3},{3,4},{4,5},{5,6},{6,7},{7,8},{8,9},{9,10},{10,1... | collective-permute-start | bytes 786440 | tf_op jit(solution)/shard_map/ppermute | solution.py:643
  71.3 9.4 %collective-permute-start.5 = (bf16[128,1024]{1,0:T(8,128)(2,1)S(1)}, bf16[128,1024]{1,0:T(8,128)(2,1)S(1)}, u32[]{:S(2)}, u32[]{:S(2)}) collective-permute-start(bf16[128,1024]{1,0:T(8,128)(2,1)S(1)} %get-tuple-element.64), channel_id=1, source_target_pairs={{1,0},{2,1},{3,2},{4,3},{5,4},{6,5},{7,6},{8,7},{9,8},{10,9},{11,1... | collective-permute-start | bytes 786440 | tf_op jit(solution)/shard_map/ppermute | solution.py:642
  82.7 6.5 %collective-permute-start.6 = (bf16[96,1024]{1,0:T(8,128)(2,1)}, bf16[96,1024]{1,0:T(8,128)(2,1)S(1)}, u32[]{:S(2)}, u32[]{:S(2)}) collective-permute-start(bf16[96,1024]{1,0:T(8,128)(2,1)} %get-tuple-element.66), channel_id=1, source_target_pairs={{0,16},{16,32},{32,48},{48,64},{64,80},{80,96},{96,112},{1,17},{17... | collective-permute-start | bytes 589832 | tf_op jit(solution)/shard_map/ppermute | solution.py:651
  85.8 7.2 %collective-permute-start.7 = (bf16[96,1024]{1,0:T(8,128)(2,1)S(1)}, bf16[96,1024]{1,0:T(8,128)(2,1)S(1)}, u32[]{:S(2)}, u32[]{:S(2)}) collective-permute-start(bf16[96,1024]{1,0:T(8,128)(2,1)S(1)} %get-tuple-element.67), channel_id=1, source_target_pairs={{16,0},{32,16},{48,32},{64,48},{80,64},{96,80},{112,96},{17,1},{33... | collective-permute-start | bytes 589832 | tf_op jit(solution)/shard_map/ppermute | solution.py:650
  100.2 11.5 %collective-permute-start.8 = (bf16[5120,128]{1,0:T(8,128)(2,1)S(1)}, bf16[5120,128]{1,0:T(8,128)(2,1)S(1)}, u32[]{:S(2)}, u32[]{:S(2)}) collective-permute-start(bf16[5120,128]{1,0:T(8,128)(2,1)S(1)} %get-tuple-element.74), channel_id=1, source_target_pairs={{0,1},{1,0},{2,3},{3,2},{4,5},{5,4},{6,7},{7,6},{8,9},{9,8},{10,11... | collective-permute-start | bytes 3932168 | tf_op jit(solution)/shard_map/ppermute | solution.py:665
  113.1 26.3 %all-to-all-start.2 = ((bf16[8,640,128]{2,1,0:T(8,128)(2,1)}), bf16[8,640,128]{2,1,0:T(8,128)(2,1)S(1)}, u32[]{:S(2)}, u32[]{:S(2)}) async-start(bf16[8,640,128]{2,1,0:T(8,128)(2,1)} %bitcast.14), calls=%async_computation.2 | async-start | bytes 2621440 | tf_op jit(solution)/shard_map/all_to_all | solution.py:575
  120.8 2.3 %collective-permute-start.9 = (bf16[2048,128]{1,0:T(8,128)(2,1)S(1)}, bf16[2048,128]{1,0:T(8,128)(2,1)S(1)}, u32[]{:S(2)}, u32[]{:S(2)}) collective-permute-start(bf16[2048,128]{1,0:T(8,128)(2,1)S(1)} %get-tuple-element.76), channel_id=1, source_target_pairs={{0,1},{1,0},{2,3},{3,2},{4,5},{5,4},{6,7},{7,6},{8,9},{9,8},{10,11... | collective-permute-start | bytes 1572872 | tf_op jit(solution)/shard_map/ppermute | solution.py:697
  123.2 9.1 %collective-permute-start.10 = (bf16[512,128]{1,0:T(8,128)(2,1)S(1)}, bf16[512,128]{1,0:T(8,128)(2,1)S(1)}, u32[]{:S(2)}, u32[]{:S(2)}) collective-permute-start(bf16[512,128]{1,0:T(8,128)(2,1)S(1)} %get-tuple-element.78), channel_id=1, source_target_pairs={{0,4},{4,8},{8,12},{12,0},{1,5},{5,9},{9,13},{13,1},{2,6},{6,10},{... | collective-permute-start | bytes 393224 | tf_op jit(solution)/shard_map/ppermute | solution.py:557
  123.3 9.1 %collective-permute-start.11 = (bf16[512,128]{1,0:T(8,128)(2,1)S(1)}, bf16[512,128]{1,0:T(8,128)(2,1)S(1)}, u32[]{:S(2)}, u32[]{:S(2)}) collective-permute-start(bf16[512,128]{1,0:T(8,128)(2,1)S(1)} %get-tuple-element.79), channel_id=1, source_target_pairs={{0,8},{4,12},{8,0},{12,4},{1,9},{5,13},{9,1},{13,5},{2,10},{6,14},... | collective-permute-start | bytes 393224 | tf_op jit(solution)/shard_map/ppermute | solution.py:557
  123.4 9.0 %collective-permute-start.12 = (bf16[512,128]{1,0:T(8,128)(2,1)S(1)}, bf16[512,128]{1,0:T(8,128)(2,1)S(1)}, u32[]{:S(2)}, u32[]{:S(2)}) collective-permute-start(bf16[512,128]{1,0:T(8,128)(2,1)S(1)} %get-tuple-element.80), channel_id=1, source_target_pairs={{0,12},{4,0},{8,4},{12,8},{1,13},{5,1},{9,5},{13,9},{2,14},{6,2},{... | collective-permute-start | bytes 393224 | tf_op jit(solution)/shard_map/ppermute | solution.py:557
  132.4 12.1 %collective-permute-start.13 = (bf16[128,128]{1,0:T(8,128)(2,1)S(1)}, bf16[128,128]{1,0:T(8,128)(2,1)S(1)}, u32[]{:S(2)}, u32[]{:S(2)}) collective-permute-start(bf16[128,128]{1,0:T(8,128)(2,1)S(1)} %get-tuple-element.82), channel_id=1, source_target_pairs={{0,16},{16,32},{32,48},{48,0},{1,17},{17,33},{33,49},{49,1},{2,18}... | collective-permute-start | bytes 98312 | tf_op jit(solution)/shard_map/ppermute | solution.py:557
  134.3 10.3 %collective-permute-start.14 = (bf16[128,128]{1,0:T(8,128)(2,1)S(1)}, bf16[128,128]{1,0:T(8,128)(2,1)S(1)}, u32[]{:S(2)}, u32[]{:S(2)}) collective-permute-start(bf16[128,128]{1,0:T(8,128)(2,1)S(1)} %get-tuple-element.83), channel_id=1, source_target_pairs={{0,32},{16,48},{32,0},{48,16},{1,33},{17,49},{33,1},{49,17},{2,34}... | collective-permute-start | bytes 98312 | tf_op jit(solution)/shard_map/ppermute | solution.py:557
  136.6 7.9 %collective-permute-start.15 = (bf16[128,128]{1,0:T(8,128)(2,1)S(1)}, bf16[128,128]{1,0:T(8,128)(2,1)S(1)}, u32[]{:S(2)}, u32[]{:S(2)}) collective-permute-start(bf16[128,128]{1,0:T(8,128)(2,1)S(1)} %get-tuple-element.84), channel_id=1, source_target_pairs={{0,48},{16,0},{32,16},{48,32},{1,49},{17,1},{33,17},{49,33},{2,50}... | collective-permute-start | bytes 98312 | tf_op jit(solution)/shard_map/ppermute | solution.py:557
  139.4 30.4 %all-to-all-start.1 = ((bf16[128,8,256]{2,1,0:T(8,128)(2,1)}), bf16[128,8,256]{2,1,0:T(8,128)(2,1)S(1)}, u32[]{:S(2)}, u32[]{:S(2)}) async-start(bf16[128,8,256]{2,1,0:T(8,128)(2,1)} %bitcast.11), calls=%async_computation.1 | async-start | bytes 1048576 | tf_op jit(solution)/shard_map/all_to_all | solution.py:689
  144.6 8.0 %collective-permute-start.19 = (bf16[128,128]{1,0:T(8,128)(2,1)S(1)}, bf16[128,128]{1,0:T(8,128)(2,1)S(1)}, u32[]{:S(2)}, u32[]{:S(2)}) collective-permute-start(bf16[128,128]{1,0:T(8,128)(2,1)S(1)} %shard_map.180.refs_2_.refs_1_), channel_id=1, source_target_pairs={{0,2},{2,64},{64,66},{66,0},{1,3},{3,65},{65,67},{67,1},{4,6},{6,6... | collective-permute-start | bytes 98312 | tf_op jit(solution)/shard_map/ppermute | solution.py:557
  147.9 7.3 %collective-permute-start.20 = (bf16[128,128]{1,0:T(8,128)(2,1)S(1)}, bf16[128,128]{1,0:T(8,128)(2,1)S(1)}, u32[]{:S(2)}, u32[]{:S(2)}) collective-permute-start(bf16[128,128]{1,0:T(8,128)(2,1)S(1)} %shard_map.180.refs_2_.refs_1_), channel_id=1, source_target_pairs={{0,64},{2,66},{64,0},{66,2},{1,65},{3,67},{65,1},{67,3},{4,68},{6,... | collective-permute-start | bytes 98312 | tf_op jit(solution)/shard_map/ppermute | solution.py:557
  148.5 6.8 %collective-permute-start.21 = (bf16[128,128]{1,0:T(8,128)(2,1)S(1)}, bf16[128,128]{1,0:T(8,128)(2,1)S(1)}, u32[]{:S(2)}, u32[]{:S(2)}) collective-permute-start(bf16[128,128]{1,0:T(8,128)(2,1)S(1)} %shard_map.180.refs_2_.refs_1_), channel_id=1, source_target_pairs={{0,66},{2,0},{64,2},{66,64},{1,67},{3,1},{65,3},{67,65},{4,70},{6,... | collective-permute-start | bytes 98312 | tf_op jit(solution)/shard_map/ppermute | solution.py:557
  148.7 12.1 %collective-permute-start.16 = (bf16[160,128]{1,0:T(8,128)(2,1)S(1)}, bf16[160,128]{1,0:T(8,128)(2,1)S(1)}, u32[]{:S(2)}, u32[]{:S(2)}) collective-permute-start(bf16[160,128]{1,0:T(8,128)(2,1)S(1)} %get-tuple-element.86), channel_id=1, source_target_pairs={{0,4},{4,8},{8,12},{12,0},{1,5},{5,9},{9,13},{13,1},{2,6},{6,10},{... | collective-permute-start | bytes 122888 | tf_op jit(solution)/shard_map/ppermute | solution.py:557
  150.1 11.8 %collective-permute-start.17 = (bf16[160,128]{1,0:T(8,128)(2,1)S(1)}, bf16[160,128]{1,0:T(8,128)(2,1)S(1)}, u32[]{:S(2)}, u32[]{:S(2)}) collective-permute-start(bf16[160,128]{1,0:T(8,128)(2,1)S(1)} %get-tuple-element.87), channel_id=1, source_target_pairs={{0,8},{4,12},{8,0},{12,4},{1,9},{5,13},{9,1},{13,5},{2,10},{6,14},... | collective-permute-start | bytes 122888 | tf_op jit(solution)/shard_map/ppermute | solution.py:557
  152.6 9.3 %collective-permute-start.18 = (bf16[160,128]{1,0:T(8,128)(2,1)S(1)}, bf16[160,128]{1,0:T(8,128)(2,1)S(1)}, u32[]{:S(2)}, u32[]{:S(2)}) collective-permute-start(bf16[160,128]{1,0:T(8,128)(2,1)S(1)} %get-tuple-element.88), channel_id=1, source_target_pairs={{0,12},{4,0},{8,4},{12,8},{1,13},{5,1},{9,5},{13,9},{2,14},{6,2},{... | collective-permute-start | bytes 122888 | tf_op jit(solution)/shard_map/ppermute | solution.py:557
  155.3 6.8 %collective-permute-start.23 = (bf16[128,128]{1,0:T(8,128)(2,1)S(1)}, bf16[128,128]{1,0:T(8,128)(2,1)S(1)}, u32[]{:S(2)}, u32[]{:S(2)}) collective-permute-start(bf16[128,128]{1,0:T(8,128)(2,1)S(1)} %shard_map.182.refs_4_.refs_1_), channel_id=1, source_target_pairs={{0,16},{16,32},{32,48},{48,0},{1,17},{17,33},{33,49},{49,1},{2,18}... | collective-permute-start | bytes 98312 | tf_op jit(solution)/shard_map/ppermute | solution.py:557
  158.2 4.3 %collective-permute-start.24 = (bf16[128,128]{1,0:T(8,128)(2,1)S(1)}, bf16[128,128]{1,0:T(8,128)(2,1)S(1)}, u32[]{:S(2)}, u32[]{:S(2)}) collective-permute-start(bf16[128,128]{1,0:T(8,128)(2,1)S(1)} %shard_map.182.refs_4_.refs_1_), channel_id=1, source_target_pairs={{0,32},{16,48},{32,0},{48,16},{1,33},{17,49},{33,1},{49,17},{2,34}... | collective-permute-start | bytes 98312 | tf_op jit(solution)/shard_map/ppermute | solution.py:557
  160.8 3.1 %collective-permute-start.25 = (bf16[128,128]{1,0:T(8,128)(2,1)S(1)}, bf16[128,128]{1,0:T(8,128)(2,1)S(1)}, u32[]{:S(2)}, u32[]{:S(2)}) collective-permute-start(bf16[128,128]{1,0:T(8,128)(2,1)S(1)} %shard_map.182.refs_4_.refs_1_), channel_id=1, source_target_pairs={{0,48},{16,0},{32,16},{48,32},{1,49},{17,1},{33,17},{49,33},{2,50}... | collective-permute-start | bytes 98312 | tf_op jit(solution)/shard_map/ppermute | solution.py:557
  161.9 4.4 %collective-permute-start.22 = (bf16[160,128]{1,0:T(8,128)(2,1)S(1)}, bf16[160,128]{1,0:T(8,128)(2,1)S(1)}, u32[]{:S(2)}, u32[]{:S(2)}) collective-permute-start(bf16[160,128]{1,0:T(8,128)(2,1)S(1)} %shard_map.183.refs_0_), channel_id=1, source_target_pairs={{0,2},{2,0},{1,3},{3,1},{4,6},{6,4},{5,7},{7,5},{8,10},{10,8},{9,1... | collective-permute-start | bytes 122888 | tf_op jit(solution)/shard_map/ppermute | solution.py:719
  166.4 4.4 %collective-permute-start.29 = (bf16[160,128]{1,0:T(8,128)(2,1)S(1)}, bf16[160,128]{1,0:T(8,128)(2,1)S(1)}, u32[]{:S(2)}, u32[]{:S(2)}) collective-permute-start(bf16[160,128]{1,0:T(8,128)(2,1)S(1)} %shard_map.185.refs_2_.refs_1_), channel_id=1, source_target_pairs={{0,4},{4,8},{8,12},{12,0},{1,5},{5,9},{9,13},{13,1},{2,6},{6,10},{... | collective-permute-start | bytes 122888 | tf_op jit(solution)/shard_map/ppermute | solution.py:557
  166.5 4.5 %collective-permute-start.30 = (bf16[160,128]{1,0:T(8,128)(2,1)S(1)}, bf16[160,128]{1,0:T(8,128)(2,1)S(1)}, u32[]{:S(2)}, u32[]{:S(2)}) collective-permute-start(bf16[160,128]{1,0:T(8,128)(2,1)S(1)} %shard_map.185.refs_2_.refs_1_), channel_id=1, source_target_pairs={{0,8},{4,12},{8,0},{12,4},{1,9},{5,13},{9,1},{13,5},{2,10},{6,14},... | collective-permute-start | bytes 122888 | tf_op jit(solution)/shard_map/ppermute | solution.py:557
  168.6 2.9 %collective-permute-start.31 = (bf16[160,128]{1,0:T(8,128)(2,1)S(1)}, bf16[160,128]{1,0:T(8,128)(2,1)S(1)}, u32[]{:S(2)}, u32[]{:S(2)}) collective-permute-start(bf16[160,128]{1,0:T(8,128)(2,1)S(1)} %shard_map.185.refs_2_.refs_1_), channel_id=1, source_target_pairs={{0,12},{4,0},{8,4},{12,8},{1,13},{5,1},{9,5},{13,9},{2,14},{6,2},{... | collective-permute-start | bytes 122888 | tf_op jit(solution)/shard_map/ppermute | solution.py:557
  173.7 21.4 %all-to-all-start.3 = ((bf16[8,640,128]{2,1,0:T(8,128)(2,1)}), bf16[8,640,128]{2,1,0:T(8,128)(2,1)S(1)}, u32[]{:S(2)}, u32[]{:S(2)}) async-start(bf16[8,640,128]{2,1,0:T(8,128)(2,1)} %shard_map.187.refs_5_), calls=%async_computation.3 | async-start | bytes 2621440 | tf_op jit(solution)/shard_map/all_to_all | solution.py:729
  177.2 5.1 %collective-permute-start.26 = (bf16[512,128]{1,0:T(8,128)(2,1)S(1)}, bf16[512,128]{1,0:T(8,128)(2,1)S(1)}, u32[]{:S(2)}, u32[]{:S(2)}) collective-permute-start(bf16[512,128]{1,0:T(8,128)(2,1)S(1)} %shard_map.184.refs_2_.refs_1_), channel_id=1, source_target_pairs={{0,4},{4,8},{8,12},{12,0},{1,5},{5,9},{9,13},{13,1},{2,6},{6,10},{... | collective-permute-start | bytes 393224 | tf_op jit(solution)/shard_map/ppermute | solution.py:557
  178.4 6.3 %collective-permute-start.27 = (bf16[512,128]{1,0:T(8,128)(2,1)S(1)}, bf16[512,128]{1,0:T(8,128)(2,1)S(1)}, u32[]{:S(2)}, u32[]{:S(2)}) collective-permute-start(bf16[512,128]{1,0:T(8,128)(2,1)S(1)} %shard_map.184.refs_2_.refs_1_), channel_id=1, source_target_pairs={{0,8},{4,12},{8,0},{12,4},{1,9},{5,13},{9,1},{13,5},{2,10},{6,14},... | collective-permute-start | bytes 393224 | tf_op jit(solution)/shard_map/ppermute | solution.py:557
  180.9 4.1 %collective-permute-start.28 = (bf16[512,128]{1,0:T(8,128)(2,1)S(1)}, bf16[512,128]{1,0:T(8,128)(2,1)S(1)}, u32[]{:S(2)}, u32[]{:S(2)}) collective-permute-start(bf16[512,128]{1,0:T(8,128)(2,1)S(1)} %shard_map.184.refs_2_.refs_1_), channel_id=1, source_target_pairs={{0,12},{4,0},{8,4},{12,8},{1,13},{5,1},{9,5},{13,9},{2,14},{6,2},{... | collective-permute-start | bytes 393224 | tf_op jit(solution)/shard_map/ppermute | solution.py:557
  195.2 6.8 %collective-permute-start.33 = (bf16[5120,128]{1,0:T(8,128)(2,1)S(1)}, bf16[5120,128]{1,0:T(8,128)(2,1)S(1)}, u32[]{:S(2)}, u32[]{:S(2)}) collective-permute-start(bf16[5120,128]{1,0:T(8,128)(2,1)S(1)} %shard_map.190.refs_1_), channel_id=1, source_target_pairs={{0,1},{1,0},{2,3},{3,2},{4,5},{5,4},{6,7},{7,6},{8,9},{9,8},{10,11... | collective-permute-start | bytes 3932168 | tf_op jit(solution)/shard_map/ppermute | solution.py:741
  197.0 3.4 %collective-permute-start.32 = (bf16[2048,128]{1,0:T(8,128)(2,1)S(1)}, bf16[2048,128]{1,0:T(8,128)(2,1)S(1)}, u32[]{:S(2)}, u32[]{:S(2)}) collective-permute-start(bf16[2048,128]{1,0:T(8,128)(2,1)S(1)} %shard_map.188.refs_1_), channel_id=1, source_target_pairs={{0,1},{1,0},{2,3},{3,2},{4,5},{5,4},{6,7},{7,6},{8,9},{9,8},{10,11... | collective-permute-start | bytes 1572872 | tf_op jit(solution)/shard_map/ppermute | solution.py:737
  (21 other events, 53.8 us)
